TPU v7x, 32 devices: a whole 2x2x4 slice. The times are simulated.
32 devices in a mesh: seq: 4 (over z), dp: 2 (over core), head: 4 (over y, x).
Axes of the slice: x: 2, y: 2, z: 4, core: 2. Of those that a mesh axis runs over, the one named last changes fastest.
Arguments:
- inputs: bfloat16 [2, 1536, 3072], P('dp', 'seq'), may hold values from -40 to 40
- w_query: bfloat16 [3072, 2048], P(None, 'head'), may hold values from -0.21650635 to 0.21650635
- w_key: bfloat16 [3072, 2048], P(None, 'head'), may hold values from -0.07216878 to 0.07216878
- w_value: bfloat16 [3072, 2048], P(None, 'head'), may hold values from -0.108253175 to 0.108253175
- gate_bias: float32 [8], P('head'), may hold values from 0 to 2.5
- cotangent: bfloat16 [2, 1536, 2048], P('dp', 'seq', 'head'), may hold values from -8 to 8
Outputs:
- blended: bfloat16 [2, 1536, 2048], P('dp', 'seq', 'head')
- grad_weights: float32 [3072, 3, 2048], P(('seq', 'dp'), None, 'head')
All inputs are finite; a program needn't handle non-finite values.
Results may differ from a plain program's by a relative error of at most 0.012.
Values may be sent and summed in bfloat16 or wider, within the bound.
No kernel may reach another device: no remote copies, remote signals or barrier semaphores. Data moves between devices by JAX's collectives and lax.ppermute only.
A program may use at most 128 MiB of HBM per device.

v0:
```python
import math

import jax
import jax.numpy as jnp
from jax import lax
from jax.sharding import PartitionSpec as P

exact_mode = lax.Precision.HIGHEST


def prefix(value, axis, join, neutral, backward):
    count, mine = (lax.axis_size(axis), lax.axis_index(axis))
    pieces = jax.tree.map(lambda part: lax.all_gather(part, axis), value)
    if backward:
        pieces = jax.tree.map(lambda part: part[::-1], pieces)
        mine = count - 1 - mine
    subtotal = jax.tree.map(
        lambda part, zero: jnp.full_like(part, 0) + jnp.asarray(zero, part.dtype), value, neutral
    )

    def turn(position, subtotal):
        longer = join(subtotal, jax.tree.map(lambda part: part[position], pieces))
        return jax.tree.map(lambda new, old: jnp.where(position < mine, new, old), longer, subtotal)

    return lax.fori_loop(0, count - 1, turn, subtotal)


def passed_along(x, axis, by):
    devices = lax.axis_size(axis)
    pairs = [(i, i + by) for i in range(devices) if 0 <= i + by < devices]
    return lax.ppermute(x, axis, pairs)


def product(form, left, right):
    return jnp.einsum(form, left, right, preferred_element_type=jnp.float32)


def feature(values_in):
    return jnp.where(values_in > 0, values_in + 1.0, jnp.exp(jnp.minimum(values_in, 0.0)))


def feature_slope(values_in):
    return jnp.where(values_in > 0, 1.0, jnp.exp(jnp.minimum(values_in, 0.0)))


def add_pair(earlier, latter):
    return (earlier[0] + latter[0], earlier[1] + latter[1])


def write_memory(keys_own, values_own):
    phi_key = feature(keys_own.astype(jnp.float32))
    memory = jnp.einsum(
        "shd,she->hde", phi_key, values_own.astype(jnp.float32), precision=exact_mode
    )
    return (memory, jnp.sum(phi_key, axis=0))


def write_grads(keys_own, values_own, grad_memory, grad_norm):
    key_float = keys_own.astype(jnp.float32)
    phi_key = feature(key_float)
    grad_phi = (
        jnp.einsum(
            "hde,she->shd", grad_memory, values_own.astype(jnp.float32), precision=exact_mode
        )
        + grad_norm[None]
    )
    grad_value = jnp.einsum("shd,hde->she", phi_key, grad_memory, precision=exact_mode)
    return (grad_phi * feature_slope(key_float), grad_value)


def attend(
    queries, keys_own, values_own, keys_prev, values_prev, has_prev, memory, normaliser, gate_bias
):
    seg_len, head_count, head_dim = queries.shape
    all_keys = jnp.concatenate([keys_prev, keys_own], 0)
    all_values = jnp.concatenate([values_prev, values_own], 0)
    score_scale = head_dim ** (-0.5)
    scores = product("shd,thd->hst", queries, all_keys) * score_scale
    row_ids = lax.broadcasted_iota(jnp.int32, (seg_len, 2 * seg_len), 0)
    col_ids = lax.broadcasted_iota(jnp.int32, (seg_len, 2 * seg_len), 1)
    allowed = (col_ids <= row_ids + seg_len) & ((col_ids >= seg_len) | has_prev)
    scores = jnp.where(allowed[None], scores, -1e30)
    row_max = jnp.max(scores, axis=2, keepdims=True)
    weights = jnp.exp(scores - row_max)
    softmax = weights / jnp.sum(weights, axis=2, keepdims=True)
    soft_bf = softmax.astype(jnp.bfloat16)
    local_out = product("hst,thd->shd", soft_bf, all_values)
    phi_query = feature(queries.astype(jnp.float32))
    numerator = jnp.einsum("shd,hde->she", phi_query, memory, precision=exact_mode)
    denominator = jnp.einsum("shd,hd->sh", phi_query, normaliser, precision=exact_mode) + 1.0
    retrieved = numerator / denominator[:, :, None]
    mixing = jax.nn.sigmoid(gate_bias)[None, :, None]
    blended = mixing * retrieved + (1.0 - mixing) * local_out
    stored = (all_keys, all_values, softmax, soft_bf, phi_query, retrieved, denominator)
    return (blended.astype(jnp.bfloat16), stored)


def backprop(cotangent, queries, memory, normaliser, gate_bias, stored):
    all_keys, all_values, softmax, soft_bf, phi_query, retrieved, denominator = stored
    head_dim = queries.shape[2]
    mixing = jax.nn.sigmoid(gate_bias)[None, :, None]
    upstream = cotangent.astype(jnp.float32)
    grad_ret = mixing * upstream
    grad_local = ((1.0 - mixing) * upstream).astype(jnp.bfloat16)
    grad_soft = product("shd,thd->hst", grad_local, all_values)
    grad_values = product("hst,shd->thd", soft_bf, grad_local)
    row_dot = jnp.sum(softmax * grad_soft, axis=2, keepdims=True)
    grad_scores = (softmax * (grad_soft - row_dot) * head_dim ** (-0.5)).astype(jnp.bfloat16)
    grad_query = product("hst,thd->shd", grad_scores, all_keys)
    grad_keys = product("hst,shd->thd", grad_scores, queries)
    grad_num = grad_ret / denominator[:, :, None]
    grad_den = -jnp.sum(grad_ret * retrieved, axis=2) / denominator
    grad_phi = (
        jnp.einsum("she,hde->shd", grad_num, memory, precision=exact_mode)
        + grad_den[:, :, None] * normaliser[None]
    )
    grad_memory = jnp.einsum("shd,she->hde", phi_query, grad_num, precision=exact_mode)
    grad_norm = jnp.einsum("shd,sh->hd", phi_query, grad_den, precision=exact_mode)
    grad_query = grad_query + grad_phi * feature_slope(queries.astype(jnp.float32))
    return (grad_query, grad_keys, grad_values, grad_memory, grad_norm)


def local(inputs, w_query, w_key, w_value, gate_bias, cotangent):
    tokens = inputs[0]
    seg_len, model_dim = tokens.shape
    head_count = gate_bias.shape[0]
    columns = w_query.shape[1]
    head_dim = columns // head_count

    def project(weight):
        return jnp.dot(tokens, weight, preferred_element_type=jnp.float32).astype(jnp.bfloat16)

    query_flat = project(w_query)
    key_flat = project(w_key)
    value_flat = project(w_value)
    queries = query_flat.reshape(seg_len, head_count, head_dim)
    keys_own = key_flat.reshape(seg_len, head_count, head_dim)
    values_own = value_flat.reshape(seg_len, head_count, head_dim)
    memory_own, norm_own = write_memory(keys_own, values_own)
    zero_pair = (jnp.zeros_like(memory_own), jnp.zeros_like(norm_own))
    memory_prev, norm_prev = prefix((memory_own, norm_own), "seq", add_pair, zero_pair, False)
    neighbour = passed_along(jnp.stack([key_flat, value_flat]), "seq", 1)
    keys_prev = neighbour[0].reshape(seg_len, head_count, head_dim)
    values_prev = neighbour[1].reshape(seg_len, head_count, head_dim)
    has_prev = lax.axis_index("seq") > 0
    blended, stored = attend(
        queries,
        keys_own,
        values_own,
        keys_prev,
        values_prev,
        has_prev,
        memory_prev,
        norm_prev,
        gate_bias,
    )
    cot_local = cotangent[0].reshape(seg_len, head_count, head_dim)
    grad_query, grad_keys, grad_values, grad_memory, grad_norm = backprop(
        cot_local, queries, memory_prev, norm_prev, gate_bias, stored
    )
    grad_mem_seg, grad_norm_seg = prefix((grad_memory, grad_norm), "seq", add_pair, zero_pair, True)
    outgoing = jnp.stack([grad_keys[:seg_len], grad_values[:seg_len]]).astype(jnp.bfloat16)
    incoming = passed_along(outgoing, "seq", -1).astype(jnp.float32)
    write_key, write_value = write_grads(keys_own, values_own, grad_mem_seg, grad_norm_seg)
    grad_key = (grad_keys[seg_len:] + incoming[0] + write_key).astype(jnp.bfloat16)
    grad_value = (grad_values[seg_len:] + incoming[1] + write_value).astype(jnp.bfloat16)
    grad_all = jnp.concatenate(
        [
            grad_query.astype(jnp.bfloat16).reshape(seg_len, columns),
            grad_key.reshape(seg_len, columns),
            grad_value.reshape(seg_len, columns),
        ],
        1,
    )
    seq_count = lax.axis_size("seq")
    dp_count = lax.axis_size("dp")
    grad_scale = 1.0 / math.sqrt(seq_count * dp_count * seg_len)
    part_rows = model_dim // (seq_count * dp_count)
    contract = (((0,), (0,)), ((), ()))
    summed = lax.psum_scatter(
        lax.dot_general(tokens, grad_all, contract, preferred_element_type=jnp.float32)
        * grad_scale,
        ("seq", "dp"),
        scatter_dimension=0,
        tiled=True,
    )
    grad_weights = summed.reshape(part_rows, 3, columns)
    return (blended.reshape(1, seg_len, columns), grad_weights)


def solution(mesh):
    return jax.shard_map(
        local,
        mesh=mesh,
        in_specs=(
            P("dp", "seq", None),
            P(None, "head"),
            P(None, "head"),
            P(None, "head"),
            P("head"),
            P("dp", "seq", "head"),
        ),
        out_specs=(P("dp", "seq", "head"), P(("seq", "dp"), None, "head")),
        check_vma=False,
    )
```

profile of v0, /device:TPU:0, one launch (start us, length us, event | category | flops | bytes accessed | tf_op | source)
XLA Modules:
  0.0 407.1 jit_solution(8405248749326121540)
XLA Ops:
  7.2 0.0 copy-start
  7.2 0.0 all-gather.7.cloned.1.call-start
  7.2 4.1 %fusion.38 = bf16[384,512]{1,0:T(8,128)(2,1)S(1)} fusion(bf16[3072,512]{1,0:T(8,128)(2,1)} %param.13, bf16[1,384,3072]{2,1,0:T(8,128)(2,1)} %param.10), kind=kOutput, calls=%fused_computation.41 | convolution fusion | flops 1208156160 | bytes 5898240 | tf_op jit(solution)/shard_map/dot_general | solution.py:131
  11.4 0.0 copy-start.8
  11.4 0.7 copy-done.8
  12.1 0.9 copy.66
  13.0 3.2 fusion.59
  16.2 0.9 copy.79
  17.1 2.7 fusion.71
  19.8 0.0 all-gather.7.cloned.1.call-update
  19.8 0.0 all-gather.9.cloned.1.call-start
  19.9 2.0 pad_maximum_fusion
  21.8 5.8 %collective-permute-start = (bf16[2,384,512]{2,1,0:T(8,128)(2,1)}, bf16[2,384,512]{2,1,0:T(8,128)(2,1)}, u32[]{:S(2)}, u32[]{:S(2)}) collective-permute-start(bf16[2,384,512]{2,1,0:T(8,128)(2,1)} %pad_maximum_fusion), channel_id=1, source_target_pairs={{0,8},{8,16},{16,24},{1,9},{9,17},{17,25},{2,10},{10,18},{18,26},{... | collective-permute-start | bytes 2359304 | tf_op jit(solution)/shard_map/ppermute | solution.py:31
  27.7 5.0 %fusion.41 = bf16[384,512]{1,0:T(8,128)(2,1)} fusion(bf16[3072,512]{1,0:T(8,128)(2,1)} %param.11, bf16[1,384,3072]{2,1,0:T(8,128)(2,1)} %param.10), kind=kOutput, calls=%fused_computation.42 | convolution fusion | flops 1208156160 | bytes 5898240 | tf_op jit(solution)/shard_map/dot_general | solution.py:131
  32.6 1.9 copy.67
  34.5 2.1 copy.40
  36.6 44.6 %all_gather.27 = f32[4,2,256]{2,1,0:T(2,128)S(1)} all-gather(f32[1,2,256]{2,1,0:T(2,128)S(1)} %all_gather.26), channel_id=1, replica_groups=mesh['seq'=4,'dp'=2,'head'=4] {'seq'}, dimensions={0}, use_global_device_ids=true | all-gather | bytes 10240 | tf_op jit(solution)/shard_map/all_gather | solution.py:13
  81.2 1.2 broadcast_subtract_fusion
  82.4 1.0 fusion.53
  83.4 2.1 fusion.126
  85.4 1.8 reshape_squeeze.8
  87.2 1.0 copy_dynamic-update-slice_fusion
  88.3 0.9 copy-done.12
  89.3 4.4 %fusion.127 = (f32[2,384]{1,0:T(2,128)}, f32[2,384,768]{2,1,0:T(8,128)}) fusion(pred[384,768]{1,0:T(8,128)(4,1)} %fusion.53, bf16[384,2,256]{0,2,1:T(8,128)(2,1)} %bitcast.159, bf16[768,2,256]{2,0,1:T(8,128)(2,1)} %copy-done.12), kind=kOutput, calls=%fused_computation.147 | convolution fusion | flops 304349952 | bytes 3836928 | tf_op jit(solution)/shard_map/sub | solution.py:84
  93.7 6.2 %while.32 = (s32[]{:T(128)}, f32[2,256,256]{2,1,0:T(8,128)}, f32[2,256]{1,0:T(2,128)S(1)}, s32[]{:T(128)}, f32[4,2,256,256]{3,2,1,0:T(8,128)}, /*index=5*/f32[4,2,256]{2,1,0:T(2,128)S(1)}, s32[]{:T(128)}, s32[]{:T(128)}) while((s32[]{:T(128)}, f32[2,256,256]{2,1,0:T(8,128)}, f32[2,256]{1,0:T(2,128)S(1)}, s32[]{:T(128)}, ...), condition=%wide.region_2.3_spmd.clone, body=%wide.region_1.2_spmd.clone.sunk | while | flops 394756 | bytes 1579131 | solution.py:25
  93.7 2.0 add_select_fusion.8
  95.7 2.1 add_select_fusion.8
  97.8 2.1 add_select_fusion.8
  99.9 0.6 fusion.81
  100.6 3.3 fusion.79
  103.9 0.0 all-gather.9.cloned.1.call-update
  103.9 0.0 reduce-scatter.2.cloned.1.call-start
  104.0 3.7 convolution_bitcast_fusion
  107.7 1.9 copy.65
  109.7 1.9 fusion.86
  111.6 3.3 fusion.84
  114.9 9.0 %fusion.19 = f32[768,2,256]{0,2,1:T(8,128)} fusion(bf16[384,2,256]{0,2,1:T(8,128)(2,1)} %bitcast.160, f32[2,384,768]{2,1,0:T(8,128)} %fusion.84, f32[2,384,768]{2,1,0:T(8,128)} %get-tuple-element.303, f32[2,384]{1,0:T(2,128)} %get-tuple-element.302), kind=kOutput, calls=%fused_computation.22 | convolution fusion | flops 306120192 | bytes 6687744 | tf_op jit(solution)/shard_map/hst,shd->thd/dot_general | solution.py:35
  123.9 1.2 fusion.85
  125.1 2.0 pad_maximum_fusion.2
  127.1 1.5 collective-permute-start.1
  128.6 10.1 %fusion.22 = f32[384,2,256]{0,2,1:T(8,128)} fusion(bf16[768,2,256]{2,0,1:T(8,128)(2,1)} %copy-done.12, f32[2,384,768]{2,1,0:T(8,128)} %fusion.84, f32[2,384,768]{2,1,0:T(8,128)} %get-tuple-element.303, f32[2,384]{1,0:T(2,128)} %get-tuple-element.302), kind=kOutput, calls=%fused_computation.24 | convolution fusion | flops 306120192 | bytes 6294528 | tf_op jit(solution)/shard_map/hst,thd->shd/dot_general | solution.py:35
  138.8 24.5 %collective-permute-done.1 = bf16[2,384,2,256]{1,3,2,0:T(8,128)(2,1)} collective-permute-done((bf16[2,384,2,256]{1,3,2,0:T(8,128)(2,1)}, bf16[2,384,2,256]{1,3,2,0:T(8,128)(2,1)}, u32[]{:S(2)}, u32[]{:S(2)}) %collective-permute-start.1) | collective-permute-done | bytes 786464 | tf_op jit(solution)/shard_map/ppermute | solution.py:31
  163.3 2.5 convert_element_type.66
  165.8 2.1 multiply_reduce_fusion.1
  167.9 0.9 fusion.77
  168.8 0.0 copy-done.14
  168.8 12.5 %all-gather.3 = f32[4,2,256]{2,1,0:T(2,128)} all-gather(f32[1,2,256]{2,1,0:T(2,128)S(1)} %bitcast.169), channel_id=4, replica_groups=mesh['seq'=4,'dp'=2,'head'=4] {'seq'}, dimensions={0}, use_global_device_ids=true | all-gather | bytes 10240 | tf_op jit(solution)/shard_map/all_gather | solution.py:13
  181.3 0.7 reverse
  182.1 3.8 fusion.33
  185.8 3.1 rev.6
  188.9 6.1 %while.33 = (s32[]{:T(128)}, f32[2,256,256]{2,1,0:T(8,128)}, f32[2,256]{1,0:T(2,128)S(1)}, s32[]{:T(128)}, f32[4,2,256,256]{3,2,1,0:T(8,128)}, /*index=5*/f32[4,2,256]{2,1,0:T(2,128)S(1)}, s32[]{:T(128)}, s32[]{:T(128)}) while((s32[]{:T(128)}, f32[2,256,256]{2,1,0:T(8,128)}, f32[2,256]{1,0:T(2,128)S(1)}, s32[]{:T(128)}, ...), condition=%wide.region_8.9_spmd.clone, body=%wide.region_7.8_spmd.clone.sunk | while | flops 394756 | bytes 1579131 | solution.py:25
  188.9 1.9 add_select_fusion.10
  190.8 2.1 add_select_fusion.10
  192.9 2.1 add_select_fusion.10
  195.0 3.0 fusion.66
  198.0 2.1 fusion.69
  200.1 10.7 %multiply_bitcast_fusion = f32[3072,1536]{0,1:T(8,128)} fusion(bf16[1,384,3072]{2,1,0:T(8,128)(2,1)S(1)} %copy-done.7, bf16[384,512]{0,1:T(8,128)(2,1)S(1)} %bitcast.157, bf16[384,512]{0,1:T(8,128)(2,1)S(1)} %bitcast.158, bf16[384,512]{0,1:T(8,128)(2,1)S(1)} %bitcast.167), kind=kOutput, calls=%fused_computation.6 | convolution fusion | flops 3632136192 | bytes 22413312 | tf_op jit(solution)/shard_map/dot_general | solution.py:181
  210.8 0.0 reduce-scatter.2.cloned.1.call-update
  210.8 0.6 copy-done.16
  211.4 0.1 copy-done.19
  211.5 3.4 fusion.34
  214.9 2.0 copy.50
  216.9 180.6 %reduce-scatter.2.cloned.1.call-done = f32[384,1536]{0,1:T(8,128)} async-done(((f32[3072,1536]{0,1:T(8,128)}), f32[384,1536]{0,1:T(8,128)}) %reduce-scatter.2.cloned.1.call-update) | async-done | bytes 2359312 | tf_op jit(solution)/shard_map/reduce_scatter | solution.py:180
  397.5 3.0 copy.51
  (53 shorter events, 0.2 us)
Async XLA Ops:
  7.2 5.9 %copy-start = (bf16[3072,512]{1,0:T(8,128)(2,1)S(1)}, bf16[3072,512]{1,0:T(8,128)(2,1)}, u32[]{:S(2)}) copy-start(bf16[3072,512]{1,0:T(8,128)(2,1)} %param.12) | copy-start | bytes 9437188
  7.2 86.5 %all-gather.7.cloned.1.call-start = ((), (), s32[]{:S(2)}) async-start(), calls=%async_computation.2 | async-start | bytes 2621440 | tf_op jit(solution)/shard_map/all_gather | solution.py:13
  11.4 0.7 copy-start.8
  19.8 166.0 %all-gather.9.cloned.1.call-start = ((), (), s32[]{:S(2)}) async-start(), calls=%async_computation.3 | async-start | bytes 2621440 | tf_op jit(solution)/shard_map/all_gather | solution.py:13
  21.8 61.5 %collective-permute-start = (bf16[2,384,512]{2,1,0:T(8,128)(2,1)}, bf16[2,384,512]{2,1,0:T(8,128)(2,1)}, u32[]{:S(2)}, u32[]{:S(2)}) collective-permute-start(bf16[2,384,512]{2,1,0:T(8,128)(2,1)} %pad_maximum_fusion), channel_id=1, source_target_pairs={{0,8},{8,16},{16,24},{1,9},{9,17},{17,25},{2,10},{10,18},{18,26},{... | collective-permute-start | bytes 2359304 | tf_op jit(solution)/shard_map/ppermute | solution.py:31
  88.3 1.0 copy-start.12
  93.7 6.3 %copy-start.9 = (bf16[384,512]{0,1:T(8,128)(2,1)S(1)}, bf16[384,512]{0,1:T(8,128)(2,1)}, u32[]{:S(2)}) copy-start(bf16[384,512]{0,1:T(8,128)(2,1)} %copy.67) | copy-start | bytes 1179652
  100.6 65.1 %copy-start.13 = (f32[384,2]{0,1:T(2,128)}, f32[384,2]{0,1:T(2,128)S(1)}, u32[]{:S(2)}) copy-start(f32[384,2]{0,1:T(2,128)S(1)} %fusion.102) | copy-start | bytes 9220
  100.6 3.4 copy-start.15
  103.9 293.6 %reduce-scatter.2.cloned.1.call-start = ((), (), s32[]{:S(2)}) async-start(), calls=%async_computation.1 | async-start | bytes 21233664 | tf_op jit(solution)/shard_map/reduce_scatter | solution.py:180
  104.0 7.6 %copy-start.4 = (bf16[384,512]{0,1:T(8,128)(2,1)S(1)}, bf16[384,512]{0,1:T(8,128)(2,1)}, u32[]{:S(2)}) copy-start(bf16[384,512]{0,1:T(8,128)(2,1)} %copy.66) | copy-start | bytes 1179652
  127.1 36.1 %collective-permute-start.1 = (bf16[2,384,2,256]{1,3,2,0:T(8,128)(2,1)}, bf16[2,384,2,256]{1,3,2,0:T(8,128)(2,1)}, u32[]{:S(2)}, u32[]{:S(2)}) collective-permute-start(bf16[2,384,2,256]{1,3,2,0:T(8,128)(2,1)} %pad_maximum_fusion.2), channel_id=1, source_target_pairs={{8,0},{16,8},{24,16},{9,1},{17,9},{25,17},{10,2},{18,10},{26,18},{... | collective-permute-start | bytes 2359304 | tf_op jit(solution)/shard_map/ppermute | solution.py:31
  138.7 27.0 %copy-start.2 = (f32[2,256,256]{2,1,0:T(8,128)S(1)}, f32[2,256,256]{2,1,0:T(8,128)}, u32[]{:S(2)}) copy-start(f32[2,256,256]{2,1,0:T(8,128)} %get-tuple-element.222) | copy-start | bytes 1572868
  138.7 27.0 %copy-start.6 = (f32[1,384,512]{1,2,0:T(8,128)S(1)}, f32[1,384,512]{1,2,0:T(8,128)}, u32[]{:S(2)}) copy-start(f32[1,384,512]{1,2,0:T(8,128)} %copy.40) | copy-start | bytes 2359300
  138.7 27.0 %copy-start.10 = (bf16[384,512]{0,1:T(8,128)(2,1)S(1)}, bf16[384,512]{0,1:T(8,128)(2,1)}, u32[]{:S(2)}) copy-start(bf16[384,512]{0,1:T(8,128)(2,1)} %copy.67) | copy-start | bytes 1179652
  138.8 27.0 %copy-start.17 = (f32[2]{0:T(128)S(1)}, f32[2]{0:T(128)}, u32[]{:S(2)}) copy-start(f32[2]{0:T(128)} %get-tuple-element.297) | copy-start | bytes 28
  167.9 1.0 copy-start.14
  195.0 3.0 copy-start.1
  195.0 3.0 copy-start.3
  195.0 3.0 copy-start.5
  197.9 2.1 copy-start.7
  198.0 2.1 copy-start.11
  210.8 0.6 copy-start.16
  210.8 0.6 copy-start.18
  210.8 0.7 copy-start.19
Sparse Core Ops, SparseCore 0:
  20.0 58.0 all-gather.6
  104.1 51.5 all-gather.8
  210.9 186.5 reduce-scatter.1
where the time goes:
time: 408 us; the launch traced here: 407 us
  waiting for transfers between devices  205 us (50%)
  matrix products  75.4 us (18%)
  blocking collectives  57.1 us (14%)
  local copies, waits for them, and re-layouts  27.1 us (7%)
  other arithmetic  21 us (5%)
  between operations  14 us (3%)
  starting transfers between devices  7.39 us (2%)
    reduce_scatter x1, waiting for transfers between devices, local(): lax.psum_scatter(lax.dot_general(tokens, grad_all, contract, preferred_el...  181 us
    all_gather x2, blocking collectives, prefix(): pieces = jax.tree.map(lambda part: lax.all_gather(part, axis), value)  57.1 us
    dot_general x5, matrix products, product(): return jnp.einsum(form, left, right, preferred_element_type=jnp.float32)  29.6 us
    ppermute x2, waiting for transfers between devices, passed_along(): return lax.ppermute(x, axis, pairs)  24.5 us
    select_n x12, other arithmetic, turn(): jnp.where(position < mine, new, old)  12.3 us
    dot_general x3, matrix products, project(): jnp.dot(tokens, weight, preferred_element_type=jnp.float32)  12.2 us
    dot_general x1, matrix products, local(): lax.dot_general(tokens, grad_all, contract, preferred_element_type=jnp.fl...  10.7 us
    unnamed x43, local copies, waits for them, and re-layouts  8.55 us
  transfers between devices with their start and end apart: 5, of which 2 were waited for; matrix products, arithmetic and copies ran while one was open for 17% of the time, Pallas kernels for 0%

commit v1 on v0

v1 whole, which is shorter than its diff:
```python
import functools
import math

import jax
import jax.numpy as jnp
from jax import lax
from jax.experimental import pallas as pl
from jax.experimental.pallas import tpu as pltpu
from jax.sharding import PartitionSpec as P

VMEM_LIMIT = 48 * 1024 * 1024


def dot_nn(left, right):
    return lax.dot_general(
        left, right, (((1,), (0,)), ((), ())), preferred_element_type=jnp.float32
    )


def dot_nt(left, right):
    return lax.dot_general(
        left, right, (((1,), (1,)), ((), ())), preferred_element_type=jnp.float32
    )


def dot_tn(left, right):
    return lax.dot_general(
        left, right, (((0,), (0,)), ((), ())), preferred_element_type=jnp.float32
    )


def halves(value):
    high = value.astype(jnp.bfloat16)
    low = (value - high.astype(jnp.float32)).astype(jnp.bfloat16)
    return high, low


def wide(dot, left, right):
    left_high, left_low = halves(left)
    right_high, right_low = halves(right)
    return dot(left_high, right_high) + (dot(left_high, right_low) + dot(left_low, right_high))


def feature(value):
    return jnp.where(value > 0, value + 1.0, jnp.exp(jnp.minimum(value, 0.0)))


def feature_slope(value):
    return jnp.where(value > 0, 1.0, jnp.exp(jnp.minimum(value, 0.0)))


def write_kernel(key_ref, value_ref, memory_ref, norm_ref):
    phi_key = feature(key_ref[...].astype(jnp.float32))
    high, low = halves(phi_key)
    value = value_ref[...]
    memory_ref[0] = dot_tn(high, value) + dot_tn(low, value)
    norm_ref[...] = jnp.sum(phi_key, axis=0, keepdims=True)


def grad_memory_kernel(query_ref, cot_ref, norm_ref, mix_ref, out_ref):
    phi_query = feature(query_ref[...].astype(jnp.float32))
    denominator = jnp.sum(phi_query * norm_ref[...], axis=1, keepdims=True) + 1.0
    grad_num = mix_ref[...] * cot_ref[...].astype(jnp.float32) / denominator
    out_ref[0] = wide(dot_tn, phi_query, grad_num)


def attend_kernel(
    has_prev_ref,
    query_ref,
    key_ref,
    value_ref,
    key_prev_ref,
    value_prev_ref,
    cot_ref,
    mix_ref,
    out_ref,
    grad_query_ref,
    stats_ref,
):
    query = query_ref[...]
    seg_len, head_dim = query.shape
    scale = head_dim ** (-0.5)
    key, key_prev = key_ref[...], key_prev_ref[...]
    value, value_prev = value_ref[...], value_prev_ref[...]
    rows = lax.broadcasted_iota(jnp.int32, (seg_len, seg_len), 0)
    cols = lax.broadcasted_iota(jnp.int32, (seg_len, seg_len), 1)
    score_own = jnp.where(cols <= rows, dot_nt(query, key) * scale, -1e30)
    score_prev = jnp.where(has_prev_ref[0] > 0, dot_nt(query, key_prev) * scale, -1e30)
    row_max = jnp.maximum(
        jnp.max(score_own, axis=1, keepdims=True), jnp.max(score_prev, axis=1, keepdims=True)
    )
    weight_own = jnp.exp(score_own - row_max)
    weight_prev = jnp.exp(score_prev - row_max)
    inverse = 1.0 / (
        jnp.sum(weight_own, axis=1, keepdims=True) + jnp.sum(weight_prev, axis=1, keepdims=True)
    )
    soft_own = weight_own * inverse
    soft_prev = weight_prev * inverse
    out_ref[...] = dot_nn(soft_own.astype(jnp.bfloat16), value) + dot_nn(
        soft_prev.astype(jnp.bfloat16), value_prev
    )
    grad_local = ((1.0 - mix_ref[...]) * cot_ref[...].astype(jnp.float32)).astype(jnp.bfloat16)
    grad_own = dot_nt(grad_local, value)
    grad_prev = dot_nt(grad_local, value_prev)
    row_dot = jnp.sum(soft_own * grad_own, axis=1, keepdims=True) + jnp.sum(
        soft_prev * grad_prev, axis=1, keepdims=True
    )
    score_grad_own = (soft_own * (grad_own - row_dot) * scale).astype(jnp.bfloat16)
    score_grad_prev = (soft_prev * (grad_prev - row_dot) * scale).astype(jnp.bfloat16)
    grad_query_ref[...] = dot_nn(score_grad_own, key) + dot_nn(score_grad_prev, key_prev)
    lane = lax.broadcasted_iota(jnp.int32, (seg_len, 128), 1)
    stats = jnp.where(
        lane == 0, row_max, jnp.where(lane == 1, inverse, jnp.where(lane == 2, row_dot, 0.0))
    )
    stats_ref[...] = jnp.transpose(stats)[:8]


def retrieve_kernel(
    query_ref,
    cot_ref,
    memory_ref,
    norm_ref,
    mix_ref,
    local_ref,
    grad_att_ref,
    blended_ref,
    grad_query_ref,
    grad_norm_ref,
):
    query = query_ref[...].astype(jnp.float32)
    phi_query = feature(query)
    norm = norm_ref[...]
    memory = memory_ref[0]
    mix = mix_ref[...]
    denominator = jnp.sum(phi_query * norm, axis=1, keepdims=True) + 1.0
    retrieved = wide(dot_nn, phi_query, memory) / denominator
    blended = mix * retrieved + (1.0 - mix) * local_ref[...]
    blended_ref[...] = blended.astype(jnp.bfloat16)
    grad_ret = mix * cot_ref[...].astype(jnp.float32)
    grad_num = grad_ret / denominator
    grad_den = -jnp.sum(grad_ret * retrieved, axis=1, keepdims=True) / denominator
    grad_phi = wide(dot_nt, grad_num, memory) + grad_den * norm
    grad_norm_ref[...] = jnp.sum(grad_den * phi_query, axis=0, keepdims=True)
    grad_query = grad_att_ref[...] + grad_phi * feature_slope(query)
    grad_query_ref[...] = grad_query.astype(jnp.bfloat16)


def key_value_kernel(
    key_ref,
    value_ref,
    query_ref,
    cot_ref,
    stats_ref,
    query_next_ref,
    cot_next_ref,
    stats_next_ref,
    grad_memory_ref,
    mix_ref,
    grad_key_ref,
    grad_value_ref,
):
    key, value = key_ref[...], value_ref[...]
    seg_len, head_dim = key.shape
    scale = head_dim ** (-0.5)
    keep = 1.0 - mix_ref[...]

    def part(query, cot, stats, causal):
        grad_local = (keep * cot.astype(jnp.float32)).astype(jnp.bfloat16)
        score = dot_nt(key, query) * scale
        if causal:
            rows = lax.broadcasted_iota(jnp.int32, score.shape, 0)
            cols = lax.broadcasted_iota(jnp.int32, score.shape, 1)
            score = jnp.where(rows <= cols, score, -1e30)
        soft = jnp.exp(score - stats[0:1]) * stats[1:2]
        grad_value = dot_nn(soft.astype(jnp.bfloat16), grad_local)
        grad_soft = dot_nt(value, grad_local)
        score_grad = (soft * (grad_soft - stats[2:3]) * scale).astype(jnp.bfloat16)
        return dot_nn(score_grad, query), grad_value

    own_key, own_value = part(query_ref[...], cot_ref[...], stats_ref[...], True)
    next_key, next_value = part(query_next_ref[...], cot_next_ref[...], stats_next_ref[...], False)
    key_float = key.astype(jnp.float32)
    high, low = halves(grad_memory_ref[0])
    phi_high, phi_low = halves(feature(key_float))
    from_memory = dot_nt(value, high) + dot_nt(value, low)
    grad_key_ref[...] = own_key + next_key + from_memory * feature_slope(key_float)
    to_value = dot_nn(phi_high, high) + (dot_nn(phi_high, low) + dot_nn(phi_low, high))
    grad_value_ref[...] = (own_value + next_value + to_value).astype(jnp.bfloat16)


def call(kernel, heads, seg_len, head_dim, ins, outs, flops):
    specs = {
        "f": pl.BlockSpec(memory_space=pltpu.SMEM),
        "c": pl.BlockSpec((seg_len, head_dim), lambda h: (0, h)),
        "r": pl.BlockSpec((1, head_dim), lambda h: (0, h)),
        "m": pl.BlockSpec((1, head_dim, head_dim), lambda h: (h, 0, 0)),
        "s": pl.BlockSpec((8, seg_len), lambda h: (h, 0)),
    }
    shapes = {
        "c": (seg_len, heads * head_dim),
        "r": (1, heads * head_dim),
        "m": (heads, head_dim, head_dim),
        "s": (8 * heads, seg_len),
    }
    return pl.pallas_call(
        kernel,
        grid=(heads,),
        in_specs=[specs[kind] for kind in ins],
        out_specs=[specs[kind] for kind, _ in outs],
        out_shape=[jax.ShapeDtypeStruct(shapes[kind], dtype) for kind, dtype in outs],
        compiler_params=pltpu.CompilerParams(vmem_limit_bytes=VMEM_LIMIT),
        cost_estimate=pl.CostEstimate(
            flops=flops, bytes_accessed=4 * 1024 * 1024, transcendentals=0
        ),
    )


def local(inputs, w_query, w_key, w_value, gate_bias, cotangent):
    tokens = inputs[0]
    cot = cotangent[0]
    seg_len, model_dim = tokens.shape
    heads = gate_bias.shape[0]
    columns = w_query.shape[1]
    head_dim = columns // heads
    seq_count, seq_at = lax.axis_size("seq"), lax.axis_index("seq")
    dp_count, dp_at = lax.axis_size("dp"), lax.axis_index("dp")
    part_rows = model_dim // (seq_count * dp_count)
    f32, bf16 = jnp.float32, jnp.bfloat16

    def shifted(x, by, first=0, last=None):
        last = seq_count - 1 if last is None else last
        pairs = [
            (i, i + by) for i in range(first, last + 1) if 0 <= i + by < seq_count
        ]
        return lax.ppermute(x, "seq", pairs)

    def chain(own, by):
        total = jnp.zeros_like(own)
        for hop in range(seq_count - 1):
            at = hop if by > 0 else seq_count - 1 - hop
            total = total + shifted(total + own, by, at, at)
        return total

    def small_sums(own, by):
        total = jnp.zeros_like(own)
        for distance in range(1, seq_count):
            total = total + shifted(own, by * distance)
        return total

    def project(weight):
        return jnp.dot(tokens, weight, preferred_element_type=f32).astype(bf16)

    work = functools.partial(call, heads=heads, seg_len=seg_len, head_dim=head_dim)
    mix = jnp.repeat(jax.nn.sigmoid(gate_bias), head_dim)[None]
    has_prev = jnp.reshape((seq_at > 0).astype(jnp.int32), (1,))

    token_blocks = tokens.reshape(seg_len, seq_count, dp_count, part_rows)

    def rows_for(core):
        return lax.dynamic_index_in_dim(token_blocks, core, 2, False).reshape(
            seg_len, seq_count * part_rows
        )

    def from_core(x, step):
        return lax.ppermute(x, "dp", [(i, (i + step) % dp_count) for i in range(dp_count)])

    key = project(w_key)
    key_prev = shifted(key, 1)
    value = project(w_value)
    value_prev = shifted(value, 1)
    memory_own, norm_own = work(
        write_kernel, ins="cc", outs=(("m", f32), ("r", f32)), flops=3 * 10**8
    )(key, value)
    norm = small_sums(norm_own, 1)
    memory = chain(memory_own, 1)
    cot_next = shifted(cot, -1)
    query = project(w_query)
    query_next = shifted(query, -1)
    (grad_memory_own,) = work(
        grad_memory_kernel, ins="ccrr", outs=(("m", f32),), flops=3 * 10**8
    )(query, cot, norm, mix)
    grad_memory = chain(grad_memory_own, -1)

    token_parts = [rows_for(dp_at)] + [
        from_core(rows_for((dp_at + step) % dp_count), step) for step in range(1, dp_count)
    ]

    local_out, grad_att, stats = work(
        attend_kernel,
        ins="fccccccr",
        outs=(("c", f32), ("c", f32), ("s", f32)),
        flops=2 * 10**9,
    )(has_prev, query, key, value, key_prev, value_prev, cot, mix)
    stats_next = shifted(stats, -1)
    blended, grad_query, grad_norm_own = work(
        retrieve_kernel,
        ins="ccmrrcc",
        outs=(("c", bf16), ("c", bf16), ("r", f32)),
        flops=6 * 10**8,
    )(query, cot, memory, norm, mix, local_out, grad_att)
    grad_norm = small_sums(grad_norm_own, -1)
    grad_key_rest, grad_value = work(
        key_value_kernel, ins="ccccsccsmr", outs=(("c", f32), ("c", bf16)), flops=2 * 10**9
    )(key, value, query, cot, stats, query_next, cot_next, stats_next, grad_memory, mix)
    grad_key = (grad_key_rest + grad_norm * feature_slope(key.astype(f32))).astype(bf16)

    contract = (((0,), (0,)), ((), ()))
    grad_scale = 1.0 / math.sqrt(seq_count * dp_count * seg_len)

    def weight_term(grad):
        grads = [grad] + [from_core(grad, step) for step in range(1, dp_count)]
        total = None
        for rows, term in zip(token_parts, grads):
            product = lax.dot_general(rows, term, contract, preferred_element_type=f32)
            total = product if total is None else total + product
        terms = total.reshape(seq_count, part_rows, columns)

        def block(index):
            return lax.dynamic_index_in_dim(terms, jnp.clip(index, 0, seq_count - 1), 0, False)

        ups = jnp.zeros((part_rows, columns), bf16)
        downs = ups
        for turn in range(1, seq_count):
            ahead = seq_count - turn
            ups = shifted(
                (ups.astype(f32) + block(seq_at + ahead)).astype(bf16), 1, 0, turn - 1
            )
            downs = shifted(
                (downs.astype(f32) + block(seq_at - ahead)).astype(bf16), -1, ahead
            )
        return (ups.astype(f32) + downs.astype(f32) + block(seq_at)) * grad_scale

    pieces = [weight_term(grad) for grad in (grad_query, grad_key, grad_value)]
    return (blended[None], jnp.stack(pieces, 1))


def solution(mesh):
    return jax.shard_map(
        local,
        mesh=mesh,
        in_specs=(
            P("dp", "seq", None),
            P(None, "head"),
            P(None, "head"),
            P(None, "head"),
            P("head"),
            P("dp", "seq", "head"),
        ),
        out_specs=(P("dp", "seq", "head"), P(("seq", "dp"), None, "head")),
        check_vma=False,
    )
```

time: 408 us -> 202 us (0.50)
  waiting for transfers between devices: 205 us -> 69.2 us
  starting transfers between devices: 7.39 us -> 77.8 us
  matrix products: 75.4 us -> 16.1 us
  blocking collectives: 57.1 us -> 0 us
  local copies, waits for them, and re-layouts: 27.1 us -> 11.7 us
  between operations: 14 us -> 1.42 us
  Pallas kernels: 0 us -> 11.9 us
  other arithmetic: 21 us -> 12.8 us
    reduce_scatter x1 -> x0, waiting for transfers between devices: 181 us -> none  [local(): lax.psum_scatter(lax.dot_general(tokens, grad_all, contract, preferred_el...]
    ppermute x2 -> x39, starting transfers between devices: 7.27 us -> 77.8 us  [the longest x35 77.1 us: shifted(): return lax.ppermute(x, 'seq', pairs)]
    all_gather x2 -> x0, blocking collectives: 57.1 us -> none  [prefix(): pieces = jax.tree.map(lambda part: lax.all_gather(part, axis), value)]
    dot_general x17 -> x9, matrix products: 71 us -> 16.1 us  [the longest x6 9.67 us: weight_term(): product = lax.dot_general(rows, term, contract, preferred_element_type=f32)]
    ppermute x2 -> x39, waiting for transfers between devices: 24.5 us -> 69.2 us  [the longest x35 69.2 us: shifted(): return lax.ppermute(x, 'seq', pairs)]
    select_n x12 -> x0, other arithmetic: 12.3 us -> none  [turn(): jnp.where(position < mine, new, old)]
    pallas_call x0 -> x5, Pallas kernels: none -> 11.9 us  [the longest x1 3.92 us: local(): work(key_value_kernel, ins='ccccsccsmr', outs=(('c', f32), ('c', bf16)),...]
    add x2 -> x8, other arithmetic: 0.01 us -> 8.64 us  [the longest x6 8.63 us: chain(): total = total + shifted(total + own, by, at, at)]
  transfers between devices with their start and end apart: 5 -> 39, of which waited for: 2 -> 13; matrix products, arithmetic and copies ran while one was open for 17% -> 15% of each run, Pallas kernels for 0% -> 5%
where the time goes in v1:
time: 202 us; the launch traced here: 201 us
  starting transfers between devices  77.8 us (39%)
  waiting for transfers between devices  69.2 us (34%)
  matrix products  16.1 us (8%)
  other arithmetic  12.8 us (6%)
  Pallas kernels  11.9 us (6%)
  local copies, waits for them, and re-layouts  11.7 us (6%)
    ppermute x35, starting transfers between devices, shifted(): return lax.ppermute(x, 'seq', pairs)  77.1 us
    ppermute x35, waiting for transfers between devices, shifted(): return lax.ppermute(x, 'seq', pairs)  69.2 us
    dot_general x6, matrix products, weight_term(): product = lax.dot_general(rows, term, contract, preferred_element_type=f32)  9.67 us
    add x6, other arithmetic, chain(): total = total + shifted(total + own, by, at, at)  8.63 us
    unnamed x33, local copies, waits for them, and re-layouts  8 us
    dot_general x3, matrix products, project(): return jnp.dot(tokens, weight, preferred_element_type=f32).astype(bf16)  6.43 us
  transfers between devices with their start and end apart: 39, of which 13 were waited for; matrix products, arithmetic and copies ran while one was open for 15% of the time, Pallas kernels for 5%

profile of v1, /device:TPU:0, one launch (start us, length us, event | category | flops | bytes accessed | tf_op | source)
XLA Modules:
  0.0 200.9 jit_solution(16333250557229066521)
XLA Ops:
  0.7 1.9 copy-done
  2.5 3.7 %fusion.9.key_ref = bf16[384,512]{1,0:T(8,128)(2,1)S(1)} fusion(bf16[3072,512]{1,0:T(8,128)(2,1)S(1)} %copy-done, bf16[1,384,3072]{2,1,0:T(8,128)(2,1)} %param.6), kind=kOutput, calls=%fused_computation.11 | convolution fusion | flops 1208156160 | bytes 5898240 | tf_op jit(solution)/shard_map/dot_general | solution.py:251
  6.2 1.4 fusion.12.value_ref
  8.6 4.9 %collective-permute-start.3 = (f32[1,512]{1,0:T(1,128)S(1)}, f32[1,512]{1,0:T(1,128)S(1)}, u32[]{:S(2)}, u32[]{:S(2)}) collective-permute-start(f32[1,512]{1,0:T(1,128)S(1)} %get-tuple-element.13), channel_id=1, source_target_pairs={{0,8},{8,16},{16,24},{1,9},{9,17},{17,25},{2,10},{10,18},{18,26},{... | collective-permute-start | bytes 6152 | tf_op jit(solution)/shard_map/ppermute | solution.py:235
  13.5 4.5 %collective-permute-start.4 = (f32[1,512]{1,0:T(1,128)S(1)}, f32[1,512]{1,0:T(1,128)S(1)}, u32[]{:S(2)}, u32[]{:S(2)}) collective-permute-start(f32[1,512]{1,0:T(1,128)S(1)} %get-tuple-element.13), channel_id=1, source_target_pairs={{0,16},{8,24},{1,17},{9,25},{2,18},{10,26},{3,19},{11,27},{4,20},{... | collective-permute-start | bytes 6152 | tf_op jit(solution)/shard_map/ppermute | solution.py:235
  18.0 1.3 collective-permute-start.5
  19.3 1.5 collective-permute-start
  20.8 1.4 fusion.6.query_ref
  22.3 1.2 shard_map.80
  24.2 7.4 %collective-permute-done = f32[2,256,256]{2,1,0:T(8,128)S(1)} collective-permute-done((f32[2,256,256]{2,1,0:T(8,128)S(1)}, f32[2,256,256]{2,1,0:T(8,128)S(1)}, u32[]{:S(2)}, u32[]{:S(2)}) %collective-permute-start) | collective-permute-done | bytes 524320 | tf_op jit(solution)/shard_map/ppermute | solution.py:235
  31.7 1.0 add.165
  32.6 1.5 collective-permute-start.1
  35.1 1.5 collective-permute-start.20
  36.5 4.9 %collective-permute-start.6 = (bf16[384,512]{1,0:T(8,128)(2,1)S(1)}, bf16[384,512]{1,0:T(8,128)(2,1)S(1)}, u32[]{:S(2)}, u32[]{:S(2)}) collective-permute-start(bf16[384,512]{1,0:T(8,128)(2,1)S(1)} %fusion.9.key_ref), channel_id=1, source_target_pairs={{0,8},{8,16},{16,24},{1,9},{9,17},{17,25},{2,10},{10,18},{18,26},{... | collective-permute-start | bytes 1179656 | tf_op jit(solution)/shard_map/ppermute | solution.py:235
  41.4 5.3 %collective-permute-start.7 = (bf16[384,512]{1,0:T(8,128)(2,1)S(1)}, bf16[384,512]{1,0:T(8,128)(2,1)S(1)}, u32[]{:S(2)}, u32[]{:S(2)}) collective-permute-start(bf16[384,512]{1,0:T(8,128)(2,1)S(1)} %fusion.12.value_ref), channel_id=1, source_target_pairs={{0,8},{8,16},{16,24},{1,9},{9,17},{17,25},{2,10},{10,18},{18,26},{... | collective-permute-start | bytes 1179656 | tf_op jit(solution)/shard_map/ppermute | solution.py:235
  46.8 4.3 %copy.8 = bf16[1,384,3072]{1,2,0:T(8,128)(2,1)} copy(bf16[1,384,3072]{2,1,0:T(8,128)(2,1)} %param.6) | data formatting | bytes 4718592 | tf_op args[0]
  51.1 3.4 %constant_dynamic-slice_fusion.1 = (bf16[384,4,1,384]{0,3,2,1:T(8,128)(2,1)}, bf16[384,4,1,384]{0,3,2,1:T(8,128)(2,1)}) fusion(bf16[384,4,2,384]{0,3,2,1:T(8,128)(2,1)} %bitcast.150, s32[]{:T(128)S(6)} %select_n.40, s32[]{:T(128)S(6)} %select_n.42), kind=kLoop, calls=%fused_computation.66 | loop fusion | bytes 4718600 | tf_op jit(solution)/shard_map/jit(dynamic_index_in_dim)/dynamic_slice | solution.py:260
  54.4 2.1 %fusion.45 = (f32[2,256,256]{2,1,0:T(8,128)}, f32[2,256,256]{2,1,0:T(8,128)}) fusion(f32[2,256,256]{2,1,0:T(8,128)S(1)} %get-tuple-element.12, f32[2,256,256]{2,1,0:T(8,128)S(1)} %copy-done.8, f32[2,256,256]{2,1,0:T(8,128)} %collective-permute-done.1), kind=kLoop, calls=%fused_computation.72 | loop fusion | flops 262144 | bytes 2621440 | tf_op jit(solution)/shard_map/add | solution.py:241
  56.6 1.5 collective-permute-start.2
  58.0 2.2 %fusion.44 = (f32[2,256,256]{2,1,0:T(8,128)}, f32[2,256,256]{2,1,0:T(8,128)}) fusion(f32[2,256,256]{2,1,0:T(8,128)S(1)} %shard_map.80, f32[2,256,256]{2,1,0:T(8,128)S(1)} %copy-done.10, f32[2,256,256]{2,1,0:T(8,128)} %collective-permute-done.20), kind=kLoop, calls=%fused_computation.71 | loop fusion | flops 262144 | bytes 2621440 | tf_op jit(solution)/shard_map/add | solution.py:241
  60.2 1.3 collective-permute-start.21
  61.5 1.3 collective-permute-start.16
  63.6 1.3 collective-permute-start.17
  64.9 1.0 copy-done.4
  65.9 3.8 %shard_map.78 = (f32[384,512]{1,0:T(8,128)S(1)}, f32[384,512]{1,0:T(8,128)S(1)}, f32[16,384]{1,0:T(8,128)S(1)}) custom-call(s32[1]{0:T(128)} %bitcast.2.has_prev_ref, bf16[384,512]{1,0:T(8,128)(2,1)S(1)} %fusion.6.query_ref, bf16[384,512]{1,0:T(8,128)(2,1)S(1)} %fusion.9.key_ref, bf16[384,512]{1,0:T(8,128)(2,1)S(1)} %fusion.12.value_ref, ...), custom_call_target="tpu_custom_call" | custom-call | flops 2000000000 | bytes 4194304 | tf_op jit(solution)/shard_map/pallas_call | solution.py:288
  69.6 1.1 add.168.memory_ref
  70.8 2.1 %shard_map.79 = (bf16[384,512]{1,0:T(8,128)(2,1)}, bf16[384,512]{1,0:T(8,128)(2,1)S(1)}, f32[1,512]{1,0:T(1,128)S(1)}) custom-call(bf16[384,512]{1,0:T(8,128)(2,1)S(1)} %fusion.6.query_ref, bf16[384,512]{1,0:T(8,128)(2,1)S(1)} %bitcast.129, f32[2,256,256]{2,1,0:T(8,128)S(1)} %add.168.memory_ref, f32[1,512]{1,0:T(1,128)S(1)} %add_add_fusion.1.norm_ref, ...), custom_call_target="tpu_custom_call" | custom-call | flops 600000000 | bytes 4194304 | tf_op jit(solution)/shard_map/pallas_call | solution.py:295
  72.9 1.3 collective-permute-start.22
  74.1 19.4 %collective-permute-done.22 = f32[1,512]{1,0:T(1,128)S(1)} collective-permute-done((f32[1,512]{1,0:T(1,128)S(1)}, f32[1,512]{1,0:T(1,128)S(1)}, u32[]{:S(2)}, u32[]{:S(2)}) %collective-permute-start.22) | collective-permute-done | bytes 2080 | tf_op jit(solution)/shard_map/ppermute | solution.py:235
  93.5 1.3 collective-permute-start.23
  94.8 5.1 %collective-permute-done.23 = f32[1,512]{1,0:T(1,128)S(1)} collective-permute-done((f32[1,512]{1,0:T(1,128)S(1)}, f32[1,512]{1,0:T(1,128)S(1)}, u32[]{:S(2)}, u32[]{:S(2)}) %collective-permute-start.23) | collective-permute-done | bytes 2080 | tf_op jit(solution)/shard_map/ppermute | solution.py:235
  99.9 1.3 collective-permute-start.24
  101.2 6.0 %collective-permute-done.24 = f32[1,512]{1,0:T(1,128)S(1)} collective-permute-done((f32[1,512]{1,0:T(1,128)S(1)}, f32[1,512]{1,0:T(1,128)S(1)}, u32[]{:S(2)}, u32[]{:S(2)}) %collective-permute-start.24) | collective-permute-done | bytes 2080 | tf_op jit(solution)/shard_map/ppermute | solution.py:235
  107.2 1.5 collective-permute-start.18
  108.7 1.3 add.189.grad_memory_ref
  110.0 2.8 %collective-permute-done.18.stats_next_ref = f32[16,384]{1,0:T(8,128)S(1)} collective-permute-done((f32[16,384]{1,0:T(8,128)S(1)}, f32[16,384]{1,0:T(8,128)S(1)}, u32[]{:S(2)}, u32[]{:S(2)}) %collective-permute-start.18) | collective-permute-done | bytes 24608 | tf_op jit(solution)/shard_map/ppermute | solution.py:235
  112.9 3.9 %shard_map.81 = (f32[384,512]{1,0:T(8,128)S(1)}, bf16[384,512]{1,0:T(8,128)(2,1)S(1)}) custom-call(bf16[384,512]{1,0:T(8,128)(2,1)S(1)} %fusion.9.key_ref, bf16[384,512]{1,0:T(8,128)(2,1)S(1)} %fusion.12.value_ref, bf16[384,512]{1,0:T(8,128)(2,1)S(1)} %fusion.6.query_ref, bf16[384,512]{1,0:T(8,128)(2,1)S(1)} %bitcast.130, ...), custom_call_target="tpu_custom_call" | custom-call | flops 2000000000 | bytes 4194304 | tf_op jit(solution)/shard_map/pallas_call | solution.py:302
  117.6 2.2 %fusion.46 = f32[1536,512]{1,0:T(8,128)S(1)} fusion(bf16[384,1536]{0,1:T(8,128)(2,1)} %collective-permute-done.8, bf16[384,512]{1,0:T(8,128)(2,1)S(1)} %collective-permute-done.9), kind=kOutput, calls=%fused_computation.73 | convolution fusion | flops 603979776 | bytes 4718592 | tf_op jit(solution)/shard_map/dot_general | solution.py:314
  119.9 1.0 convolution_add_fusion.2
  121.0 1.8 collective-permute-start.10
  123.5 2.2 %fusion.47 = f32[1536,512]{1,0:T(8,128)S(1)} fusion(bf16[384,1536]{0,1:T(8,128)(2,1)} %collective-permute-done.8, bf16[384,512]{1,0:T(8,128)(2,1)S(1)} %collective-permute-done.25), kind=kOutput, calls=%fused_computation.74 | convolution fusion | flops 603979776 | bytes 4718592 | tf_op jit(solution)/shard_map/dot_general | solution.py:314
  125.8 1.0 convolution_add_fusion.1
  126.9 1.3 collective-permute-start.26
  128.9 2.2 %fusion.48 = f32[1536,512]{1,0:T(8,128)S(1)} fusion(bf16[384,1536]{0,1:T(8,128)(2,1)} %collective-permute-done.8, bf16[384,512]{1,0:T(8,128)(2,1)S(1)} %collective-permute-done.32), kind=kOutput, calls=%fused_computation.75 | convolution fusion | flops 603979776 | bytes 4718592 | tf_op jit(solution)/shard_map/dot_general | solution.py:314
  131.1 1.0 convolution_add_fusion
  132.2 1.3 collective-permute-start.33
  134.6 3.0 %collective-permute-start.11 = (bf16[384,512]{1,0:T(8,128)(2,1)S(1)}, bf16[384,512]{1,0:T(8,128)(2,1)S(1)}, u32[]{:S(2)}, u32[]{:S(2)}) collective-permute-start(bf16[384,512]{1,0:T(8,128)(2,1)S(1)} %get-tuple-element.28), channel_id=1, source_target_pairs={{0,8},{8,16},{1,9},{9,17},{2,10},{10,18},{3,11},{11,19},{4,12},{12... | collective-permute-start | bytes 1179656 | tf_op jit(solution)/shard_map/ppermute | solution.py:235
  137.6 3.0 %collective-permute-done.26 = bf16[384,512]{1,0:T(8,128)(2,1)S(1)} collective-permute-done((bf16[384,512]{1,0:T(8,128)(2,1)S(1)}, bf16[384,512]{1,0:T(8,128)(2,1)S(1)}, u32[]{:S(2)}, u32[]{:S(2)}) %collective-permute-start.26) | collective-permute-done | bytes 393248 | tf_op jit(solution)/shard_map/ppermute | solution.py:235
  141.6 5.0 %collective-permute-start.27 = (bf16[384,512]{1,0:T(8,128)(2,1)S(1)}, bf16[384,512]{1,0:T(8,128)(2,1)S(1)}, u32[]{:S(2)}, u32[]{:S(2)}) collective-permute-start(bf16[384,512]{1,0:T(8,128)(2,1)S(1)} %get-tuple-element.34), channel_id=1, source_target_pairs={{0,8},{8,16},{1,9},{9,17},{2,10},{10,18},{3,11},{11,19},{4,12},{12... | collective-permute-start | bytes 1179656 | tf_op jit(solution)/shard_map/ppermute | solution.py:235
  146.7 2.4 %collective-permute-done.33 = bf16[384,512]{1,0:T(8,128)(2,1)S(1)} collective-permute-done((bf16[384,512]{1,0:T(8,128)(2,1)S(1)}, bf16[384,512]{1,0:T(8,128)(2,1)S(1)}, u32[]{:S(2)}, u32[]{:S(2)}) %collective-permute-start.33) | collective-permute-done | bytes 393248 | tf_op jit(solution)/shard_map/ppermute | solution.py:235
  150.0 5.0 %collective-permute-start.34 = (bf16[384,512]{1,0:T(8,128)(2,1)S(1)}, bf16[384,512]{1,0:T(8,128)(2,1)S(1)}, u32[]{:S(2)}, u32[]{:S(2)}) collective-permute-start(bf16[384,512]{1,0:T(8,128)(2,1)S(1)} %get-tuple-element.40), channel_id=1, source_target_pairs={{0,8},{8,16},{1,9},{9,17},{2,10},{10,18},{3,11},{11,19},{4,12},{12... | collective-permute-start | bytes 1179656 | tf_op jit(solution)/shard_map/ppermute | solution.py:235
  155.1 2.4 %collective-permute-done.11 = bf16[384,512]{1,0:T(8,128)(2,1)S(1)} collective-permute-done((bf16[384,512]{1,0:T(8,128)(2,1)S(1)}, bf16[384,512]{1,0:T(8,128)(2,1)S(1)}, u32[]{:S(2)}, u32[]{:S(2)}) %collective-permute-start.11) | collective-permute-done | bytes 393248 | tf_op jit(solution)/shard_map/ppermute | solution.py:235
  158.5 5.0 %collective-permute-start.12 = (bf16[384,512]{1,0:T(8,128)(2,1)S(1)}, bf16[384,512]{1,0:T(8,128)(2,1)S(1)}, u32[]{:S(2)}, u32[]{:S(2)}) collective-permute-start(bf16[384,512]{1,0:T(8,128)(2,1)S(1)} %get-tuple-element.26), channel_id=1, source_target_pairs={{0,8},{8,16},{16,24},{1,9},{9,17},{17,25},{2,10},{10,18},{18,26},{... | collective-permute-start | bytes 1179656 | tf_op jit(solution)/shard_map/ppermute | solution.py:235
  163.5 2.4 %collective-permute-done.27 = bf16[384,512]{1,0:T(8,128)(2,1)S(1)} collective-permute-done((bf16[384,512]{1,0:T(8,128)(2,1)S(1)}, bf16[384,512]{1,0:T(8,128)(2,1)S(1)}, u32[]{:S(2)}, u32[]{:S(2)}) %collective-permute-start.27) | collective-permute-done | bytes 393248 | tf_op jit(solution)/shard_map/ppermute | solution.py:235
  165.9 1.3 collective-permute-start.15
  167.5 5.0 %collective-permute-start.28 = (bf16[384,512]{1,0:T(8,128)(2,1)S(1)}, bf16[384,512]{1,0:T(8,128)(2,1)S(1)}, u32[]{:S(2)}, u32[]{:S(2)}) collective-permute-start(bf16[384,512]{1,0:T(8,128)(2,1)S(1)} %get-tuple-element.32), channel_id=1, source_target_pairs={{0,8},{8,16},{16,24},{1,9},{9,17},{17,25},{2,10},{10,18},{18,26},{... | collective-permute-start | bytes 1179656 | tf_op jit(solution)/shard_map/ppermute | solution.py:235
  172.6 1.8 collective-permute-done.34
  174.3 1.3 collective-permute-start.31
  175.9 5.0 %collective-permute-start.35 = (bf16[384,512]{1,0:T(8,128)(2,1)S(1)}, bf16[384,512]{1,0:T(8,128)(2,1)S(1)}, u32[]{:S(2)}, u32[]{:S(2)}) collective-permute-start(bf16[384,512]{1,0:T(8,128)(2,1)S(1)} %get-tuple-element.38), channel_id=1, source_target_pairs={{0,8},{8,16},{16,24},{1,9},{9,17},{17,25},{2,10},{10,18},{18,26},{... | collective-permute-start | bytes 1179656 | tf_op jit(solution)/shard_map/ppermute | solution.py:235
  181.0 1.8 collective-permute-done.12
  182.8 1.3 collective-permute-start.38
  184.3 6.9 %collective-permute-done.28 = bf16[384,512]{1,0:T(8,128)(2,1)S(1)} collective-permute-done((bf16[384,512]{1,0:T(8,128)(2,1)S(1)}, bf16[384,512]{1,0:T(8,128)(2,1)S(1)}, u32[]{:S(2)}, u32[]{:S(2)}) %collective-permute-start.28) | collective-permute-done | bytes 393248 | tf_op jit(solution)/shard_map/ppermute | solution.py:235
  191.4 7.8 %collective-permute-done.35 = bf16[384,512]{1,0:T(8,128)(2,1)S(1)} collective-permute-done((bf16[384,512]{1,0:T(8,128)(2,1)S(1)}, bf16[384,512]{1,0:T(8,128)(2,1)S(1)}, u32[]{:S(2)}, u32[]{:S(2)}) %collective-permute-start.35) | collective-permute-done | bytes 393248 | tf_op jit(solution)/shard_map/ppermute | solution.py:235
  199.3 1.6 pad_maximum_fusion
  (85 shorter events, 11.2 us)
Async XLA Ops:
  0.6 1.9 copy-start
  0.6 5.6 %copy-start.6 = (bf16[1,384,3072]{2,1,0:T(8,128)(2,1)S(1)}, bf16[1,384,3072]{2,1,0:T(8,128)(2,1)}, u32[]{:S(2)}) copy-start(bf16[1,384,3072]{2,1,0:T(8,128)(2,1)} %param.6) | copy-start | bytes 7077892
  0.7 5.6 %copy-start.12 = (bf16[3072,512]{1,0:T(8,128)(2,1)S(1)}, bf16[3072,512]{1,0:T(8,128)(2,1)}, u32[]{:S(2)}) copy-start(bf16[3072,512]{1,0:T(8,128)(2,1)} %param.9) | copy-start | bytes 9437188
  6.2 14.6 %copy-start.13 = (bf16[3072,512]{1,0:T(8,128)(2,1)S(1)}, bf16[3072,512]{1,0:T(8,128)(2,1)}, u32[]{:S(2)}) copy-start(bf16[3072,512]{1,0:T(8,128)(2,1)} %param.7) | copy-start | bytes 9437188
  8.6 13.7 %collective-permute-start.3 = (f32[1,512]{1,0:T(1,128)S(1)}, f32[1,512]{1,0:T(1,128)S(1)}, u32[]{:S(2)}, u32[]{:S(2)}) collective-permute-start(f32[1,512]{1,0:T(1,128)S(1)} %get-tuple-element.13), channel_id=1, source_target_pairs={{0,8},{8,16},{16,24},{1,9},{9,17},{17,25},{2,10},{10,18},{18,26},{... | collective-permute-start | bytes 6152 | tf_op jit(solution)/shard_map/ppermute | solution.py:235
  13.5 8.8 %collective-permute-start.4 = (f32[1,512]{1,0:T(1,128)S(1)}, f32[1,512]{1,0:T(1,128)S(1)}, u32[]{:S(2)}, u32[]{:S(2)}) collective-permute-start(f32[1,512]{1,0:T(1,128)S(1)} %get-tuple-element.13), channel_id=1, source_target_pairs={{0,16},{8,24},{1,17},{9,25},{2,18},{10,26},{3,19},{11,27},{4,20},{... | collective-permute-start | bytes 6152 | tf_op jit(solution)/shard_map/ppermute | solution.py:235
  18.0 4.3 %collective-permute-start.5 = (f32[1,512]{1,0:T(1,128)S(1)}, f32[1,512]{1,0:T(1,128)S(1)}, u32[]{:S(2)}, u32[]{:S(2)}) collective-permute-start(f32[1,512]{1,0:T(1,128)S(1)} %get-tuple-element.13), channel_id=1, source_target_pairs={{0,24},{1,25},{2,26},{3,27},{4,28},{5,29},{6,30},{7,31}} | collective-permute-start | bytes 6152 | tf_op jit(solution)/shard_map/ppermute | solution.py:235
  19.3 2.9 %copy-start.14 = (f32[2]{0:T(128)S(1)}, f32[2]{0:T(128)}, u32[]{:S(2)}) copy-start(f32[2]{0:T(128)} %param.10) | copy-start | bytes 28
  19.3 3.0 %copy-start.2 = (bf16[1,384,512]{2,1,0:T(8,128)(2,1)S(1)}, bf16[1,384,512]{2,1,0:T(8,128)(2,1)}, u32[]{:S(2)}) copy-start(bf16[1,384,512]{2,1,0:T(8,128)(2,1)} %param.11) | copy-start | bytes 1179652
  19.3 12.3 %collective-permute-start = (f32[2,256,256]{2,1,0:T(8,128)S(1)}, f32[2,256,256]{2,1,0:T(8,128)S(1)}, u32[]{:S(2)}, u32[]{:S(2)}) collective-permute-start(f32[2,256,256]{2,1,0:T(8,128)S(1)} %get-tuple-element.12), channel_id=1, source_target_pairs={{0,8},{1,9},{2,10},{3,11},{4,12},{5,13},{6,14},{7,15}} | collective-permute-start | bytes 1572872 | tf_op jit(solution)/shard_map/ppermute | solution.py:235
  23.5 10.6 %collective-permute-start.19 = (f32[2,256,256]{2,1,0:T(8,128)S(1)}, f32[2,256,256]{2,1,0:T(8,128)S(1)}, u32[]{:S(2)}, u32[]{:S(2)}) collective-permute-start(f32[2,256,256]{2,1,0:T(8,128)S(1)} %shard_map.80), channel_id=1, source_target_pairs={{24,16},{25,17},{26,18},{27,19},{28,20},{29,21},{30,22},{31,23}} | collective-permute-start | bytes 1572872 | tf_op jit(solution)/shard_map/ppermute | solution.py:235
  31.7 3.4 %copy-start.7 = (f32[2,256,256]{2,1,0:T(8,128)}, f32[2,256,256]{2,1,0:T(8,128)S(1)}, u32[]{:S(2)}) copy-start(f32[2,256,256]{2,1,0:T(8,128)S(1)} %collective-permute-done) | copy-start | bytes 1572868
  32.6 21.8 %collective-permute-start.1 = (f32[2,256,256]{2,1,0:T(8,128)}, f32[2,256,256]{2,1,0:T(8,128)}, u32[]{:S(2)}, u32[]{:S(2)}) collective-permute-start(f32[2,256,256]{2,1,0:T(8,128)} %add.165), channel_id=1, source_target_pairs={{8,16},{9,17},{10,18},{11,19},{12,20},{13,21},{14,22},{15,23}} | collective-permute-start | bytes 1572872 | tf_op jit(solution)/shard_map/ppermute | solution.py:235
  34.1 2.4 %copy-start.9 = (f32[2,256,256]{2,1,0:T(8,128)}, f32[2,256,256]{2,1,0:T(8,128)S(1)}, u32[]{:S(2)}) copy-start(f32[2,256,256]{2,1,0:T(8,128)S(1)} %collective-permute-done.19) | copy-start | bytes 1572868
  35.1 23.0 %collective-permute-start.20 = (f32[2,256,256]{2,1,0:T(8,128)}, f32[2,256,256]{2,1,0:T(8,128)}, u32[]{:S(2)}, u32[]{:S(2)}) collective-permute-start(f32[2,256,256]{2,1,0:T(8,128)} %add.186), channel_id=1, source_target_pairs={{16,8},{17,9},{18,10},{19,11},{20,12},{21,13},{22,14},{23,15}} | collective-permute-start | bytes 1572872 | tf_op jit(solution)/shard_map/ppermute | solution.py:235
  36.5 25.0 %collective-permute-start.6 = (bf16[384,512]{1,0:T(8,128)(2,1)S(1)}, bf16[384,512]{1,0:T(8,128)(2,1)S(1)}, u32[]{:S(2)}, u32[]{:S(2)}) collective-permute-start(bf16[384,512]{1,0:T(8,128)(2,1)S(1)} %fusion.9.key_ref), channel_id=1, source_target_pairs={{0,8},{8,16},{16,24},{1,9},{9,17},{17,25},{2,10},{10,18},{18,26},{... | collective-permute-start | bytes 1179656 | tf_op jit(solution)/shard_map/ppermute | solution.py:235
  41.4 21.4 %collective-permute-start.7 = (bf16[384,512]{1,0:T(8,128)(2,1)S(1)}, bf16[384,512]{1,0:T(8,128)(2,1)S(1)}, u32[]{:S(2)}, u32[]{:S(2)}) collective-permute-start(bf16[384,512]{1,0:T(8,128)(2,1)S(1)} %fusion.12.value_ref), channel_id=1, source_target_pairs={{0,8},{8,16},{16,24},{1,9},{9,17},{17,25},{2,10},{10,18},{18,26},{... | collective-permute-start | bytes 1179656 | tf_op jit(solution)/shard_map/ppermute | solution.py:235
  51.1 3.4 %copy-start.8 = (f32[2,256,256]{2,1,0:T(8,128)S(1)}, f32[2,256,256]{2,1,0:T(8,128)}, u32[]{:S(2)}) copy-start(f32[2,256,256]{2,1,0:T(8,128)} %copy-done.7) | copy-start | bytes 1572868
  51.1 7.0 %copy-start.10 = (f32[2,256,256]{2,1,0:T(8,128)S(1)}, f32[2,256,256]{2,1,0:T(8,128)}, u32[]{:S(2)}) copy-start(f32[2,256,256]{2,1,0:T(8,128)} %copy-done.9) | copy-start | bytes 1572868
  54.4 63.2 %collective-permute-start.8 = (bf16[384,1536]{0,1:T(8,128)(2,1)}, bf16[384,1536]{0,1:T(8,128)(2,1)}, u32[]{:S(2)}, u32[]{:S(2)}) collective-permute-start(bf16[384,1536]{0,1:T(8,128)(2,1)} %bitcast.6), channel_id=1, source_target_pairs={{0,4},{4,0},{1,5},{5,1},{2,6},{6,2},{3,7},{7,3},{8,12},{12,8},{9,1... | collective-permute-start | bytes 3538952 | tf_op jit(solution)/shard_map/ppermute | solution.py:265
  56.6 13.0 %collective-permute-start.2 = (f32[2,256,256]{2,1,0:T(8,128)}, f32[2,256,256]{2,1,0:T(8,128)}, u32[]{:S(2)}, u32[]{:S(2)}) collective-permute-start(f32[2,256,256]{2,1,0:T(8,128)} %get-tuple-element.24), channel_id=1, source_target_pairs={{16,24},{17,25},{18,26},{19,27},{20,28},{21,29},{22,30},{23,31}} | collective-permute-start | bytes 1572872 | tf_op jit(solution)/shard_map/ppermute | solution.py:235
  60.2 48.4 %collective-permute-start.21 = (f32[2,256,256]{2,1,0:T(8,128)}, f32[2,256,256]{2,1,0:T(8,128)}, u32[]{:S(2)}, u32[]{:S(2)}) collective-permute-start(f32[2,256,256]{2,1,0:T(8,128)} %get-tuple-element.22), channel_id=1, source_target_pairs={{8,0},{9,1},{10,2},{11,3},{12,4},{13,5},{14,6},{15,7}} | collective-permute-start | bytes 1572872 | tf_op jit(solution)/shard_map/ppermute | solution.py:235
  61.5 48.5 %collective-permute-start.16 = (bf16[384,512]{1,0:T(8,128)(2,1)S(1)}, bf16[384,512]{1,0:T(8,128)(2,1)S(1)}, u32[]{:S(2)}, u32[]{:S(2)}) collective-permute-start(bf16[384,512]{1,0:T(8,128)(2,1)S(1)} %fusion.6.query_ref), channel_id=1, source_target_pairs={{8,0},{16,8},{24,16},{9,1},{17,9},{25,17},{10,2},{18,10},{26,18},{... | collective-permute-start | bytes 1179656 | tf_op jit(solution)/shard_map/ppermute | solution.py:235
  62.8 0.7 copy-start.3
  63.6 46.4 %collective-permute-start.17 = (bf16[384,512]{1,0:T(8,128)(2,1)S(1)}, bf16[384,512]{1,0:T(8,128)(2,1)S(1)}, u32[]{:S(2)}, u32[]{:S(2)}) collective-permute-start(bf16[384,512]{1,0:T(8,128)(2,1)S(1)} %bitcast.127), channel_id=1, source_target_pairs={{8,0},{16,8},{24,16},{9,1},{17,9},{25,17},{10,2},{18,10},{26,18},{... | collective-permute-start | bytes 1179656 | tf_op jit(solution)/shard_map/ppermute | solution.py:235
  64.9 1.0 copy-start.4
  65.9 3.8 %copy-start.11 = (f32[2,256,256]{2,1,0:T(8,128)S(1)}, f32[2,256,256]{2,1,0:T(8,128)}, u32[]{:S(2)}) copy-start(f32[2,256,256]{2,1,0:T(8,128)} %get-tuple-element.25) | copy-start | bytes 1572868
  72.9 20.7 %collective-permute-start.22 = (f32[1,512]{1,0:T(1,128)S(1)}, f32[1,512]{1,0:T(1,128)S(1)}, u32[]{:S(2)}, u32[]{:S(2)}) collective-permute-start(f32[1,512]{1,0:T(1,128)S(1)} %get-tuple-element.20), channel_id=1, source_target_pairs={{8,0},{16,8},{24,16},{9,1},{17,9},{25,17},{10,2},{18,10},{26,18},{... | collective-permute-start | bytes 6152 | tf_op jit(solution)/shard_map/ppermute | solution.py:235
  93.5 6.4 %collective-permute-start.23 = (f32[1,512]{1,0:T(1,128)S(1)}, f32[1,512]{1,0:T(1,128)S(1)}, u32[]{:S(2)}, u32[]{:S(2)}) collective-permute-start(f32[1,512]{1,0:T(1,128)S(1)} %get-tuple-element.20), channel_id=1, source_target_pairs={{16,0},{24,8},{17,1},{25,9},{18,2},{26,10},{19,3},{27,11},{20,4},{... | collective-permute-start | bytes 6152 | tf_op jit(solution)/shard_map/ppermute | solution.py:235
  99.9 7.3 %collective-permute-start.24 = (f32[1,512]{1,0:T(1,128)S(1)}, f32[1,512]{1,0:T(1,128)S(1)}, u32[]{:S(2)}, u32[]{:S(2)}) collective-permute-start(f32[1,512]{1,0:T(1,128)S(1)} %get-tuple-element.20), channel_id=1, source_target_pairs={{24,0},{25,1},{26,2},{27,3},{28,4},{29,5},{30,6},{31,7}} | collective-permute-start | bytes 6152 | tf_op jit(solution)/shard_map/ppermute | solution.py:235
  107.2 5.7 %collective-permute-start.18 = (f32[16,384]{1,0:T(8,128)S(1)}, f32[16,384]{1,0:T(8,128)S(1)}, u32[]{:S(2)}, u32[]{:S(2)}) collective-permute-start(f32[16,384]{1,0:T(8,128)S(1)} %get-tuple-element.18.stats_ref), channel_id=1, source_target_pairs={{8,0},{16,8},{24,16},{9,1},{17,9},{25,17},{10,2},{18,10},{26,18},{... | collective-permute-start | bytes 73736 | tf_op jit(solution)/shard_map/ppermute | solution.py:235
  108.7 9.0 %collective-permute-start.9 = (bf16[384,512]{1,0:T(8,128)(2,1)S(1)}, bf16[384,512]{1,0:T(8,128)(2,1)S(1)}, u32[]{:S(2)}, u32[]{:S(2)}) collective-permute-start(bf16[384,512]{1,0:T(8,128)(2,1)S(1)} %get-tuple-element.17), channel_id=1, source_target_pairs={{0,4},{4,0},{1,5},{5,1},{2,6},{6,2},{3,7},{7,3},{8,12},{12,8},{9,1... | collective-permute-start | bytes 1179656 | tf_op jit(solution)/shard_map/ppermute | solution.py:265
  116.8 3.1 %copy-start.5 = (bf16[384,4,1,384]{0,3,2,1:T(8,128)(2,1)S(1)}, bf16[384,4,1,384]{0,3,2,1:T(8,128)(2,1)}, u32[]{:S(2)}) copy-start(bf16[384,4,1,384]{0,3,2,1:T(8,128)(2,1)} %get-tuple-element.44) | copy-start | bytes 3538948
  117.0 6.5 %collective-permute-start.25 = (bf16[384,512]{1,0:T(8,128)(2,1)S(1)}, bf16[384,512]{1,0:T(8,128)(2,1)S(1)}, u32[]{:S(2)}, u32[]{:S(2)}) collective-permute-start(bf16[384,512]{1,0:T(8,128)(2,1)S(1)} %fusion.19), channel_id=1, source_target_pairs={{0,4},{4,0},{1,5},{5,1},{2,6},{6,2},{3,7},{7,3},{8,12},{12,8},{9,1... | collective-permute-start | bytes 1179656 | tf_op jit(solution)/shard_map/ppermute | solution.py:265
  117.1 11.8 %collective-permute-start.32 = (bf16[384,512]{1,0:T(8,128)(2,1)S(1)}, bf16[384,512]{1,0:T(8,128)(2,1)S(1)}, u32[]{:S(2)}, u32[]{:S(2)}) collective-permute-start(bf16[384,512]{1,0:T(8,128)(2,1)S(1)} %get-tuple-element.21), channel_id=1, source_target_pairs={{0,4},{4,0},{1,5},{5,1},{2,6},{6,2},{3,7},{7,3},{8,12},{12,8},{9,1... | collective-permute-start | bytes 1179656 | tf_op jit(solution)/shard_map/ppermute | solution.py:265
  121.0 12.6 %collective-permute-start.10 = (bf16[384,512]{1,0:T(8,128)(2,1)S(1)}, bf16[384,512]{1,0:T(8,128)(2,1)S(1)}, u32[]{:S(2)}, u32[]{:S(2)}) collective-permute-start(bf16[384,512]{1,0:T(8,128)(2,1)S(1)} %get-tuple-element.30), channel_id=1, source_target_pairs={{0,8},{1,9},{2,10},{3,11},{4,12},{5,13},{6,14},{7,15}} | collective-permute-start | bytes 1179656 | tf_op jit(solution)/shard_map/ppermute | solution.py:235
  122.8 11.5 %collective-permute-start.13 = (bf16[384,512]{1,0:T(8,128)(2,1)S(1)}, bf16[384,512]{1,0:T(8,128)(2,1)S(1)}, u32[]{:S(2)}, u32[]{:S(2)}) collective-permute-start(bf16[384,512]{1,0:T(8,128)(2,1)S(1)} %get-tuple-element.31), channel_id=1, source_target_pairs={{24,16},{25,17},{26,18},{27,19},{28,20},{29,21},{30,22},{31,23}} | collective-permute-start | bytes 1179656 | tf_op jit(solution)/shard_map/ppermute | solution.py:235
  126.9 13.8 %collective-permute-start.26 = (bf16[384,512]{1,0:T(8,128)(2,1)S(1)}, bf16[384,512]{1,0:T(8,128)(2,1)S(1)}, u32[]{:S(2)}, u32[]{:S(2)}) collective-permute-start(bf16[384,512]{1,0:T(8,128)(2,1)S(1)} %get-tuple-element.36), channel_id=1, source_target_pairs={{0,8},{1,9},{2,10},{3,11},{4,12},{5,13},{6,14},{7,15}} | collective-permute-start | bytes 1179656 | tf_op jit(solution)/shard_map/ppermute | solution.py:235
  128.2 13.1 %collective-permute-start.29 = (bf16[384,512]{1,0:T(8,128)(2,1)S(1)}, bf16[384,512]{1,0:T(8,128)(2,1)S(1)}, u32[]{:S(2)}, u32[]{:S(2)}) collective-permute-start(bf16[384,512]{1,0:T(8,128)(2,1)S(1)} %get-tuple-element.37), channel_id=1, source_target_pairs={{24,16},{25,17},{26,18},{27,19},{28,20},{29,21},{30,22},{31,23}} | collective-permute-start | bytes 1179656 | tf_op jit(solution)/shard_map/ppermute | solution.py:235
  132.2 16.8 %collective-permute-start.33 = (bf16[384,512]{1,0:T(8,128)(2,1)S(1)}, bf16[384,512]{1,0:T(8,128)(2,1)S(1)}, u32[]{:S(2)}, u32[]{:S(2)}) collective-permute-start(bf16[384,512]{1,0:T(8,128)(2,1)S(1)} %get-tuple-element.42), channel_id=1, source_target_pairs={{0,8},{1,9},{2,10},{3,11},{4,12},{5,13},{6,14},{7,15}} | collective-permute-start | bytes 1179656 | tf_op jit(solution)/shard_map/ppermute | solution.py:235
  133.6 16.2 %collective-permute-start.36 = (bf16[384,512]{1,0:T(8,128)(2,1)S(1)}, bf16[384,512]{1,0:T(8,128)(2,1)S(1)}, u32[]{:S(2)}, u32[]{:S(2)}) collective-permute-start(bf16[384,512]{1,0:T(8,128)(2,1)S(1)} %get-tuple-element.43), channel_id=1, source_target_pairs={{24,16},{25,17},{26,18},{27,19},{28,20},{29,21},{30,22},{31,23}} | collective-permute-start | bytes 1179656 | tf_op jit(solution)/shard_map/ppermute | solution.py:235
  134.6 22.9 %collective-permute-start.11 = (bf16[384,512]{1,0:T(8,128)(2,1)S(1)}, bf16[384,512]{1,0:T(8,128)(2,1)S(1)}, u32[]{:S(2)}, u32[]{:S(2)}) collective-permute-start(bf16[384,512]{1,0:T(8,128)(2,1)S(1)} %get-tuple-element.28), channel_id=1, source_target_pairs={{0,8},{8,16},{1,9},{9,17},{2,10},{10,18},{3,11},{11,19},{4,12},{12... | collective-permute-start | bytes 1179656 | tf_op jit(solution)/shard_map/ppermute | solution.py:235
  140.6 17.5 %collective-permute-start.14 = (bf16[384,512]{1,0:T(8,128)(2,1)S(1)}, bf16[384,512]{1,0:T(8,128)(2,1)S(1)}, u32[]{:S(2)}, u32[]{:S(2)}) collective-permute-start(bf16[384,512]{1,0:T(8,128)(2,1)S(1)} %get-tuple-element.29), channel_id=1, source_target_pairs={{16,8},{24,16},{17,9},{25,17},{18,10},{26,18},{19,11},{27,19},{20,... | collective-permute-start | bytes 1179656 | tf_op jit(solution)/shard_map/ppermute | solution.py:235
  141.6 24.3 %collective-permute-start.27 = (bf16[384,512]{1,0:T(8,128)(2,1)S(1)}, bf16[384,512]{1,0:T(8,128)(2,1)S(1)}, u32[]{:S(2)}, u32[]{:S(2)}) collective-permute-start(bf16[384,512]{1,0:T(8,128)(2,1)S(1)} %get-tuple-element.34), channel_id=1, source_target_pairs={{0,8},{8,16},{1,9},{9,17},{2,10},{10,18},{3,11},{11,19},{4,12},{12... | collective-permute-start | bytes 1179656 | tf_op jit(solution)/shard_map/ppermute | solution.py:235
  149.1 18.1 %collective-permute-start.30 = (bf16[384,512]{1,0:T(8,128)(2,1)S(1)}, bf16[384,512]{1,0:T(8,128)(2,1)S(1)}, u32[]{:S(2)}, u32[]{:S(2)}) collective-permute-start(bf16[384,512]{1,0:T(8,128)(2,1)S(1)} %get-tuple-element.35), channel_id=1, source_target_pairs={{16,8},{24,16},{17,9},{25,17},{18,10},{26,18},{19,11},{27,19},{20,... | collective-permute-start | bytes 1179656 | tf_op jit(solution)/shard_map/ppermute | solution.py:235
  150.0 24.3 %collective-permute-start.34 = (bf16[384,512]{1,0:T(8,128)(2,1)S(1)}, bf16[384,512]{1,0:T(8,128)(2,1)S(1)}, u32[]{:S(2)}, u32[]{:S(2)}) collective-permute-start(bf16[384,512]{1,0:T(8,128)(2,1)S(1)} %get-tuple-element.40), channel_id=1, source_target_pairs={{0,8},{8,16},{1,9},{9,17},{2,10},{10,18},{3,11},{11,19},{4,12},{12... | collective-permute-start | bytes 1179656 | tf_op jit(solution)/shard_map/ppermute | solution.py:235
  157.5 18.1 %collective-permute-start.37 = (bf16[384,512]{1,0:T(8,128)(2,1)S(1)}, bf16[384,512]{1,0:T(8,128)(2,1)S(1)}, u32[]{:S(2)}, u32[]{:S(2)}) collective-permute-start(bf16[384,512]{1,0:T(8,128)(2,1)S(1)} %get-tuple-element.41), channel_id=1, source_target_pairs={{16,8},{24,16},{17,9},{25,17},{18,10},{26,18},{19,11},{27,19},{20,... | collective-permute-start | bytes 1179656 | tf_op jit(solution)/shard_map/ppermute | solution.py:235
  158.5 24.3 %collective-permute-start.12 = (bf16[384,512]{1,0:T(8,128)(2,1)S(1)}, bf16[384,512]{1,0:T(8,128)(2,1)S(1)}, u32[]{:S(2)}, u32[]{:S(2)}) collective-permute-start(bf16[384,512]{1,0:T(8,128)(2,1)S(1)} %get-tuple-element.26), channel_id=1, source_target_pairs={{0,8},{8,16},{16,24},{1,9},{9,17},{17,25},{2,10},{10,18},{18,26},{... | collective-permute-start | bytes 1179656 | tf_op jit(solution)/shard_map/ppermute | solution.py:235
  165.9 18.1 %collective-permute-start.15 = (bf16[384,512]{1,0:T(8,128)(2,1)S(1)}, bf16[384,512]{1,0:T(8,128)(2,1)S(1)}, u32[]{:S(2)}, u32[]{:S(2)}) collective-permute-start(bf16[384,512]{1,0:T(8,128)(2,1)S(1)} %get-tuple-element.27), channel_id=1, source_target_pairs={{8,0},{16,8},{24,16},{9,1},{17,9},{25,17},{10,2},{18,10},{26,18},{... | collective-permute-start | bytes 1179656 | tf_op jit(solution)/shard_map/ppermute | solution.py:235
  167.5 23.7 %collective-permute-start.28 = (bf16[384,512]{1,0:T(8,128)(2,1)S(1)}, bf16[384,512]{1,0:T(8,128)(2,1)S(1)}, u32[]{:S(2)}, u32[]{:S(2)}) collective-permute-start(bf16[384,512]{1,0:T(8,128)(2,1)S(1)} %get-tuple-element.32), channel_id=1, source_target_pairs={{0,8},{8,16},{16,24},{1,9},{9,17},{17,25},{2,10},{10,18},{18,26},{... | collective-permute-start | bytes 1179656 | tf_op jit(solution)/shard_map/ppermute | solution.py:235
  174.3 16.9 %collective-permute-start.31 = (bf16[384,512]{1,0:T(8,128)(2,1)S(1)}, bf16[384,512]{1,0:T(8,128)(2,1)S(1)}, u32[]{:S(2)}, u32[]{:S(2)}) collective-permute-start(bf16[384,512]{1,0:T(8,128)(2,1)S(1)} %get-tuple-element.33), channel_id=1, source_target_pairs={{8,0},{16,8},{24,16},{9,1},{17,9},{25,17},{10,2},{18,10},{26,18},{... | collective-permute-start | bytes 1179656 | tf_op jit(solution)/shard_map/ppermute | solution.py:235
  175.9 23.2 %collective-permute-start.35 = (bf16[384,512]{1,0:T(8,128)(2,1)S(1)}, bf16[384,512]{1,0:T(8,128)(2,1)S(1)}, u32[]{:S(2)}, u32[]{:S(2)}) collective-permute-start(bf16[384,512]{1,0:T(8,128)(2,1)S(1)} %get-tuple-element.38), channel_id=1, source_target_pairs={{0,8},{8,16},{16,24},{1,9},{9,17},{17,25},{2,10},{10,18},{18,26},{... | collective-permute-start | bytes 1179656 | tf_op jit(solution)/shard_map/ppermute | solution.py:235
  182.8 16.4 %collective-permute-start.38 = (bf16[384,512]{1,0:T(8,128)(2,1)S(1)}, bf16[384,512]{1,0:T(8,128)(2,1)S(1)}, u32[]{:S(2)}, u32[]{:S(2)}) collective-permute-start(bf16[384,512]{1,0:T(8,128)(2,1)S(1)} %get-tuple-element.39), channel_id=1, source_target_pairs={{8,0},{16,8},{24,16},{9,1},{17,9},{25,17},{10,2},{18,10},{26,18},{... | collective-permute-start | bytes 1179656 | tf_op jit(solution)/shard_map/ppermute | solution.py:235
  191.2 9.7 %copy-start.1 = (bf16[3072,512]{1,0:T(8,128)(2,1)S(1)}, bf16[3072,512]{1,0:T(8,128)(2,1)}, u32[]{:S(2)}) copy-start(bf16[3072,512]{1,0:T(8,128)(2,1)} %param.8) | copy-start | bytes 9437188

commit v2 on v1

v2 whole, which is shorter than its diff:
```python
import math

import jax
import jax.numpy as jnp
from jax import lax
from jax.experimental import pallas as pl
from jax.experimental.pallas import tpu as pltpu
from jax.sharding import PartitionSpec as P

VMEM_LIMIT = 48 * 1024 * 1024


def dot_nn(left, right):
    return lax.dot_general(
        left, right, (((1,), (0,)), ((), ())), preferred_element_type=jnp.float32
    )


def dot_nt(left, right):
    return lax.dot_general(
        left, right, (((1,), (1,)), ((), ())), preferred_element_type=jnp.float32
    )


def dot_tn(left, right):
    return lax.dot_general(
        left, right, (((0,), (0,)), ((), ())), preferred_element_type=jnp.float32
    )


def halves(value):
    high = value.astype(jnp.bfloat16)
    low = (value - high.astype(jnp.float32)).astype(jnp.bfloat16)
    return high, low


def wide(dot, left, right):
    left_high, left_low = halves(left)
    right_high, right_low = halves(right)
    return dot(left_high, right_high) + (dot(left_high, right_low) + dot(left_low, right_high))


def feature(value):
    return jnp.where(value > 0, value + 1.0, jnp.exp(jnp.minimum(value, 0.0)))


def feature_slope(value):
    return jnp.where(value > 0, 1.0, jnp.exp(jnp.minimum(value, 0.0)))


def key_value_project_kernel(tokens_ref, w_key_ref, w_value_ref, out_ref, row_ref):
    tokens = tokens_ref[...]
    head_dim = w_key_ref.shape[1]
    key = dot_nn(tokens, w_key_ref[...]).astype(jnp.bfloat16)
    value = dot_nn(tokens, w_value_ref[...]).astype(jnp.bfloat16)
    out_ref[:, :head_dim] = key
    out_ref[:, head_dim:] = value
    row_ref[:, :head_dim] = jnp.sum(feature(key.astype(jnp.float32)), axis=0, keepdims=True)
    row_ref[:, head_dim:] = jnp.mean(value.astype(jnp.float32), axis=0, keepdims=True)


def query_project_kernel(tokens_ref, w_query_ref, cot_ref, out_ref):
    head_dim = w_query_ref.shape[1]
    out_ref[:, :head_dim] = dot_nn(tokens_ref[...], w_query_ref[...]).astype(jnp.bfloat16)
    out_ref[:, head_dim:] = cot_ref[...]


def write_kernel(pair_ref, row_ref, memory_ref):
    head_dim = pair_ref.shape[1] // 2
    phi_key = feature(pair_ref[:, :head_dim].astype(jnp.float32))
    centred = pair_ref[:, head_dim:].astype(jnp.float32) - row_ref[:, head_dim:]
    memory_ref[0] = wide(dot_tn, phi_key, centred)


def grad_memory_kernel(pair_ref, rows_ref, mix_ref, out_ref):
    head_dim = pair_ref.shape[1] // 2
    phi_query = feature(pair_ref[:, :head_dim].astype(jnp.float32))
    norm = jnp.sum(rows_ref[:, :head_dim], axis=0, keepdims=True)
    denominator = jnp.sum(phi_query * norm, axis=1, keepdims=True) + 1.0
    grad_num = mix_ref[...] * pair_ref[:, head_dim:].astype(jnp.float32) / denominator
    out_ref[0] = wide(dot_tn, phi_query, grad_num)


def attend_kernel(
    has_prev_ref,
    query_ref,
    pair_ref,
    prev_ref,
    mix_ref,
    out_ref,
    grad_query_ref,
    stats_ref,
):
    seg_len, head_dim = pair_ref.shape[0], pair_ref.shape[1] // 2
    scale = head_dim ** (-0.5)
    query, cot = query_ref[:, :head_dim], query_ref[:, head_dim:]
    key, key_prev = pair_ref[:, :head_dim], prev_ref[:, :head_dim]
    value, value_prev = pair_ref[:, head_dim:], prev_ref[:, head_dim:]
    rows = lax.broadcasted_iota(jnp.int32, (seg_len, seg_len), 0)
    cols = lax.broadcasted_iota(jnp.int32, (seg_len, seg_len), 1)
    score_own = jnp.where(cols <= rows, dot_nt(query, key) * scale, -1e30)
    score_prev = jnp.where(has_prev_ref[0] > 0, dot_nt(query, key_prev) * scale, -1e30)
    row_max = jnp.maximum(
        jnp.max(score_own, axis=1, keepdims=True), jnp.max(score_prev, axis=1, keepdims=True)
    )
    weight_own = jnp.exp(score_own - row_max)
    weight_prev = jnp.exp(score_prev - row_max)
    inverse = 1.0 / (
        jnp.sum(weight_own, axis=1, keepdims=True) + jnp.sum(weight_prev, axis=1, keepdims=True)
    )
    soft_own = weight_own * inverse
    soft_prev = weight_prev * inverse
    out_ref[...] = dot_nn(soft_own.astype(jnp.bfloat16), value) + dot_nn(
        soft_prev.astype(jnp.bfloat16), value_prev
    )
    grad_local = ((1.0 - mix_ref[...]) * cot.astype(jnp.float32)).astype(jnp.bfloat16)
    grad_own = dot_nt(grad_local, value)
    grad_prev = dot_nt(grad_local, value_prev)
    row_dot = jnp.sum(soft_own * grad_own, axis=1, keepdims=True) + jnp.sum(
        soft_prev * grad_prev, axis=1, keepdims=True
    )
    score_grad_own = (soft_own * (grad_own - row_dot) * scale).astype(jnp.bfloat16)
    score_grad_prev = (soft_prev * (grad_prev - row_dot) * scale).astype(jnp.bfloat16)
    grad_query_ref[...] = dot_nn(score_grad_own, key) + dot_nn(score_grad_prev, key_prev)
    lane = lax.broadcasted_iota(jnp.int32, (seg_len, 128), 1)
    stats = jnp.where(
        lane == 0, row_max, jnp.where(lane == 1, inverse, jnp.where(lane == 2, row_dot, 0.0))
    )
    stats_ref[...] = jnp.transpose(stats)[:8]


def retrieve_kernel(
    query_ref,
    memory_ref,
    rows_ref,
    mix_ref,
    local_ref,
    grad_att_ref,
    blended_ref,
    grad_query_ref,
    grad_norm_ref,
):
    head_dim = query_ref.shape[1] // 2
    query = query_ref[:, :head_dim].astype(jnp.float32)
    phi_query = feature(query)
    norms = rows_ref[:, :head_dim]
    norm = jnp.sum(norms, axis=0, keepdims=True)
    memory = memory_ref[0].astype(jnp.float32) + wide(dot_tn, norms, rows_ref[:, head_dim:])
    mix = mix_ref[...]
    denominator = jnp.sum(phi_query * norm, axis=1, keepdims=True) + 1.0
    retrieved = wide(dot_nn, phi_query, memory) / denominator
    blended = mix * retrieved + (1.0 - mix) * local_ref[...]
    blended_ref[...] = blended.astype(jnp.bfloat16)
    grad_ret = mix * query_ref[:, head_dim:].astype(jnp.float32)
    grad_num = grad_ret / denominator
    grad_den = -jnp.sum(grad_ret * retrieved, axis=1, keepdims=True) / denominator
    grad_phi = wide(dot_nt, grad_num, memory) + grad_den * norm
    grad_norm_ref[...] = jnp.sum(grad_den * phi_query, axis=0, keepdims=True)
    grad_query = grad_att_ref[...] + grad_phi * feature_slope(query)
    grad_query_ref[...] = grad_query.astype(jnp.bfloat16)


def key_value_kernel(
    pair_ref,
    query_ref,
    stats_ref,
    query_next_ref,
    stats_next_ref,
    grad_memory_ref,
    mix_ref,
    grad_key_ref,
    grad_value_ref,
):
    seg_len, head_dim = pair_ref.shape[0], pair_ref.shape[1] // 2
    key, value = pair_ref[:, :head_dim], pair_ref[:, head_dim:]
    scale = head_dim ** (-0.5)
    keep = 1.0 - mix_ref[...]

    def part(query, cot, stats, causal):
        grad_local = (keep * cot.astype(jnp.float32)).astype(jnp.bfloat16)
        score = dot_nt(key, query) * scale
        if causal:
            rows = lax.broadcasted_iota(jnp.int32, score.shape, 0)
            cols = lax.broadcasted_iota(jnp.int32, score.shape, 1)
            score = jnp.where(rows <= cols, score, -1e30)
        soft = jnp.exp(score - stats[0:1]) * stats[1:2]
        grad_value = dot_nn(soft.astype(jnp.bfloat16), grad_local)
        grad_soft = dot_nt(value, grad_local)
        score_grad = (soft * (grad_soft - stats[2:3]) * scale).astype(jnp.bfloat16)
        return dot_nn(score_grad, query), grad_value

    def both(ref, stats, causal):
        return part(ref[:, :head_dim], ref[:, head_dim:], stats, causal)

    own_key, own_value = both(query_ref, stats_ref[...], True)
    next_key, next_value = both(query_next_ref, stats_next_ref[...], False)
    key_float = key.astype(jnp.float32)
    grad_memory = grad_memory_ref[0]
    phi_high, phi_low = halves(feature(key_float))
    from_memory = dot_nt(value, grad_memory)
    grad_key_ref[...] = own_key + next_key + from_memory * feature_slope(key_float)
    to_value = dot_nn(phi_high, grad_memory) + dot_nn(phi_low, grad_memory)
    grad_value_ref[...] = (own_value + next_value + to_value).astype(jnp.bfloat16)


def call(kernel, sizes, ins, outs):
    heads, seg_len, head_dim, model_dim, count = sizes
    blocks = {
        "t": (seg_len, model_dim),
        "w": (model_dim, head_dim),
        "c": (seg_len, head_dim),
        "p": (seg_len, 2 * head_dim),
        "r": (1, head_dim),
        "o": (1, 2 * head_dim),
        "R": (count, 2 * head_dim),
        "m": (1, head_dim, head_dim),
        "s": (8, seg_len),
    }

    def spec(kind):
        if kind == "f":
            return pl.BlockSpec(memory_space=pltpu.SMEM)
        if kind == "t":
            return pl.BlockSpec(blocks[kind], lambda h: (0, 0))
        if kind == "m":
            return pl.BlockSpec(blocks[kind], lambda h: (h, 0, 0))
        if kind == "s":
            return pl.BlockSpec(blocks[kind], lambda h: (h, 0))
        return pl.BlockSpec(blocks[kind], lambda h: (0, h))

    def shape(kind):
        block = blocks[kind]
        if kind in "ms":
            return (heads * block[0],) + block[1:]
        return (block[0], heads * block[1])

    return pl.pallas_call(
        kernel,
        grid=(heads,),
        in_specs=[spec(kind) for kind in ins],
        out_specs=[spec(kind) for kind, _ in outs],
        out_shape=[jax.ShapeDtypeStruct(shape(kind), dtype) for kind, dtype in outs],
        compiler_params=pltpu.CompilerParams(vmem_limit_bytes=VMEM_LIMIT),
        cost_estimate=pl.CostEstimate(flops=1000, bytes_accessed=1000, transcendentals=0),
    )


def local(inputs, w_query, w_key, w_value, gate_bias, cotangent):
    tokens = inputs[0]
    cot = cotangent[0]
    seg_len, model_dim = tokens.shape
    heads = gate_bias.shape[0]
    columns = w_query.shape[1]
    head_dim = columns // heads
    seq_count, seq_at = lax.axis_size("seq"), lax.axis_index("seq")
    dp_count, dp_at = lax.axis_size("dp"), lax.axis_index("dp")
    part_rows = model_dim // (seq_count * dp_count)
    f32, bf16 = jnp.float32, jnp.bfloat16

    def shifted(x, by, first=0, last=None):
        last = seq_count - 1 if last is None else last
        pairs = [
            (i, i + by) for i in range(first, last + 1) if 0 <= i + by < seq_count
        ]
        return lax.ppermute(x, "seq", pairs)

    def chain(own, by):
        total = jnp.zeros(own.shape, bf16)
        for hop in range(seq_count - 1):
            at = hop if by > 0 else seq_count - 1 - hop
            total = total + shifted((total + own).astype(bf16), by, at, at)
        return total

    def rows_before(own, by):
        window, step, known = own, 1, []
        while step < seq_count:
            arrived = shifted(window, by * step)
            known.append(arrived)
            window = jnp.concatenate([window, arrived], 0)
            step *= 2
        missing = -sum(part.shape[0] for part in known) % 8
        known.append(jnp.zeros((missing,) + own.shape[1:], own.dtype))
        return jnp.concatenate(known, 0)

    count = 1
    while count < seq_count:
        count *= 2
    count = -(-(count - 1) // 8) * 8
    sizes = (heads, seg_len, head_dim, model_dim, count)
    mix = jnp.repeat(jax.nn.sigmoid(gate_bias), head_dim)[None]
    has_prev = jnp.reshape((seq_at > 0).astype(jnp.int32), (1,))

    def rows_for(core):
        return jnp.concatenate(
            [
                lax.dynamic_slice_in_dim(tokens, (block * dp_count + core) * part_rows, part_rows, 1)
                for block in range(seq_count)
            ],
            1,
        )

    def from_core(x, step):
        return lax.ppermute(x, "dp", [(i, (i + step) % dp_count) for i in range(dp_count)])

    pair, row = call(key_value_project_kernel, sizes, "tww", (("p", bf16), ("o", f32)))(
        tokens, w_key, w_value
    )
    pair_prev = shifted(pair, 1)
    rows = rows_before(row, 1)
    (query,) = call(query_project_kernel, sizes, "twc", (("p", bf16),))(tokens, w_query, cot)
    query_next = shifted(query, -1)
    (memory_own,) = call(write_kernel, sizes, "po", (("m", f32),))(pair, row)
    memory = chain(memory_own, 1)
    (grad_memory_own,) = call(grad_memory_kernel, sizes, "pRr", (("m", f32),))(query, rows, mix)
    grad_memory = chain(grad_memory_own, -1)

    token_parts = [rows_for(dp_at)] + [
        from_core(rows_for((dp_at + step) % dp_count), step) for step in range(1, dp_count)
    ]

    local_out, grad_att, stats = call(
        attend_kernel, sizes, "fpppr", (("c", f32), ("c", f32), ("s", f32))
    )(has_prev, query, pair, pair_prev, mix)
    stats_next = shifted(stats, -1)
    blended, grad_query, grad_norm_own = call(
        retrieve_kernel, sizes, "pmRrcc", (("c", bf16), ("c", bf16), ("r", f32))
    )(query, memory, rows, mix, local_out, grad_att)
    grad_norm = jnp.sum(rows_before(grad_norm_own, -1), 0, keepdims=True)
    grad_key_rest, grad_value = call(
        key_value_kernel, sizes, "ppspsmr", (("c", f32), ("c", bf16))
    )(pair, query, stats, query_next, stats_next, grad_memory, mix)
    key = jnp.concatenate(
        [pair[:, 2 * h * head_dim : (2 * h + 1) * head_dim] for h in range(heads)], 1
    )
    grad_key = (grad_key_rest + grad_norm * feature_slope(key.astype(f32))).astype(bf16)

    contract = (((0,), (0,)), ((), ()))
    grad_scale = 1.0 / math.sqrt(seq_count * dp_count * seg_len)

    def weight_term(grad):
        grads = [grad] + [from_core(grad, step) for step in range(1, dp_count)]
        total = None
        for rows, term in zip(token_parts, grads):
            product = lax.dot_general(rows, term, contract, preferred_element_type=f32)
            total = product if total is None else total + product
        terms = total.reshape(seq_count, part_rows, columns)

        def block(index):
            return lax.dynamic_index_in_dim(terms, jnp.clip(index, 0, seq_count - 1), 0, False)

        ups = jnp.zeros((part_rows, columns), bf16)
        downs = ups
        for turn in range(1, seq_count):
            ahead = seq_count - turn
            ups = shifted(
                (ups.astype(f32) + block(seq_at + ahead)).astype(bf16), 1, 0, turn - 1
            )
            downs = shifted(
                (downs.astype(f32) + block(seq_at - ahead)).astype(bf16), -1, ahead
            )
        return (ups.astype(f32) + downs.astype(f32) + block(seq_at)) * grad_scale

    pieces = [weight_term(grad) for grad in (grad_query, grad_value, grad_key)]
    return (blended[None], jnp.stack([pieces[0], pieces[2], pieces[1]], 1))


def solution(mesh):
    return jax.shard_map(
        local,
        mesh=mesh,
        in_specs=(
            P("dp", "seq", None),
            P(None, "head"),
            P(None, "head"),
            P(None, "head"),
            P("head"),
            P("dp", "seq", "head"),
        ),
        out_specs=(P("dp", "seq", "head"), P(("seq", "dp"), None, "head")),
        check_vma=False,
    )
```

time: 202 us -> 175 us (0.87)
  waiting for transfers between devices: 69.2 us -> 55.4 us
  Pallas kernels: 11.9 us -> 24 us
  starting transfers between devices: 77.8 us -> 67.8 us
  local copies, waits for them, and re-layouts: 11.7 us -> 4.52 us
  matrix products: 16.1 us -> 9.9 us
  other arithmetic: 12.8 us -> 10.7 us
    ppermute x35 -> x31, waiting for transfers between devices: 69.2 us -> 55.3 us  [shifted(): return lax.ppermute(x, 'seq', pairs)]
    pallas_call x5 -> x7, Pallas kernels: 11.9 us -> 24 us  [the longest x1 5.72 us: local(): call(key_value_project_kernel, sizes, 'tww', (('p', bf16), ('o', f32)))]
    ppermute x35 -> x31, starting transfers between devices: 77.1 us -> 67.2 us  [shifted(): return lax.ppermute(x, 'seq', pairs)]
    add x8 -> x2, other arithmetic: 8.64 us -> 1.08 us  [chain(): total = total + shifted((total + own).astype(bf16), by, at, at)]
    dot_general x3 -> x0, matrix products: 6.43 us -> none  [project(): return jnp.dot(tokens, weight, preferred_element_type=f32).astype(bf16)]
    unnamed x33 -> x26, local copies, waits for them, and re-layouts: 8 us -> 1.78 us
    convert_element_type x0 -> x6, other arithmetic: none -> 4.21 us  [chain(): total = total + shifted((total + own).astype(bf16), by, at, at)]
    dynamic_slice x1, local copies, waits for them, and re-layouts: 3.37 us -> 1.29 us  [rows_for(): lax.dynamic_slice_in_dim(tokens, (block * dp_count + core) * part_rows, p...]
  transfers between devices with their start and end apart: 39 -> 35, of which waited for: 13 -> 12; matrix products, arithmetic and copies ran while one was open for 15% -> 12% of each run, Pallas kernels for 5% -> 11%
where the time goes in v2:
time: 175 us; the launch traced here: 174 us
  starting transfers between devices  67.8 us (39%)
  waiting for transfers between devices  55.4 us (32%)
  Pallas kernels  24 us (14%)
  other arithmetic  10.7 us (6%)
  matrix products  9.9 us (6%)
  local copies, waits for them, and re-layouts  4.52 us (3%)
    ppermute x31, starting transfers between devices, shifted(): return lax.ppermute(x, 'seq', pairs)  67.2 us
    ppermute x31, waiting for transfers between devices, shifted(): return lax.ppermute(x, 'seq', pairs)  55.3 us
    dot_general x6, matrix products, weight_term(): product = lax.dot_general(rows, term, contract, preferred_element_type=f32)  9.9 us
    pallas_call x1, Pallas kernels, local(): call(key_value_project_kernel, sizes, 'tww', (('p', bf16), ('o', f32)))  5.72 us
    pallas_call x1, Pallas kernels, local(): call(attend_kernel, sizes, 'fpppr', (('c', f32), ('c', f32), ('s', f32)))  4.76 us
    pallas_call x1, Pallas kernels, local(): call(key_value_kernel, sizes, 'ppspsmr', (('c', f32), ('c', bf16)))  4.5 us
    convert_element_type x6, other arithmetic, chain(): total = total + shifted((total + own).astype(bf16), by, at, at)  4.21 us
  transfers between devices with their start and end apart: 35, of which 12 were waited for; matrix products, arithmetic and copies ran while one was open for 12% of the time, Pallas kernels for 11%

profile of v2, /device:TPU:0, one launch (start us, length us, event | category | flops | bytes accessed | tf_op | source)
XLA Modules:
  0.0 173.7 jit_solution(8740915242823689346)
XLA Ops:
  0.6 1.7 copy-done
  2.3 5.7 %shard_map.78 = (bf16[384,1024]{1,0:T(8,128)(2,1)}, f32[1,1024]{1,0:T(1,128)S(1)}) custom-call(bf16[384,3072]{1,0:T(8,128)(2,1)S(1)} %bitcast.122, bf16[3072,512]{1,0:T(8,128)(2,1)} %w_key_ref.1, bf16[3072,512]{1,0:T(8,128)(2,1)} %w_value_ref.1), custom_call_target="tpu_custom_call" | custom-call | flops 1000 | bytes 1000 | tf_op jit(solution)/shard_map/pallas_call | solution.py:305
  8.0 4.9 %collective-permute-start.3 = (f32[1,1024]{1,0:T(1,128)S(1)}, f32[1,1024]{1,0:T(1,128)S(1)}, u32[]{:S(2)}, u32[]{:S(2)}) collective-permute-start(f32[1,1024]{1,0:T(1,128)S(1)} %get-tuple-element.13.row_ref), channel_id=1, source_target_pairs={{0,8},{8,16},{16,24},{1,9},{9,17},{17,25},{2,10},{10,18},{18,26},{... | collective-permute-start | bytes 12296 | tf_op jit(solution)/shard_map/ppermute | solution.py:265
  12.9 4.4 %collective-permute-start.5 = (bf16[384,1024]{1,0:T(8,128)(2,1)}, bf16[384,1024]{1,0:T(8,128)(2,1)}, u32[]{:S(2)}, u32[]{:S(2)}) collective-permute-start(bf16[384,1024]{1,0:T(8,128)(2,1)} %get-tuple-element.12.pair_ref), channel_id=1, source_target_pairs={{0,8},{8,16},{16,24},{1,9},{9,17},{17,25},{2,10},{10,18},{18,26},{... | collective-permute-start | bytes 2359304 | tf_op jit(solution)/shard_map/ppermute | solution.py:265
  17.3 2.1 %shard_map.79 = f32[2,256,256]{2,1,0:T(8,128)S(1)} custom-call(bf16[384,1024]{1,0:T(8,128)(2,1)} %get-tuple-element.12.pair_ref, f32[1,1024]{1,0:T(1,128)S(1)} %get-tuple-element.13.row_ref), custom_call_target="tpu_custom_call" | custom-call | flops 1000 | bytes 1000 | tf_op jit(solution)/shard_map/pallas_call | solution.py:312
  19.4 0.8 convert_element_type.173
  20.2 2.6 %collective-permute-start = (bf16[2,256,256]{2,1,0:T(8,128)(2,1)}, bf16[2,256,256]{2,1,0:T(8,128)(2,1)S(1)}, u32[]{:S(2)}, u32[]{:S(2)}) collective-permute-start(bf16[2,256,256]{2,1,0:T(8,128)(2,1)} %convert_element_type.173), channel_id=1, source_target_pairs={{0,8},{1,9},{2,10},{3,11},{4,12},{5,13},{6,14},{7,15}} | collective-permute-start | bytes 786440 | tf_op jit(solution)/shard_map/ppermute | solution.py:265
  22.8 1.3 dynamic-slice_bitcast_fusion.7
  24.1 1.1 pad_maximum_fusion.2
  25.3 1.3 collective-permute-start.4
  26.6 12.4 %collective-permute-done = bf16[2,256,256]{2,1,0:T(8,128)(2,1)S(1)} collective-permute-done((bf16[2,256,256]{2,1,0:T(8,128)(2,1)}, bf16[2,256,256]{2,1,0:T(8,128)(2,1)S(1)}, u32[]{:S(2)}, u32[]{:S(2)}) %collective-permute-start) | collective-permute-done | bytes 262176 | tf_op jit(solution)/shard_map/ppermute | solution.py:265
  39.0 0.7 collective-permute-start.1
  39.8 3.0 %shard_map.77.query_ref.pair_ref = bf16[384,1024]{1,0:T(8,128)(2,1)S(1)} custom-call(bf16[384,3072]{1,0:T(8,128)(2,1)S(1)} %bitcast.123, bf16[3072,512]{1,0:T(8,128)(2,1)} %w_query_ref.1, bf16[384,512]{1,0:T(8,128)(2,1)S(1)} %bitcast.124), custom_call_target="tpu_custom_call" | custom-call | flops 1000 | bytes 1000 | tf_op jit(solution)/shard_map/pallas_call | solution.py:310
  43.0 1.2 shard_map.82
  44.2 0.7 collective-permute-start.16
  45.0 0.8 add_convert_fusion.2
  46.4 0.8 add_convert_fusion.1
  47.2 1.4 collective-permute-start.17
  48.6 1.3 collective-permute-start.14
  50.0 4.8 %shard_map.80 = (f32[384,512]{1,0:T(8,128)S(1)}, f32[384,512]{1,0:T(8,128)S(1)}, f32[16,384]{1,0:T(8,128)S(1)}) custom-call(s32[1]{0:T(128)} %bitcast.2.has_prev_ref, bf16[384,1024]{1,0:T(8,128)(2,1)S(1)} %shard_map.77.query_ref.pair_ref, bf16[384,1024]{1,0:T(8,128)(2,1)} %get-tuple-element.12.pair_ref, bf16[384,1024]{1,0:T(8,128)(2,1)} %collective-permute-done.5.prev_ref, ...), custom_call_target="tpu_custom_call" | custom-call | flops 1000 | bytes 1000 | tf_op jit(solution)/shard_map/pallas_call | solution.py:321
  54.8 2.7 %shard_map.81 = (bf16[384,512]{1,0:T(8,128)(2,1)}, bf16[384,512]{1,0:T(8,128)(2,1)S(1)}, f32[1,512]{1,0:T(1,128)S(1)}) custom-call(bf16[384,1024]{1,0:T(8,128)(2,1)S(1)} %shard_map.77.query_ref.pair_ref, bf16[2,256,256]{2,1,0:T(8,128)(2,1)S(1)} %add.194.memory_ref, f32[8,1024]{1,0:T(8,128)S(1)} %maximum_maximum_fusion.rows_ref, f32[1,512]{1,0:T(1,128)S(1)} %bitcast.127, ...), custom_call_target="tpu_custom_call" | custom-call | flops 1000 | bytes 1000 | tf_op jit(solution)/shard_map/pallas_call | solution.py:325
  57.5 1.3 collective-permute-start.19
  58.8 1.8 %add_convert_fusion = (bf16[2,256,256]{2,1,0:T(8,128)(2,1)}, bf16[2,256,256]{2,1,0:T(8,128)(2,1)S(1)}) fusion(f32[2,256,256]{2,1,0:T(8,128)S(1)} %shard_map.82, bf16[2,256,256]{2,1,0:T(8,128)(2,1)S(1)} %copy-done.10, bf16[2,256,256]{2,1,0:T(8,128)(2,1)} %collective-permute-done.17), kind=kLoop, calls=%fused_computation.52 | loop fusion | flops 524288 | bytes 1572864 | tf_op jit(solution)/shard_map/convert_element_type | solution.py:271
  60.5 1.3 collective-permute-start.18
  61.8 10.1 %collective-permute-done.19 = f32[1,512]{1,0:T(1,128)S(1)} collective-permute-done((f32[1,512]{1,0:T(1,128)S(1)}, f32[1,512]{1,0:T(1,128)S(1)}, u32[]{:S(2)}, u32[]{:S(2)}) %collective-permute-start.19) | collective-permute-done | bytes 2080 | tf_op jit(solution)/shard_map/ppermute | solution.py:265
  71.9 1.3 collective-permute-start.20
  73.2 1.3 collective-permute-start.15
  74.5 3.8 %collective-permute-done.20 = f32[2,512]{1,0:T(2,128)S(1)} collective-permute-done((f32[2,512]{1,0:T(2,128)S(1)}, f32[2,512]{1,0:T(2,128)S(1)}, u32[]{:S(2)}, u32[]{:S(2)}) %collective-permute-start.20) | collective-permute-done | bytes 4128 | tf_op jit(solution)/shard_map/ppermute | solution.py:265
  78.4 1.1 fusion.29
  79.5 1.0 add.225.grad_memory_ref
  81.1 4.5 %shard_map.83 = (f32[384,512]{1,0:T(8,128)S(1)}, bf16[384,512]{1,0:T(8,128)(2,1)S(1)}) custom-call(bf16[384,1024]{1,0:T(8,128)(2,1)} %get-tuple-element.12.pair_ref, bf16[384,1024]{1,0:T(8,128)(2,1)S(1)} %shard_map.77.query_ref.pair_ref, f32[16,384]{1,0:T(8,128)S(1)} %get-tuple-element.18.stats_ref, ...), custom_call_target="tpu_custom_call" | custom-call | flops 1000 | bytes 1000 | tf_op jit(solution)/shard_map/pallas_call | solution.py:329
  86.5 2.3 %fusion.30 = f32[1536,512]{1,0:T(8,128)S(1)} fusion(bf16[384,1536]{1,0:T(8,128)(2,1)} %collective-permute-done.6, bf16[384,512]{1,0:T(8,128)(2,1)S(1)} %collective-permute-done.7), kind=kOutput, calls=%fused_computation.76 | convolution fusion | flops 603979776 | bytes 4718592 | tf_op jit(solution)/shard_map/dot_general | solution.py:344
  88.8 1.0 convolution_add_fusion.2
  89.9 5.6 %collective-permute-start.8 = (bf16[384,512]{1,0:T(8,128)(2,1)S(1)}, bf16[384,512]{1,0:T(8,128)(2,1)S(1)}, u32[]{:S(2)}, u32[]{:S(2)}) collective-permute-start(bf16[384,512]{1,0:T(8,128)(2,1)S(1)} %get-tuple-element.30), channel_id=1, source_target_pairs={{0,8},{1,9},{2,10},{3,11},{4,12},{5,13},{6,14},{7,15}} | collective-permute-start | bytes 1179656 | tf_op jit(solution)/shard_map/ppermute | solution.py:265
  95.6 0.9 collective-permute-start.11
  96.5 2.3 %fusion.32 = f32[1536,512]{1,0:T(8,128)S(1)} fusion(bf16[384,1536]{1,0:T(8,128)(2,1)} %collective-permute-done.6, bf16[384,512]{1,0:T(8,128)(2,1)S(1)} %collective-permute-done.28), kind=kOutput, calls=%fused_computation.78 | convolution fusion | flops 603979776 | bytes 4718592 | tf_op jit(solution)/shard_map/dot_general | solution.py:344
  98.7 1.0 convolution_add_fusion
  99.9 1.3 collective-permute-start.29
  101.2 0.7 collective-permute-start.32
  101.9 2.3 %fusion.31 = f32[1536,512]{1,0:T(8,128)S(1)} fusion(bf16[384,1536]{1,0:T(8,128)(2,1)} %collective-permute-done.6, bf16[384,512]{1,0:T(8,128)(2,1)S(1)} %collective-permute-done.21), kind=kOutput, calls=%fused_computation.77 | convolution fusion | flops 603979776 | bytes 4718592 | tf_op jit(solution)/shard_map/dot_general | solution.py:344
  104.2 1.0 convolution_add_fusion.1
  105.3 1.3 collective-permute-start.22
  106.7 0.7 collective-permute-start.25
  107.7 2.7 %collective-permute-start.9 = (bf16[384,512]{1,0:T(8,128)(2,1)S(1)}, bf16[384,512]{1,0:T(8,128)(2,1)S(1)}, u32[]{:S(2)}, u32[]{:S(2)}) collective-permute-start(bf16[384,512]{1,0:T(8,128)(2,1)S(1)} %get-tuple-element.28), channel_id=1, source_target_pairs={{0,8},{8,16},{1,9},{9,17},{2,10},{10,18},{3,11},{11,19},{4,12},{12... | collective-permute-start | bytes 1179656 | tf_op jit(solution)/shard_map/ppermute | solution.py:265
  110.4 3.0 %collective-permute-done.29 = bf16[384,512]{1,0:T(8,128)(2,1)S(1)} collective-permute-done((bf16[384,512]{1,0:T(8,128)(2,1)S(1)}, bf16[384,512]{1,0:T(8,128)(2,1)S(1)}, u32[]{:S(2)}, u32[]{:S(2)}) %collective-permute-start.29) | collective-permute-done | bytes 393248 | tf_op jit(solution)/shard_map/ppermute | solution.py:265
  113.4 0.7 collective-permute-start.12
  114.4 5.0 %collective-permute-start.30 = (bf16[384,512]{1,0:T(8,128)(2,1)S(1)}, bf16[384,512]{1,0:T(8,128)(2,1)S(1)}, u32[]{:S(2)}, u32[]{:S(2)}) collective-permute-start(bf16[384,512]{1,0:T(8,128)(2,1)S(1)} %get-tuple-element.40), channel_id=1, source_target_pairs={{0,8},{8,16},{1,9},{9,17},{2,10},{10,18},{3,11},{11,19},{4,12},{12... | collective-permute-start | bytes 1179656 | tf_op jit(solution)/shard_map/ppermute | solution.py:265
  119.5 2.4 %collective-permute-done.22 = bf16[384,512]{1,0:T(8,128)(2,1)S(1)} collective-permute-done((bf16[384,512]{1,0:T(8,128)(2,1)S(1)}, bf16[384,512]{1,0:T(8,128)(2,1)S(1)}, u32[]{:S(2)}, u32[]{:S(2)}) %collective-permute-start.22) | collective-permute-done | bytes 393248 | tf_op jit(solution)/shard_map/ppermute | solution.py:265
  121.8 0.7 collective-permute-start.33
  122.9 5.0 %collective-permute-start.23 = (bf16[384,512]{1,0:T(8,128)(2,1)S(1)}, bf16[384,512]{1,0:T(8,128)(2,1)S(1)}, u32[]{:S(2)}, u32[]{:S(2)}) collective-permute-start(bf16[384,512]{1,0:T(8,128)(2,1)S(1)} %get-tuple-element.34), channel_id=1, source_target_pairs={{0,8},{8,16},{1,9},{9,17},{2,10},{10,18},{3,11},{11,19},{4,12},{12... | collective-permute-start | bytes 1179656 | tf_op jit(solution)/shard_map/ppermute | solution.py:265
  127.9 2.4 %collective-permute-done.9 = bf16[384,512]{1,0:T(8,128)(2,1)S(1)} collective-permute-done((bf16[384,512]{1,0:T(8,128)(2,1)S(1)}, bf16[384,512]{1,0:T(8,128)(2,1)S(1)}, u32[]{:S(2)}, u32[]{:S(2)}) %collective-permute-start.9) | collective-permute-done | bytes 393248 | tf_op jit(solution)/shard_map/ppermute | solution.py:265
  130.3 0.7 collective-permute-start.26
  131.3 5.0 %collective-permute-start.10 = (bf16[384,512]{1,0:T(8,128)(2,1)S(1)}, bf16[384,512]{1,0:T(8,128)(2,1)S(1)}, u32[]{:S(2)}, u32[]{:S(2)}) collective-permute-start(bf16[384,512]{1,0:T(8,128)(2,1)S(1)} %get-tuple-element.26), channel_id=1, source_target_pairs={{0,8},{8,16},{16,24},{1,9},{9,17},{17,25},{2,10},{10,18},{18,26},{... | collective-permute-start | bytes 1179656 | tf_op jit(solution)/shard_map/ppermute | solution.py:265
  136.3 2.4 %collective-permute-done.30 = bf16[384,512]{1,0:T(8,128)(2,1)S(1)} collective-permute-done((bf16[384,512]{1,0:T(8,128)(2,1)S(1)}, bf16[384,512]{1,0:T(8,128)(2,1)S(1)}, u32[]{:S(2)}, u32[]{:S(2)}) %collective-permute-start.30) | collective-permute-done | bytes 393248 | tf_op jit(solution)/shard_map/ppermute | solution.py:265
  138.7 1.3 collective-permute-start.13
  140.3 5.0 %collective-permute-start.31 = (bf16[384,512]{1,0:T(8,128)(2,1)S(1)}, bf16[384,512]{1,0:T(8,128)(2,1)S(1)}, u32[]{:S(2)}, u32[]{:S(2)}) collective-permute-start(bf16[384,512]{1,0:T(8,128)(2,1)S(1)} %get-tuple-element.38), channel_id=1, source_target_pairs={{0,8},{8,16},{16,24},{1,9},{9,17},{17,25},{2,10},{10,18},{18,26},{... | collective-permute-start | bytes 1179656 | tf_op jit(solution)/shard_map/ppermute | solution.py:265
  145.3 1.8 %collective-permute-done.23 = bf16[384,512]{1,0:T(8,128)(2,1)S(1)} collective-permute-done((bf16[384,512]{1,0:T(8,128)(2,1)S(1)}, bf16[384,512]{1,0:T(8,128)(2,1)S(1)}, u32[]{:S(2)}, u32[]{:S(2)}) %collective-permute-start.23) | collective-permute-done | bytes 393248 | tf_op jit(solution)/shard_map/ppermute | solution.py:265
  147.1 1.3 collective-permute-start.34
  148.7 5.0 %collective-permute-start.24 = (bf16[384,512]{1,0:T(8,128)(2,1)S(1)}, bf16[384,512]{1,0:T(8,128)(2,1)S(1)}, u32[]{:S(2)}, u32[]{:S(2)}) collective-permute-start(bf16[384,512]{1,0:T(8,128)(2,1)S(1)} %get-tuple-element.32), channel_id=1, source_target_pairs={{0,8},{8,16},{16,24},{1,9},{9,17},{17,25},{2,10},{10,18},{18,26},{... | collective-permute-start | bytes 1179656 | tf_op jit(solution)/shard_map/ppermute | solution.py:265
  153.8 1.8 %collective-permute-done.10 = bf16[384,512]{1,0:T(8,128)(2,1)S(1)} collective-permute-done((bf16[384,512]{1,0:T(8,128)(2,1)S(1)}, bf16[384,512]{1,0:T(8,128)(2,1)S(1)}, u32[]{:S(2)}, u32[]{:S(2)}) %collective-permute-start.10) | collective-permute-done | bytes 393248 | tf_op jit(solution)/shard_map/ppermute | solution.py:265
  155.5 1.3 collective-permute-start.27
  157.0 7.0 %collective-permute-done.31 = bf16[384,512]{1,0:T(8,128)(2,1)S(1)} collective-permute-done((bf16[384,512]{1,0:T(8,128)(2,1)S(1)}, bf16[384,512]{1,0:T(8,128)(2,1)S(1)}, u32[]{:S(2)}, u32[]{:S(2)}) %collective-permute-start.31) | collective-permute-done | bytes 393248 | tf_op jit(solution)/shard_map/ppermute | solution.py:265
  164.1 7.7 %collective-permute-done.24 = bf16[384,512]{1,0:T(8,128)(2,1)S(1)} collective-permute-done((bf16[384,512]{1,0:T(8,128)(2,1)S(1)}, bf16[384,512]{1,0:T(8,128)(2,1)S(1)}, u32[]{:S(2)}, u32[]{:S(2)}) %collective-permute-start.24) | collective-permute-done | bytes 393248 | tf_op jit(solution)/shard_map/ppermute | solution.py:265
  172.1 1.6 pad_maximum_fusion
  (78 shorter events, 5.2 us)
Async XLA Ops:
  0.6 1.7 copy-start
  2.3 20.5 %copy-start.1 = (bf16[1,384,3072]{2,1,0:T(8,128)(2,1)S(1)}, bf16[1,384,3072]{2,1,0:T(8,128)(2,1)}, u32[]{:S(2)}) copy-start(bf16[1,384,3072]{2,1,0:T(8,128)(2,1)} %param.6) | copy-start | bytes 7077892
  8.0 17.2 %collective-permute-start.3 = (f32[1,1024]{1,0:T(1,128)S(1)}, f32[1,1024]{1,0:T(1,128)S(1)}, u32[]{:S(2)}, u32[]{:S(2)}) collective-permute-start(f32[1,1024]{1,0:T(1,128)S(1)} %get-tuple-element.13.row_ref), channel_id=1, source_target_pairs={{0,8},{8,16},{16,24},{1,9},{9,17},{17,25},{2,10},{10,18},{18,26},{... | collective-permute-start | bytes 12296 | tf_op jit(solution)/shard_map/ppermute | solution.py:265
  12.9 37.0 %collective-permute-start.5 = (bf16[384,1024]{1,0:T(8,128)(2,1)}, bf16[384,1024]{1,0:T(8,128)(2,1)}, u32[]{:S(2)}, u32[]{:S(2)}) collective-permute-start(bf16[384,1024]{1,0:T(8,128)(2,1)} %get-tuple-element.12.pair_ref), channel_id=1, source_target_pairs={{0,8},{8,16},{16,24},{1,9},{9,17},{17,25},{2,10},{10,18},{18,26},{... | collective-permute-start | bytes 2359304 | tf_op jit(solution)/shard_map/ppermute | solution.py:265
  19.4 19.6 %copy-start.2 = (f32[2,256,256]{2,1,0:T(8,128)}, f32[2,256,256]{2,1,0:T(8,128)S(1)}, u32[]{:S(2)}) copy-start(f32[2,256,256]{2,1,0:T(8,128)S(1)} %shard_map.79) | copy-start | bytes 1572868
  20.2 18.8 %collective-permute-start = (bf16[2,256,256]{2,1,0:T(8,128)(2,1)}, bf16[2,256,256]{2,1,0:T(8,128)(2,1)S(1)}, u32[]{:S(2)}, u32[]{:S(2)}) collective-permute-start(bf16[2,256,256]{2,1,0:T(8,128)(2,1)} %convert_element_type.173), channel_id=1, source_target_pairs={{0,8},{1,9},{2,10},{3,11},{4,12},{5,13},{6,14},{7,15}} | collective-permute-start | bytes 786440 | tf_op jit(solution)/shard_map/ppermute | solution.py:265
  24.1 1.1 copy-start.11
  24.1 15.7 %copy-start.4 = (bf16[1,384,512]{2,1,0:T(8,128)(2,1)S(1)}, bf16[1,384,512]{2,1,0:T(8,128)(2,1)}, u32[]{:S(2)}) copy-start(bf16[1,384,512]{2,1,0:T(8,128)(2,1)} %param.11) | copy-start | bytes 1179652
  25.2 61.2 %collective-permute-start.6 = (bf16[384,1536]{1,0:T(8,128)(2,1)}, bf16[384,1536]{1,0:T(8,128)(2,1)}, u32[]{:S(2)}, u32[]{:S(2)}) collective-permute-start(bf16[384,1536]{1,0:T(8,128)(2,1)} %pad_maximum_fusion.2), channel_id=1, source_target_pairs={{0,4},{4,0},{1,5},{5,1},{2,6},{6,2},{3,7},{7,3},{8,12},{12,8},{9,1... | collective-permute-start | bytes 3538952 | tf_op jit(solution)/shard_map/ppermute | solution.py:303
  25.3 17.7 %collective-permute-start.4 = (f32[2,1024]{1,0:T(2,128)S(1)}, f32[2,1024]{1,0:T(2,128)S(1)}, u32[]{:S(2)}, u32[]{:S(2)}) collective-permute-start(f32[2,1024]{1,0:T(2,128)S(1)} %pad_maximum_fusion.3), channel_id=1, source_target_pairs={{0,16},{8,24},{1,17},{9,25},{2,18},{10,26},{3,19},{11,27},{4,20},{... | collective-permute-start | bytes 24584 | tf_op jit(solution)/shard_map/ppermute | solution.py:265
  39.0 5.9 %collective-permute-start.1 = (bf16[2,256,256]{2,1,0:T(8,128)(2,1)S(1)}, bf16[2,256,256]{2,1,0:T(8,128)(2,1)S(1)}, u32[]{:S(2)}, u32[]{:S(2)}) collective-permute-start(bf16[2,256,256]{2,1,0:T(8,128)(2,1)S(1)} %add_convert_fusion.3), channel_id=1, source_target_pairs={{8,16},{9,17},{10,18},{11,19},{12,20},{13,21},{14,22},{15,23}} | collective-permute-start | bytes 786440 | tf_op jit(solution)/shard_map/ppermute | solution.py:265
  42.8 2.1 %copy-start.3 = (f32[2,256,256]{2,1,0:T(8,128)S(1)}, f32[2,256,256]{2,1,0:T(8,128)}, u32[]{:S(2)}) copy-start(f32[2,256,256]{2,1,0:T(8,128)} %copy-done.2) | copy-start | bytes 1572868
  44.2 2.2 %collective-permute-start.16 = (bf16[2,256,256]{2,1,0:T(8,128)(2,1)S(1)}, bf16[2,256,256]{2,1,0:T(8,128)(2,1)S(1)}, u32[]{:S(2)}, u32[]{:S(2)}) collective-permute-start(bf16[2,256,256]{2,1,0:T(8,128)(2,1)S(1)} %convert_element_type.192), channel_id=1, source_target_pairs={{24,16},{25,17},{26,18},{27,19},{28,20},{29,21},{30,22},{31,23}} | collective-permute-start | bytes 786440 | tf_op jit(solution)/shard_map/ppermute | solution.py:265
  45.8 4.1 %collective-permute-start.2 = (bf16[2,256,256]{2,1,0:T(8,128)(2,1)}, bf16[2,256,256]{2,1,0:T(8,128)(2,1)S(1)}, u32[]{:S(2)}, u32[]{:S(2)}) collective-permute-start(bf16[2,256,256]{2,1,0:T(8,128)(2,1)} %get-tuple-element.24), channel_id=1, source_target_pairs={{16,24},{17,25},{18,26},{19,27},{20,28},{21,29},{22,30},{23,31}} | collective-permute-start | bytes 786440 | tf_op jit(solution)/shard_map/ppermute | solution.py:265
  46.4 3.6 %copy-start.9 = (bf16[2,256,256]{2,1,0:T(8,128)(2,1)}, bf16[2,256,256]{2,1,0:T(8,128)(2,1)S(1)}, u32[]{:S(2)}) copy-start(bf16[2,256,256]{2,1,0:T(8,128)(2,1)S(1)} %collective-permute-done.16) | copy-start | bytes 786436
  47.2 11.5 %collective-permute-start.17 = (bf16[2,256,256]{2,1,0:T(8,128)(2,1)}, bf16[2,256,256]{2,1,0:T(8,128)(2,1)}, u32[]{:S(2)}, u32[]{:S(2)}) collective-permute-start(bf16[2,256,256]{2,1,0:T(8,128)(2,1)} %add_convert_fusion.1), channel_id=1, source_target_pairs={{16,8},{17,9},{18,10},{19,11},{20,12},{21,13},{22,14},{23,15}} | collective-permute-start | bytes 786440 | tf_op jit(solution)/shard_map/ppermute | solution.py:265
  48.6 31.9 %collective-permute-start.14 = (bf16[384,1024]{1,0:T(8,128)(2,1)S(1)}, bf16[384,1024]{1,0:T(8,128)(2,1)S(1)}, u32[]{:S(2)}, u32[]{:S(2)}) collective-permute-start(bf16[384,1024]{1,0:T(8,128)(2,1)S(1)} %shard_map.77.query_ref.pair_ref), channel_id=1, source_target_pairs={{8,0},{16,8},{24,16},{9,1},{17,9},{25,17},{10,2},{18,10},{26,18},{... | collective-permute-start | bytes 2359304 | tf_op jit(solution)/shard_map/ppermute | solution.py:265
  50.0 8.8 %copy-start.10 = (bf16[2,256,256]{2,1,0:T(8,128)(2,1)S(1)}, bf16[2,256,256]{2,1,0:T(8,128)(2,1)}, u32[]{:S(2)}) copy-start(bf16[2,256,256]{2,1,0:T(8,128)(2,1)} %copy-done.9) | copy-start | bytes 786436
  57.5 14.5 %collective-permute-start.19 = (f32[1,512]{1,0:T(1,128)S(1)}, f32[1,512]{1,0:T(1,128)S(1)}, u32[]{:S(2)}, u32[]{:S(2)}) collective-permute-start(f32[1,512]{1,0:T(1,128)S(1)} %get-tuple-element.20), channel_id=1, source_target_pairs={{8,0},{16,8},{24,16},{9,1},{17,9},{25,17},{10,2},{18,10},{26,18},{... | collective-permute-start | bytes 6152 | tf_op jit(solution)/shard_map/ppermute | solution.py:265
  60.5 19.0 %collective-permute-start.18 = (bf16[2,256,256]{2,1,0:T(8,128)(2,1)}, bf16[2,256,256]{2,1,0:T(8,128)(2,1)}, u32[]{:S(2)}, u32[]{:S(2)}) collective-permute-start(bf16[2,256,256]{2,1,0:T(8,128)(2,1)} %get-tuple-element.22), channel_id=1, source_target_pairs={{8,0},{9,1},{10,2},{11,3},{12,4},{13,5},{14,6},{15,7}} | collective-permute-start | bytes 786440 | tf_op jit(solution)/shard_map/ppermute | solution.py:265
  71.9 6.4 %collective-permute-start.20 = (f32[2,512]{1,0:T(2,128)S(1)}, f32[2,512]{1,0:T(2,128)S(1)}, u32[]{:S(2)}, u32[]{:S(2)}) collective-permute-start(f32[2,512]{1,0:T(2,128)S(1)} %pad_maximum_fusion.4), channel_id=1, source_target_pairs={{16,0},{24,8},{17,1},{25,9},{18,2},{26,10},{19,3},{27,11},{20,4},{... | collective-permute-start | bytes 12296 | tf_op jit(solution)/shard_map/ppermute | solution.py:265
  73.2 7.8 %collective-permute-start.15 = (f32[16,384]{1,0:T(8,128)S(1)}, f32[16,384]{1,0:T(8,128)S(1)}, u32[]{:S(2)}, u32[]{:S(2)}) collective-permute-start(f32[16,384]{1,0:T(8,128)S(1)} %get-tuple-element.18.stats_ref), channel_id=1, source_target_pairs={{8,0},{16,8},{24,16},{9,1},{17,9},{25,17},{10,2},{18,10},{26,18},{... | collective-permute-start | bytes 73736 | tf_op jit(solution)/shard_map/ppermute | solution.py:265
  78.4 8.1 %collective-permute-start.7 = (bf16[384,512]{1,0:T(8,128)(2,1)S(1)}, bf16[384,512]{1,0:T(8,128)(2,1)S(1)}, u32[]{:S(2)}, u32[]{:S(2)}) collective-permute-start(bf16[384,512]{1,0:T(8,128)(2,1)S(1)} %get-tuple-element.17), channel_id=1, source_target_pairs={{0,4},{4,0},{1,5},{5,1},{2,6},{6,2},{3,7},{7,3},{8,12},{12,8},{9,1... | collective-permute-start | bytes 1179656 | tf_op jit(solution)/shard_map/ppermute | solution.py:303
  85.8 16.1 %collective-permute-start.21 = (bf16[384,512]{1,0:T(8,128)(2,1)S(1)}, bf16[384,512]{1,0:T(8,128)(2,1)S(1)}, u32[]{:S(2)}, u32[]{:S(2)}) collective-permute-start(bf16[384,512]{1,0:T(8,128)(2,1)S(1)} %fusion.4), channel_id=1, source_target_pairs={{0,4},{4,0},{1,5},{5,1},{2,6},{6,2},{3,7},{7,3},{8,12},{12,8},{9,1... | collective-permute-start | bytes 1179656 | tf_op jit(solution)/shard_map/ppermute | solution.py:303
  85.9 2.9 %copy-start.5 = (bf16[384,384]{1,0:T(8,128)(2,1)S(1)}, bf16[384,384]{1,0:T(8,128)(2,1)}, u32[]{:S(2)}) copy-start(bf16[384,384]{1,0:T(8,128)(2,1)} %get-tuple-element.44) | copy-start | bytes 884740
  85.9 2.9 %copy-start.6 = (bf16[384,384]{1,0:T(8,128)(2,1)S(1)}, bf16[384,384]{1,0:T(8,128)(2,1)}, u32[]{:S(2)}) copy-start(bf16[384,384]{1,0:T(8,128)(2,1)} %get-tuple-element.47) | copy-start | bytes 884740
  85.9 2.9 %copy-start.7 = (bf16[384,384]{1,0:T(8,128)(2,1)S(1)}, bf16[384,384]{1,0:T(8,128)(2,1)}, u32[]{:S(2)}) copy-start(bf16[384,384]{1,0:T(8,128)(2,1)} %get-tuple-element.48) | copy-start | bytes 884740
  85.9 2.9 %copy-start.8 = (bf16[384,384]{1,0:T(8,128)(2,1)S(1)}, bf16[384,384]{1,0:T(8,128)(2,1)}, u32[]{:S(2)}) copy-start(bf16[384,384]{1,0:T(8,128)(2,1)} %get-tuple-element.49) | copy-start | bytes 884740
  85.9 10.5 %collective-permute-start.28 = (bf16[384,512]{1,0:T(8,128)(2,1)S(1)}, bf16[384,512]{1,0:T(8,128)(2,1)S(1)}, u32[]{:S(2)}, u32[]{:S(2)}) collective-permute-start(bf16[384,512]{1,0:T(8,128)(2,1)S(1)} %get-tuple-element.21), channel_id=1, source_target_pairs={{0,4},{4,0},{1,5},{5,1},{2,6},{6,2},{3,7},{7,3},{8,12},{12,8},{9,1... | collective-permute-start | bytes 1179656 | tf_op jit(solution)/shard_map/ppermute | solution.py:303
  89.9 16.7 %collective-permute-start.8 = (bf16[384,512]{1,0:T(8,128)(2,1)S(1)}, bf16[384,512]{1,0:T(8,128)(2,1)S(1)}, u32[]{:S(2)}, u32[]{:S(2)}) collective-permute-start(bf16[384,512]{1,0:T(8,128)(2,1)S(1)} %get-tuple-element.30), channel_id=1, source_target_pairs={{0,8},{1,9},{2,10},{3,11},{4,12},{5,13},{6,14},{7,15}} | collective-permute-start | bytes 1179656 | tf_op jit(solution)/shard_map/ppermute | solution.py:265
  95.6 11.8 %collective-permute-start.11 = (bf16[384,512]{1,0:T(8,128)(2,1)S(1)}, bf16[384,512]{1,0:T(8,128)(2,1)S(1)}, u32[]{:S(2)}, u32[]{:S(2)}) collective-permute-start(bf16[384,512]{1,0:T(8,128)(2,1)S(1)} %get-tuple-element.31), channel_id=1, source_target_pairs={{24,16},{25,17},{26,18},{27,19},{28,20},{29,21},{30,22},{31,23}} | collective-permute-start | bytes 1179656 | tf_op jit(solution)/shard_map/ppermute | solution.py:265
  99.9 13.5 %collective-permute-start.29 = (bf16[384,512]{1,0:T(8,128)(2,1)S(1)}, bf16[384,512]{1,0:T(8,128)(2,1)S(1)}, u32[]{:S(2)}, u32[]{:S(2)}) collective-permute-start(bf16[384,512]{1,0:T(8,128)(2,1)S(1)} %get-tuple-element.42), channel_id=1, source_target_pairs={{0,8},{1,9},{2,10},{3,11},{4,12},{5,13},{6,14},{7,15}} | collective-permute-start | bytes 1179656 | tf_op jit(solution)/shard_map/ppermute | solution.py:265
  101.2 12.9 %collective-permute-start.32 = (bf16[384,512]{1,0:T(8,128)(2,1)S(1)}, bf16[384,512]{1,0:T(8,128)(2,1)S(1)}, u32[]{:S(2)}, u32[]{:S(2)}) collective-permute-start(bf16[384,512]{1,0:T(8,128)(2,1)S(1)} %get-tuple-element.43), channel_id=1, source_target_pairs={{24,16},{25,17},{26,18},{27,19},{28,20},{29,21},{30,22},{31,23}} | collective-permute-start | bytes 1179656 | tf_op jit(solution)/shard_map/ppermute | solution.py:265
  105.3 16.5 %collective-permute-start.22 = (bf16[384,512]{1,0:T(8,128)(2,1)S(1)}, bf16[384,512]{1,0:T(8,128)(2,1)S(1)}, u32[]{:S(2)}, u32[]{:S(2)}) collective-permute-start(bf16[384,512]{1,0:T(8,128)(2,1)S(1)} %get-tuple-element.36), channel_id=1, source_target_pairs={{0,8},{1,9},{2,10},{3,11},{4,12},{5,13},{6,14},{7,15}} | collective-permute-start | bytes 1179656 | tf_op jit(solution)/shard_map/ppermute | solution.py:265
  106.7 15.8 %collective-permute-start.25 = (bf16[384,512]{1,0:T(8,128)(2,1)S(1)}, bf16[384,512]{1,0:T(8,128)(2,1)S(1)}, u32[]{:S(2)}, u32[]{:S(2)}) collective-permute-start(bf16[384,512]{1,0:T(8,128)(2,1)S(1)} %get-tuple-element.37), channel_id=1, source_target_pairs={{24,16},{25,17},{26,18},{27,19},{28,20},{29,21},{30,22},{31,23}} | collective-permute-start | bytes 1179656 | tf_op jit(solution)/shard_map/ppermute | solution.py:265
  107.7 22.6 %collective-permute-start.9 = (bf16[384,512]{1,0:T(8,128)(2,1)S(1)}, bf16[384,512]{1,0:T(8,128)(2,1)S(1)}, u32[]{:S(2)}, u32[]{:S(2)}) collective-permute-start(bf16[384,512]{1,0:T(8,128)(2,1)S(1)} %get-tuple-element.28), channel_id=1, source_target_pairs={{0,8},{8,16},{1,9},{9,17},{2,10},{10,18},{3,11},{11,19},{4,12},{12... | collective-permute-start | bytes 1179656 | tf_op jit(solution)/shard_map/ppermute | solution.py:265
  113.4 17.5 %collective-permute-start.12 = (bf16[384,512]{1,0:T(8,128)(2,1)S(1)}, bf16[384,512]{1,0:T(8,128)(2,1)S(1)}, u32[]{:S(2)}, u32[]{:S(2)}) collective-permute-start(bf16[384,512]{1,0:T(8,128)(2,1)S(1)} %get-tuple-element.29), channel_id=1, source_target_pairs={{16,8},{24,16},{17,9},{25,17},{18,10},{26,18},{19,11},{27,19},{20,... | collective-permute-start | bytes 1179656 | tf_op jit(solution)/shard_map/ppermute | solution.py:265
  114.4 24.3 %collective-permute-start.30 = (bf16[384,512]{1,0:T(8,128)(2,1)S(1)}, bf16[384,512]{1,0:T(8,128)(2,1)S(1)}, u32[]{:S(2)}, u32[]{:S(2)}) collective-permute-start(bf16[384,512]{1,0:T(8,128)(2,1)S(1)} %get-tuple-element.40), channel_id=1, source_target_pairs={{0,8},{8,16},{1,9},{9,17},{2,10},{10,18},{3,11},{11,19},{4,12},{12... | collective-permute-start | bytes 1179656 | tf_op jit(solution)/shard_map/ppermute | solution.py:265
  121.8 18.1 %collective-permute-start.33 = (bf16[384,512]{1,0:T(8,128)(2,1)S(1)}, bf16[384,512]{1,0:T(8,128)(2,1)S(1)}, u32[]{:S(2)}, u32[]{:S(2)}) collective-permute-start(bf16[384,512]{1,0:T(8,128)(2,1)S(1)} %get-tuple-element.41), channel_id=1, source_target_pairs={{16,8},{24,16},{17,9},{25,17},{18,10},{26,18},{19,11},{27,19},{20,... | collective-permute-start | bytes 1179656 | tf_op jit(solution)/shard_map/ppermute | solution.py:265
  122.9 24.3 %collective-permute-start.23 = (bf16[384,512]{1,0:T(8,128)(2,1)S(1)}, bf16[384,512]{1,0:T(8,128)(2,1)S(1)}, u32[]{:S(2)}, u32[]{:S(2)}) collective-permute-start(bf16[384,512]{1,0:T(8,128)(2,1)S(1)} %get-tuple-element.34), channel_id=1, source_target_pairs={{0,8},{8,16},{1,9},{9,17},{2,10},{10,18},{3,11},{11,19},{4,12},{12... | collective-permute-start | bytes 1179656 | tf_op jit(solution)/shard_map/ppermute | solution.py:265
  130.3 18.1 %collective-permute-start.26 = (bf16[384,512]{1,0:T(8,128)(2,1)S(1)}, bf16[384,512]{1,0:T(8,128)(2,1)S(1)}, u32[]{:S(2)}, u32[]{:S(2)}) collective-permute-start(bf16[384,512]{1,0:T(8,128)(2,1)S(1)} %get-tuple-element.35), channel_id=1, source_target_pairs={{16,8},{24,16},{17,9},{25,17},{18,10},{26,18},{19,11},{27,19},{20,... | collective-permute-start | bytes 1179656 | tf_op jit(solution)/shard_map/ppermute | solution.py:265
  131.3 24.3 %collective-permute-start.10 = (bf16[384,512]{1,0:T(8,128)(2,1)S(1)}, bf16[384,512]{1,0:T(8,128)(2,1)S(1)}, u32[]{:S(2)}, u32[]{:S(2)}) collective-permute-start(bf16[384,512]{1,0:T(8,128)(2,1)S(1)} %get-tuple-element.26), channel_id=1, source_target_pairs={{0,8},{8,16},{16,24},{1,9},{9,17},{17,25},{2,10},{10,18},{18,26},{... | collective-permute-start | bytes 1179656 | tf_op jit(solution)/shard_map/ppermute | solution.py:265
  138.7 18.1 %collective-permute-start.13 = (bf16[384,512]{1,0:T(8,128)(2,1)S(1)}, bf16[384,512]{1,0:T(8,128)(2,1)S(1)}, u32[]{:S(2)}, u32[]{:S(2)}) collective-permute-start(bf16[384,512]{1,0:T(8,128)(2,1)S(1)} %get-tuple-element.27), channel_id=1, source_target_pairs={{8,0},{16,8},{24,16},{9,1},{17,9},{25,17},{10,2},{18,10},{26,18},{... | collective-permute-start | bytes 1179656 | tf_op jit(solution)/shard_map/ppermute | solution.py:265
  140.3 23.7 %collective-permute-start.31 = (bf16[384,512]{1,0:T(8,128)(2,1)S(1)}, bf16[384,512]{1,0:T(8,128)(2,1)S(1)}, u32[]{:S(2)}, u32[]{:S(2)}) collective-permute-start(bf16[384,512]{1,0:T(8,128)(2,1)S(1)} %get-tuple-element.38), channel_id=1, source_target_pairs={{0,8},{8,16},{16,24},{1,9},{9,17},{17,25},{2,10},{10,18},{18,26},{... | collective-permute-start | bytes 1179656 | tf_op jit(solution)/shard_map/ppermute | solution.py:265
  147.1 16.9 %collective-permute-start.34 = (bf16[384,512]{1,0:T(8,128)(2,1)S(1)}, bf16[384,512]{1,0:T(8,128)(2,1)S(1)}, u32[]{:S(2)}, u32[]{:S(2)}) collective-permute-start(bf16[384,512]{1,0:T(8,128)(2,1)S(1)} %get-tuple-element.39), channel_id=1, source_target_pairs={{8,0},{16,8},{24,16},{9,1},{17,9},{25,17},{10,2},{18,10},{26,18},{... | collective-permute-start | bytes 1179656 | tf_op jit(solution)/shard_map/ppermute | solution.py:265
  148.7 23.1 %collective-permute-start.24 = (bf16[384,512]{1,0:T(8,128)(2,1)S(1)}, bf16[384,512]{1,0:T(8,128)(2,1)S(1)}, u32[]{:S(2)}, u32[]{:S(2)}) collective-permute-start(bf16[384,512]{1,0:T(8,128)(2,1)S(1)} %get-tuple-element.32), channel_id=1, source_target_pairs={{0,8},{8,16},{16,24},{1,9},{9,17},{17,25},{2,10},{10,18},{18,26},{... | collective-permute-start | bytes 1179656 | tf_op jit(solution)/shard_map/ppermute | solution.py:265
  155.5 16.3 %collective-permute-start.27 = (bf16[384,512]{1,0:T(8,128)(2,1)S(1)}, bf16[384,512]{1,0:T(8,128)(2,1)S(1)}, u32[]{:S(2)}, u32[]{:S(2)}) collective-permute-start(bf16[384,512]{1,0:T(8,128)(2,1)S(1)} %get-tuple-element.33), channel_id=1, source_target_pairs={{8,0},{16,8},{24,16},{9,1},{17,9},{25,17},{10,2},{18,10},{26,18},{... | collective-permute-start | bytes 1179656 | tf_op jit(solution)/shard_map/ppermute | solution.py:265

commit v3 on v2

v3 whole, which is shorter than its diff:
```python
import functools
import math

import jax
import jax.numpy as jnp
from jax import lax
from jax.experimental import pallas as pl
from jax.experimental.pallas import tpu as pltpu
from jax.sharding import PartitionSpec as P

VMEM_LIMIT = 48 * 1024 * 1024
SEQ, EVEN, CORE, PLACE = range(4)


def dot_nn(left, right):
    return lax.dot_general(
        left, right, (((1,), (0,)), ((), ())), preferred_element_type=jnp.float32
    )


def dot_nt(left, right):
    return lax.dot_general(
        left, right, (((1,), (1,)), ((), ())), preferred_element_type=jnp.float32
    )


def dot_tn(left, right):
    return lax.dot_general(
        left, right, (((0,), (0,)), ((), ())), preferred_element_type=jnp.float32
    )


def halves(value):
    high = value.astype(jnp.bfloat16)
    low = (value - high.astype(jnp.float32)).astype(jnp.bfloat16)
    return high, low


def wide(dot, left, right):
    left_high, left_low = halves(left)
    right_high, right_low = halves(right)
    return dot(left_high, right_high) + (dot(left_high, right_low) + dot(left_low, right_high))


def feature(value):
    return jnp.where(value > 0, value + 1.0, jnp.exp(jnp.minimum(value, 0.0)))


def feature_slope(value):
    return jnp.where(value > 0, 1.0, jnp.exp(jnp.minimum(value, 0.0)))


def copies_of(tokens_ref, tokens, weight_refs, weights, sems):
    pieces, depth = weights.shape[1:3]

    def token_copy(piece):
        at = pl.ds(piece * depth, depth)
        return pltpu.make_async_copy(tokens_ref.at[:, at], tokens.at[:, at], sems.at[piece])

    def weight_copy(which, piece):
        return pltpu.make_async_copy(
            weight_refs[which].at[pl.ds(piece * depth, depth)],
            weights.at[which, piece],
            sems.at[(which + 1) * pieces + piece],
        )

    for piece in range(pieces):
        token_copy(piece).start()
        weight_copy(0, piece).start()
    for which in range(1, len(weight_refs)):
        for piece in range(pieces):
            weight_copy(which, piece).start()

    def product(which):
        total = None
        for piece in range(pieces):
            if which == 0:
                token_copy(piece).wait()
            weight_copy(which, piece).wait()
            at = slice(piece * depth, (piece + 1) * depth)
            term = dot_nn(tokens[:, at], weights[which, piece])
            total = term if total is None else total + term
        return total.astype(jnp.bfloat16)

    return product


def project_kernel(
    heads,
    info_ref,
    tokens_ref,
    w_key_ref,
    w_value_ref,
    w_query_ref,
    cot_ref,
    pair_ref,
    query_ref,
    even_ref,
    odd_ref,
    row_ref,
    tokens,
    weights,
    cot,
    sems,
):
    product = copies_of(
        tokens_ref, tokens, (w_key_ref, w_value_ref, w_query_ref), weights, sems
    )
    cot_copy = pltpu.make_async_copy(cot_ref, cot, sems.at[sems.shape[0] - 1])
    cot_copy.start()
    head_dim = pair_ref.shape[1] // (2 * heads)
    even = info_ref[EVEN] > 0

    def put(ref, up, at, value):
        ref[:, at] = value

        @pl.when(even == up)
        def _():
            even_ref[:, at] = value

        @pl.when(even != up)
        def _():
            odd_ref[:, at] = value

    for which in range(2):
        result = product(which)
        for head in range(heads):
            part = result[:, head * head_dim : (head + 1) * head_dim]
            at = slice((2 * head + which) * head_dim, (2 * head + which + 1) * head_dim)
            put(pair_ref, True, at, part)
            wide_part = part.astype(jnp.float32)
            if which == 0:
                row_ref[:, at] = jnp.sum(feature(wide_part), axis=0, keepdims=True)
            else:
                row_ref[:, at] = jnp.mean(wide_part, axis=0, keepdims=True)
    query = product(2)
    cot_copy.wait()
    for head in range(heads):
        of_head = slice(head * head_dim, (head + 1) * head_dim)
        at = slice(2 * head * head_dim, (2 * head + 1) * head_dim)
        put(query_ref, False, at, query[:, of_head])
        at = slice((2 * head + 1) * head_dim, (2 * head + 2) * head_dim)
        put(query_ref, False, at, cot[:, of_head])


def lower_end(info_ref, route):
    distance, parity = route
    return lax.rem(lax.div(info_ref[SEQ], distance), 2) == parity


def total_from(info_ref, refs, routes, from_above):
    total = refs[0][0].astype(jnp.float32)
    for ref, route in zip(refs[1:], routes):
        wanted = lower_end(info_ref, route) == from_above
        total = total + jnp.where(wanted, ref[0].astype(jnp.float32), 0.0)
    return total


def neighbour_kernel(routes, info_ref, even_ref, odd_ref, far_ref, row_ref, mix_ref, *refs):
    prev_ref, next_ref, memory_ref, grad_memory_ref, row_prev_ref = refs[:5]
    even = info_ref[EVEN] > 0
    pair = jnp.where(even, odd_ref[...], even_ref[...])
    query = jnp.where(even, even_ref[...], odd_ref[...])
    prev_ref[...] = pair
    next_ref[...] = query
    head_dim = pair.shape[1] // 2
    phi_key = feature(pair[:, :head_dim].astype(jnp.float32))
    value = pair[:, head_dim:].astype(jnp.float32)
    mean = jnp.mean(value, axis=0, keepdims=True)
    centred = (value - mean).astype(jnp.bfloat16)
    memory = dot_tn(phi_key.astype(jnp.bfloat16), centred).astype(jnp.bfloat16)
    norm = jnp.sum(phi_key, axis=0, keepdims=True)
    norm = jnp.where(info_ref[SEQ] > 0, norm, 0.0)
    memory_ref[0] = memory
    row_prev_ref[:, :head_dim] = norm
    row_prev_ref[:, head_dim:] = mean

    phi_query = feature(query[:, :head_dim].astype(jnp.float32))
    norm = norm + jnp.sum(far_ref[:, :head_dim], axis=0, keepdims=True) + row_ref[:, :head_dim]
    denominator = jnp.sum(phi_query * norm, axis=1, keepdims=True) + 1.0
    grad_num = mix_ref[...] * query[:, head_dim:].astype(jnp.float32) / denominator
    grad_memory = dot_tn(phi_query.astype(jnp.bfloat16), grad_num.astype(jnp.bfloat16))
    grad_memory = grad_memory.astype(jnp.bfloat16)
    grad_memory_ref[0] = grad_memory
    for ref, route in zip(refs[5:], routes):
        ref[0] = jnp.where(lower_end(info_ref, route), memory, grad_memory)


def attend_kernel(
    info_ref,
    query_ref,
    pair_ref,
    prev_ref,
    mix_ref,
    out_ref,
    grad_query_ref,
    stats_ref,
):
    seg_len, head_dim = pair_ref.shape[0], pair_ref.shape[1] // 2
    scale = head_dim ** (-0.5)
    query, cot = query_ref[:, :head_dim], query_ref[:, head_dim:]
    key, key_prev = pair_ref[:, :head_dim], prev_ref[:, :head_dim]
    value, value_prev = pair_ref[:, head_dim:], prev_ref[:, head_dim:]
    rows = lax.broadcasted_iota(jnp.int32, (seg_len, seg_len), 0)
    cols = lax.broadcasted_iota(jnp.int32, (seg_len, seg_len), 1)
    score_own = jnp.where(cols <= rows, dot_nt(query, key) * scale, -1e30)
    score_prev = jnp.where(info_ref[SEQ] > 0, dot_nt(query, key_prev) * scale, -1e30)
    row_max = jnp.maximum(
        jnp.max(score_own, axis=1, keepdims=True), jnp.max(score_prev, axis=1, keepdims=True)
    )
    weight_own = jnp.exp(score_own - row_max)
    weight_prev = jnp.exp(score_prev - row_max)
    inverse = 1.0 / (
        jnp.sum(weight_own, axis=1, keepdims=True) + jnp.sum(weight_prev, axis=1, keepdims=True)
    )
    soft_own = weight_own * inverse
    soft_prev = weight_prev * inverse
    out_ref[...] = dot_nn(soft_own.astype(jnp.bfloat16), value) + dot_nn(
        soft_prev.astype(jnp.bfloat16), value_prev
    )
    grad_local = ((1.0 - mix_ref[...]) * cot.astype(jnp.float32)).astype(jnp.bfloat16)
    grad_own = dot_nt(grad_local, value)
    grad_prev = dot_nt(grad_local, value_prev)
    row_dot = jnp.sum(soft_own * grad_own, axis=1, keepdims=True) + jnp.sum(
        soft_prev * grad_prev, axis=1, keepdims=True
    )
    score_grad_own = (soft_own * (grad_own - row_dot) * scale).astype(jnp.bfloat16)
    score_grad_prev = (soft_prev * (grad_prev - row_dot) * scale).astype(jnp.bfloat16)
    grad_query_ref[...] = dot_nn(score_grad_own, key) + dot_nn(score_grad_prev, key_prev)
    lane = lax.broadcasted_iota(jnp.int32, (seg_len, 128), 1)
    stats = jnp.where(
        lane == 0, row_max, jnp.where(lane == 1, inverse, jnp.where(lane == 2, row_dot, 0.0))
    )
    stats_ref[...] = jnp.transpose(stats)[:8]


def retrieve_kernel(
    routes, info_ref, query_ref, row_prev_ref, far_ref, mix_ref, local_ref, grad_att_ref, stats_ref, *refs
):
    blended_ref, grad_query_ref, note_ref = refs[-3:]
    head_dim = query_ref.shape[1] // 2
    query = query_ref[:, :head_dim].astype(jnp.float32)
    phi_query = feature(query)
    free = lax.broadcasted_iota(jnp.int32, far_ref.shape, 0) == 0
    rows = jnp.where(free, row_prev_ref[...], far_ref[...])
    norms = rows[:, :head_dim]
    norm = jnp.sum(norms, axis=0, keepdims=True)
    memory = total_from(info_ref, refs[:-3], routes, False) + wide(dot_tn, norms, rows[:, head_dim:])
    mix = mix_ref[...]
    denominator = jnp.sum(phi_query * norm, axis=1, keepdims=True) + 1.0
    retrieved = wide(dot_nn, phi_query, memory) / denominator
    blended = mix * retrieved + (1.0 - mix) * local_ref[...]
    blended_ref[...] = blended.astype(jnp.bfloat16)
    grad_ret = mix * query_ref[:, head_dim:].astype(jnp.float32)
    grad_num = grad_ret / denominator
    grad_den = -jnp.sum(grad_ret * retrieved, axis=1, keepdims=True) / denominator
    grad_phi = wide(dot_nt, grad_num, memory) + grad_den * norm
    seg_len = query.shape[0]
    note_ref[:8] = stats_ref[...]
    grad_norm = jnp.sum(grad_den * phi_query, axis=0, keepdims=True)
    if seg_len > head_dim:
        filler = jnp.zeros((1, seg_len - head_dim), jnp.float32)
        grad_norm = jnp.concatenate([grad_norm, filler], 1)
    note_ref[8:] = jnp.broadcast_to(grad_norm, (8, grad_norm.shape[1]))
    grad_query = grad_att_ref[...] + grad_phi * feature_slope(query)
    grad_query_ref[...] = grad_query.astype(jnp.bfloat16)


def key_value_kernel(
    routes, notes, info_ref, pair_ref, query_ref, note_ref, query_next_ref, mix_ref, *refs
):
    note_refs, grad_key_ref, grad_value_ref = refs[:notes], refs[-2], refs[-1]
    note_next_ref = note_refs[0]
    seg_len, head_dim = pair_ref.shape[0], pair_ref.shape[1] // 2
    key, value = pair_ref[:, :head_dim], pair_ref[:, head_dim:]
    scale = head_dim ** (-0.5)
    keep = 1.0 - mix_ref[...]

    def part(query, cot, stats, causal):
        grad_local = (keep * cot.astype(jnp.float32)).astype(jnp.bfloat16)
        score = dot_nt(key, query) * scale
        if causal:
            rows = lax.broadcasted_iota(jnp.int32, score.shape, 0)
            cols = lax.broadcasted_iota(jnp.int32, score.shape, 1)
            score = jnp.where(rows <= cols, score, -1e30)
        soft = jnp.exp(score - stats[0:1]) * stats[1:2]
        grad_value = dot_nn(soft.astype(jnp.bfloat16), grad_local)
        grad_soft = dot_nt(value, grad_local)
        score_grad = (soft * (grad_soft - stats[2:3]) * scale).astype(jnp.bfloat16)
        return dot_nn(score_grad, query), grad_value

    def both(ref, stats, causal):
        return part(ref[:, :head_dim], ref[:, head_dim:], stats, causal)

    own_key, own_value = both(query_ref, note_ref[:8], True)
    next_key, next_value = both(query_next_ref, note_next_ref[:8], False)
    key_float = key.astype(jnp.float32)
    grad_memory = total_from(info_ref, refs[notes:-2], routes, True).astype(jnp.bfloat16)
    phi_high, phi_low = halves(feature(key_float))
    from_memory = dot_nt(value, grad_memory)
    norm = note_next_ref[8:9, :head_dim]
    for ref in note_refs[1:]:
        norm = norm + ref[8:9, :head_dim]
    from_memory = (from_memory + norm) * feature_slope(key_float)
    grad_key_ref[...] = (own_key + next_key + from_memory).astype(jnp.bfloat16)
    to_value = dot_nn(phi_high, grad_memory) + dot_nn(phi_low, grad_memory)
    grad_value_ref[...] = (own_value + next_value + to_value).astype(jnp.bfloat16)


def pack_kernel(seq_count, dp_count, info_ref, *refs):
    for tokens_ref, out_ref in zip(refs[:dp_count], refs[dp_count:]):
        part_rows = out_ref.shape[0] // seq_count
        own_rows = dp_count * part_rows
        for block in range(seq_count):
            at = pl.multiple_of(info_ref[CORE] * part_rows + block * own_rows, 128)
            out_ref[block * part_rows : (block + 1) * part_rows] = jnp.transpose(
                tokens_ref[:, pl.ds(at, part_rows)]
            )


def row_blocks_kernel(info_ref, *refs):
    *refs, out_ref, first_ref = refs
    count = len(refs) // 2
    total = dot_nn(refs[0][...], refs[count][...])
    for rows, grad in zip(refs[1:count], refs[count + 1 :]):
        total = total + dot_nn(rows[...], grad[...])
    total = total.astype(jnp.bfloat16)
    out_ref[0] = total
    block = pl.program_id(0)
    last = pl.num_programs(0) - 1
    place = jnp.where(info_ref[SEQ] == 0, last - block, block)

    @pl.when(place < 2)
    def _():
        first_ref[place] = total


def inner_kernel(arrived_ref, far_ref, near_ref, far_out_ref, near_out_ref):
    for at, (ref, out_ref) in enumerate(((far_ref, far_out_ref), (near_ref, near_out_ref))):
        total = arrived_ref[at].astype(jnp.float32) + ref[0].astype(jnp.float32)
        out_ref[...] = total.astype(jnp.bfloat16)


def outer_kernel(info_ref, arrived_ref, terms_ref, out_ref):
    term = terms_ref[0].astype(jnp.float32)
    total = term + arrived_ref[...].astype(jnp.float32)
    out_ref[...] = total.astype(jnp.bfloat16)


def finish_kernel(scale, info_ref, even_ref, odd_ref, terms_ref, *refs):
    out_ref = refs[-1]
    total = even_ref[...].astype(jnp.float32) + odd_ref[...].astype(jnp.float32)
    out_ref[0] = (total + terms_ref[0].astype(jnp.float32)) * scale


def limits(vmem=VMEM_LIMIT, **more):
    return dict(
        compiler_params=pltpu.CompilerParams(vmem_limit_bytes=vmem),
        cost_estimate=pl.CostEstimate(flops=0, bytes_accessed=0, transcendentals=0),
        **more,
    )


SMEM_SPEC = pl.BlockSpec(memory_space=pltpu.SMEM)
HBM_SPEC = pl.BlockSpec(memory_space=pltpu.HBM)
VMEM_SPEC = pl.BlockSpec(memory_space=pltpu.VMEM)


def call(kernel, sizes, ins, outs):
    heads, seg_len, head_dim, count = sizes
    blocks = {
        "c": (seg_len, head_dim),
        "p": (seg_len, 2 * head_dim),
        "r": (1, head_dim),
        "o": (1, 2 * head_dim),
        "R": (count, 2 * head_dim),
        "m": (1, head_dim, head_dim),
        "s": (8, seg_len),
        "n": (16, max(seg_len, head_dim)),
    }

    def spec(kind):
        if kind == "f":
            return SMEM_SPEC
        if kind == "m":
            return pl.BlockSpec(blocks[kind], lambda h: (h, 0, 0))
        if kind in "sn":
            return pl.BlockSpec(blocks[kind], lambda h: (h, 0))
        return pl.BlockSpec(blocks[kind], lambda h: (0, h))

    def shape(kind):
        block = blocks[kind]
        if kind in "msn":
            return (heads * block[0],) + block[1:]
        return (block[0], heads * block[1])

    return pl.pallas_call(
        kernel,
        grid=(heads,),
        in_specs=[spec(kind) for kind in ins],
        out_specs=[spec(kind) for kind, _ in outs],
        out_shape=[jax.ShapeDtypeStruct(shape(kind), dtype) for kind, dtype in outs],
        **limits(),
    )


def local(inputs, w_query, w_key, w_value, gate_bias, cotangent):
    tokens = inputs[0]
    cot = cotangent[0]
    seg_len, model_dim = tokens.shape
    heads = gate_bias.shape[0]
    columns = w_query.shape[1]
    head_dim = columns // heads
    seq_count, seq_at = lax.axis_size("seq"), lax.axis_index("seq")
    dp_count, dp_at = lax.axis_size("dp"), lax.axis_index("dp")
    plane, place = lax.axis_size("head"), lax.axis_index("head")
    part_rows = model_dim // (seq_count * dp_count)
    f32, bf16 = jnp.float32, jnp.bfloat16
    info = jnp.stack([seq_at, 1 - seq_at % 2, dp_at, place]).astype(jnp.int32)

    def shifted(x, by, first=0, last=None):
        last = seq_count - 1 if last is None else last
        pairs = [
            (i, i + by) for i in range(first, last + 1) if 0 <= i + by < seq_count
        ]
        return lax.ppermute(x, "seq", pairs)

    def swapped(x, distance, parity, lowest=0):
        pairs = []
        for i in range(seq_count - distance):
            if (i // distance) % 2 == parity:
                if i >= lowest:
                    pairs.append((i, i + distance))
                if seq_count - 1 - (i + distance) >= lowest:
                    pairs.append((i + distance, i))
        return lax.ppermute(x, "seq", pairs) if pairs else None

    def from_core(x, step):
        return lax.ppermute(x, "dp", [(i, (i + step) % dp_count) for i in range(dp_count)])

    count = -(-(seq_count - 1) // 8) * 8
    sizes = (heads, seg_len, head_dim, count)
    mix = jnp.repeat(jax.nn.sigmoid(gate_bias), head_dim)[None]

    by_swaps = seq_count == 4 and part_rows % 128 == 0
    pieces = 2
    wide_shape = jax.ShapeDtypeStruct((seg_len, 2 * columns), bf16)
    pair, query, even_message, odd_message, row = pl.pallas_call(
        functools.partial(project_kernel, heads),
        in_specs=[SMEM_SPEC] + [HBM_SPEC] * 5,
        out_specs=[VMEM_SPEC] * 5,
        out_shape=[wide_shape] * 4 + [jax.ShapeDtypeStruct((1, 2 * columns), f32)],
        scratch_shapes=[
            pltpu.VMEM((seg_len, model_dim), bf16),
            pltpu.VMEM((3, pieces, model_dim // pieces, columns), bf16),
            pltpu.VMEM((seg_len, columns), bf16),
            pltpu.SemaphoreType.DMA((4 * pieces + 1,)),
        ],
        **limits(62 * 1024 * 1024),
    )(info, tokens, w_key, w_value, w_query, cot)
    even_arrived = swapped(even_message, 1, 0)
    odd_arrived = swapped(odd_message, 1, 1)
    far_rows = [shifted(row, step) for step in range(2, seq_count)]
    free = jnp.zeros_like(row)
    pad = jnp.zeros((count - seq_count + 1, 2 * columns), f32)
    near = jnp.concatenate([free] + far_rows[:-1] + [free, pad], 0)
    far = jnp.concatenate([free] + far_rows + [pad], 0)

    routes = [
        (distance, parity)
        for distance in range(1, seq_count - 1)
        for parity in range(2)
        if any(
            (i // distance) % 2 == parity and (i > 0 or i + distance < seq_count - 1)
            for i in range(seq_count - distance)
        )
    ]
    routes = [route for route in routes if route != (1, 0)] + [(1, 0)]
    over = "m" * len(routes)
    pair_prev, query_next, memory, grad_memory, row_prev, *sent = call(
        functools.partial(neighbour_kernel, routes),
        sizes,
        "fppRor",
        [("p", bf16)] * 2 + [("m", bf16)] * 2 + [("o", f32)] + [("m", bf16)] * len(routes),
    )(info, even_arrived, odd_arrived, near, row, mix)
    arrived = [swapped(part, *route, lowest=1) for part, route in zip(sent, routes)]
    local_out, grad_att, stats = call(
        attend_kernel, sizes, "fpppr", (("c", f32), ("c", f32), ("s", f32))
    )(info, query, pair, pair_prev, mix)
    if by_swaps:
        all_tokens = [tokens] + [from_core(tokens, step) for step in range(1, dp_count)]
        all_tokens, stats = lax.optimization_barrier((all_tokens, stats))
        token_parts = pl.pallas_call(
            functools.partial(pack_kernel, seq_count, dp_count),
            in_specs=[SMEM_SPEC] + [VMEM_SPEC] * dp_count,
            out_specs=[VMEM_SPEC] * dp_count,
            out_shape=[jax.ShapeDtypeStruct((seq_count * part_rows, seg_len), bf16)] * dp_count,
            **limits(),
        )(info, *all_tokens)
        local_out, token_parts = lax.optimization_barrier((local_out, token_parts))
    blended, grad_query, note = call(
        functools.partial(retrieve_kernel, routes),
        sizes,
        "fpoRrccsm" + over,
        (("c", bf16), ("c", bf16), ("n", f32)),
    )(info, query, row_prev, far, mix, local_out, grad_att, stats, memory, *arrived)
    notes = [shifted(note, -step) for step in range(1, seq_count)]

    def row_blocks(grad):
        grads = [grad] + [from_core(grad, step) for step in range(1, dp_count)]
        return pl.pallas_call(
            row_blocks_kernel,
            grid=(seq_count,),
            in_specs=[SMEM_SPEC]
            + [pl.BlockSpec((part_rows, seg_len), lambda b: (b, 0))] * dp_count
            + [pl.BlockSpec((seg_len, columns), lambda b: (0, 0))] * dp_count,
            out_specs=[
                pl.BlockSpec((1, part_rows, columns), lambda b: (b, 0, 0)),
                pl.BlockSpec((2, part_rows, columns), lambda b: (0, 0, 0)),
            ],
            out_shape=[
                jax.ShapeDtypeStruct((seq_count, part_rows, columns), bf16),
                jax.ShapeDtypeStruct((2, part_rows, columns), bf16),
            ],
            **limits(),
        )(info, *token_parts, *grads)

    grad_scale = 1.0 / math.sqrt(seq_count * dp_count * seg_len)
    block = (part_rows, columns)
    part_shape = jax.ShapeDtypeStruct(block, bf16)
    whole = pl.BlockSpec(block, lambda i, info: (0, 0))

    def on_terms(kernel, ins, outs, out_shape, **more):
        return pl.pallas_call(
            kernel,
            grid_spec=pltpu.PrefetchScalarGridSpec(
                num_scalar_prefetch=1, grid=(1,), in_specs=ins, out_specs=outs
            ),
            out_shape=out_shape,
            **limits(**more),
        )

    def at_block(index):
        return pl.BlockSpec((1,) + block, lambda i, info: (index(info[SEQ]), 0, 0))

    def swapped_ends(first):
        last = seq_count - 1
        return lax.ppermute(first, "seq", [(0, 1), (last, last - 1)])

    def inner_messages(terms, arrived):
        def inner(info_ref, *refs):
            inner_kernel(*refs)

        return on_terms(
            inner,
            [
                pl.BlockSpec((2,) + block, lambda i, info: (0, 0, 0)),
                at_block(lambda z: jnp.where(z < 2, 3, 0)),
                at_block(lambda z: jnp.where(z < 2, 2, 1)),
            ],
            [whole, whole],
            [part_shape] * 2,
        )(info, arrived, terms, terms)

    def over_middle(terms, arrived):
        return [swapped(message, 1, 1) for message in inner_messages(terms, arrived)]

    def end_message(terms, far):
        return on_terms(
            outer_kernel,
            [whole, at_block(lambda z: lax.bitwise_xor(z, 1))],
            whole,
            part_shape,
        )(info, far, terms)

    def to_ends(terms, far):
        return swapped(end_message(terms, far), 1, 0)

    def finish(terms, even, odd, which, into=()):
        return on_terms(
            functools.partial(finish_kernel, grad_scale),
            [whole, whole, at_block(lambda z: z)] + [HBM_SPEC] * len(into),
            pl.BlockSpec((1,) + block, lambda i, info: (which, 0, 0)),
            jax.ShapeDtypeStruct((3,) + block, f32),
            input_output_aliases={4: 0} if into else {},
        )(info, even, odd, terms, *into)

    if by_swaps:
        query_terms, query_first = row_blocks(grad_query)
        notes[0], query_terms, query_first = lax.optimization_barrier(
            (notes[0], query_terms, query_first)
        )
        query_ends = swapped_ends(query_first)
    grad_key, grad_value = call(
        functools.partial(key_value_kernel, routes, len(notes)),
        sizes,
        "fppnpr" + "n" * len(notes) + over + "m",
        (("c", bf16), ("c", bf16)),
    )(info, pair, query, note, query_next, mix, *notes, grad_memory, *arrived)
    if not by_swaps:
        contract = (((0,), (0,)), ((), ()))

        def rows_for(core):
            return jnp.concatenate(
                [
                    lax.dynamic_slice_in_dim(
                        tokens, (block * dp_count + core) * part_rows, part_rows, 1
                    )
                    for block in range(seq_count)
                ],
                1,
            )

        token_columns = [rows_for(dp_at)] + [
            from_core(rows_for((dp_at + step) % dp_count), step) for step in range(1, dp_count)
        ]

        def summed(grad):
            grads = [grad] + [from_core(grad, step) for step in range(1, dp_count)]
            terms = sum(
                lax.dot_general(part, term, contract, preferred_element_type=f32)
                for part, term in zip(token_columns, grads)
            ).reshape(seq_count, part_rows, grad.shape[1])

            def block(index):
                index = jnp.clip(index, 0, seq_count - 1)
                return lax.dynamic_index_in_dim(terms, index, 0, False)

            ups = downs = jnp.zeros((part_rows, grad.shape[1]), bf16)
            for turn in range(1, seq_count):
                ahead = seq_count - turn
                ups = shifted((ups + block(seq_at + ahead)).astype(bf16), 1, 0, turn - 1)
                downs = shifted((downs + block(seq_at - ahead)).astype(bf16), -1, ahead)
            return ups + downs + block(seq_at)

        rows = summed(jnp.concatenate([grad_query, grad_key, grad_value], 1)) * grad_scale
        return (blended[None], rows.reshape(part_rows, 3, columns))

    value_terms, value_first = row_blocks(grad_value)
    value_ends = swapped_ends(value_first)
    grad_key, value_terms = lax.optimization_barrier((grad_key, value_terms))
    key_terms, key_first = row_blocks(grad_key)
    key_ends = swapped_ends(key_first)
    key_terms, query_ends = lax.optimization_barrier((key_terms, query_ends))
    query_far, query_near = over_middle(query_terms, query_ends)
    value_ends, query_far, query_near = lax.optimization_barrier(
        (value_ends, query_far, query_near)
    )
    query_even = to_ends(query_terms, query_far)
    value_far, value_near = over_middle(value_terms, value_ends)
    key_ends, value_far, value_near = lax.optimization_barrier((key_ends, value_far, value_near))
    value_even = to_ends(value_terms, value_far)
    key_far, key_near = over_middle(key_terms, key_ends)
    key_far, query_even = lax.optimization_barrier((key_far, query_even))
    key_even = to_ends(key_terms, key_far)
    grad_weights = finish(query_terms, query_even, query_near, 0)
    grad_weights = finish(value_terms, value_even, value_near, 2, (grad_weights,))
    grad_weights = finish(key_terms, key_even, key_near, 1, (grad_weights,))
    return (blended[None], jnp.transpose(grad_weights, (1, 0, 2)))


def solution(mesh):
    return jax.shard_map(
        local,
        mesh=mesh,
        in_specs=(
            P("dp", "seq", None),
            P(None, "head"),
            P(None, "head"),
            P(None, "head"),
            P("head"),
            P("dp", "seq", "head"),
        ),
        out_specs=(P("dp", "seq", "head"), P(("seq", "dp"), None, "head")),
        check_vma=False,
    )
```

time: 175 us -> 165 us (0.943)
  Pallas kernels: 24 us -> 44.1 us
  other arithmetic: 10.7 us -> 0.69 us
  matrix products: 9.9 us -> 0 us
  waiting for transfers between devices: 55.4 us -> 46.6 us
    ppermute x0 -> x17, starting transfers between devices: none -> 57.8 us  [the longest x14 44.9 us: swapped(): return lax.ppermute(x, 'seq', pairs) if pairs else None]
    ppermute x31 -> x5, starting transfers between devices: 67.2 us -> 10.4 us  [shifted(): return lax.ppermute(x, 'seq', pairs)]
    ppermute x31 -> x5, waiting for transfers between devices: 55.3 us -> 14.9 us  [shifted(): return lax.ppermute(x, 'seq', pairs)]
    ppermute x0 -> x17, waiting for transfers between devices: none -> 31.8 us  [the longest x3 18.4 us: swapped_ends(): return lax.ppermute(first, 'seq', [(0, 1), (last, last - 1)])]
    pallas_call x6 -> x17, Pallas kernels: 19.2 us -> 39.9 us  [the longest x1 10.3 us: local(): pl.pallas_call(functools.partial(project_kernel, heads), in_specs=[SMEM_S...]
    dot_general x6 -> x0, matrix products: 9.9 us -> none  [weight_term(): product = lax.dot_general(rows, term, contract, preferred_element_type=f32)]
    convert_element_type x13 -> x0, other arithmetic: 6.26 us -> none  [the longest x6 4.21 us: chain(): total = total + shifted((total + own).astype(bf16), by, at, at)]
  transfers between devices with their start and end apart: 35 -> 26, of which waited for: 12 -> 10; matrix products, arithmetic and copies ran while one was open for 12% -> 1% of each run, Pallas kernels for 11% -> 21%
where the time goes in v3:
time: 165 us
  starting transfers between devices  69 us (42%)
  waiting for transfers between devices  46.6 us (28%)
  Pallas kernels  44.1 us (27%)
  local copies, waits for them, and re-layouts  3.12 us (2%)
    ppermute x14, starting transfers between devices, swapped(): return lax.ppermute(x, 'seq', pairs) if pairs else None  44.9 us
    ppermute x3, waiting for transfers between devices, swapped_ends(): return lax.ppermute(first, 'seq', [(0, 1), (last, last - 1)])  18.4 us
    ppermute x5, waiting for transfers between devices, shifted(): return lax.ppermute(x, 'seq', pairs)  14.9 us
    ppermute x14, waiting for transfers between devices, swapped(): return lax.ppermute(x, 'seq', pairs) if pairs else None  13.4 us
    ppermute x3, starting transfers between devices, swapped_ends(): return lax.ppermute(first, 'seq', [(0, 1), (last, last - 1)])  12.9 us
    ppermute x5, starting transfers between devices, shifted(): return lax.ppermute(x, 'seq', pairs)  10.4 us
    pallas_call x1, Pallas kernels, local(): pl.pallas_call(functools.partial(project_kernel, heads), in_specs=[SMEM_S...  10.3 us
    pallas_call x3, Pallas kernels, row_blocks(): pl.pallas_call(row_blocks_kernel, grid=(seq_count,), in_specs=[SMEM_SPEC]...  8.75 us
  transfers between devices with their start and end apart: 26, of which 10 were waited for; matrix products, arithmetic and copies ran while one was open for 1% of the time, Pallas kernels for 21%

profile of v3, /device:TPU:0, one launch (start us, length us, event | category | flops | bytes accessed | tf_op | source)
XLA Modules:
  0.0 164.5 jit_solution(695598544303620148)
XLA Ops:
  0.6 0.5 collective-permute-start.4
  1.1 0.6 pad_add_fusion.info_ref
  1.8 10.3 %shard_map.77 = (bf16[384,1024]{1,0:T(8,128)(2,1)}, bf16[384,1024]{1,0:T(8,128)(2,1)}, bf16[384,1024]{1,0:T(8,128)(2,1)}, bf16[384,1024]{1,0:T(8,128)(2,1)}, f32[1,1024]{1,0:T(1,128)}) custom-call(s32[4]{0:T(128)} %pad_add_fusion.info_ref, bf16[384,3072]{1,0:T(8,128)(2,1)} %bitcast.13, bf16[3072,512]{1,0:T(8,128)(2,1)} %w_key_ref.1, ...), custom_call_target="tpu_custom_call" | custom-call | tf_op jit(solution)/shard_map/pallas_call | solution.py:448
  12.1 0.0 copy-start
  12.1 2.7 %collective-permute-start = (bf16[384,1024]{1,0:T(8,128)(2,1)}, bf16[384,1024]{1,0:T(8,128)(2,1)S(1)}, u32[]{:S(2)}, u32[]{:S(2)}) collective-permute-start(bf16[384,1024]{1,0:T(8,128)(2,1)} %get-tuple-element.59), channel_id=1, source_target_pairs={{0,8},{8,0},{16,24},{24,16},{1,9},{9,1},{17,25},{25,17},{2,10},{10... | collective-permute-start | bytes 2359304 | tf_op jit(solution)/shard_map/ppermute | solution.py:436
  14.8 0.7 collective-permute-start.1
  15.5 4.4 %collective-permute-start.3 = (f32[1,1024]{1,0:T(1,128)}, f32[1,1024]{1,0:T(1,128)S(1)}, u32[]{:S(2)}, u32[]{:S(2)}) collective-permute-start(f32[1,1024]{1,0:T(1,128)} %get-tuple-element.61.row_ref), channel_id=1, source_target_pairs={{0,24},{1,25},{2,26},{3,27},{4,28},{5,29},{6,30},{7,31}} | collective-permute-start | bytes 12296 | tf_op jit(solution)/shard_map/ppermute | solution.py:426
  20.0 1.9 %collective-permute-start.2 = (f32[1,1024]{1,0:T(1,128)}, f32[1,1024]{1,0:T(1,128)S(1)}, u32[]{:S(2)}, u32[]{:S(2)}) collective-permute-start(f32[1,1024]{1,0:T(1,128)} %get-tuple-element.61.row_ref), channel_id=1, source_target_pairs={{0,16},{8,24},{1,17},{9,25},{2,18},{10,26},{3,19},{11,27},{4,20},{... | collective-permute-start | bytes 12296 | tf_op jit(solution)/shard_map/ppermute | solution.py:426
  21.9 0.1 broadcast_bitcast_fusion
  22.0 0.1 pad.7.clone
  22.1 10.6 %collective-permute-done.3 = f32[1,1024]{1,0:T(1,128)S(1)} collective-permute-done((f32[1,1024]{1,0:T(1,128)}, f32[1,1024]{1,0:T(1,128)S(1)}, u32[]{:S(2)}, u32[]{:S(2)}) %collective-permute-start.3) | collective-permute-done | bytes 4128 | tf_op jit(solution)/shard_map/ppermute | solution.py:426
  32.7 0.1 fusion.1
  32.7 0.5 collective-permute-done.even_ref
  33.2 0.0 collective-permute-done.1.odd_ref
  33.2 0.7 copy-done.6
  33.9 2.1 %shard_map.78 = (bf16[384,1024]{1,0:T(8,128)(2,1)S(1)}, bf16[384,1024]{1,0:T(8,128)(2,1)S(1)}, bf16[2,256,256]{2,1,0:T(8,128)(2,1)S(1)}, bf16[2,256,256]{2,1,0:T...) custom-call(s32[4]{0:T(128)S(1)} %copy-done.5, ...), custom_call_target="tpu_custom_call" | custom-call | tf_op jit(solution)/shard_map/pallas_call | solution.py:480
  36.0 0.7 collective-permute-start.5
  36.7 1.3 collective-permute-start.6
  38.0 1.3 collective-permute-start.7
  39.3 1.1 copy-done.1
  40.4 1.1 copy-done.3
  41.6 4.2 %shard_map.79 = (f32[384,512]{1,0:T(8,128)S(1)}, f32[384,512]{1,0:T(8,128)S(1)}, f32[16,384]{1,0:T(8,128)S(1)}) custom-call(s32[4]{0:T(128)S(1)} %copy-done.5, bf16[384,1024]{1,0:T(8,128)(2,1)S(1)} %copy-done.1, bf16[384,1024]{1,0:T(8,128)(2,1)S(1)} %copy-done.3, bf16[384,1024]{1,0:T(8,128)(2,1)S(1)} %get-tuple-element.64.prev_ref, f32[1,512]{1,0:T(1,128)S(1)} %bitcast.16), custom_call_target="tpu_custom_call" | custom-call | tf_op jit(solution)/shard_map/pallas_call | solution.py:487
  45.8 2.4 %shard_map.80 = (bf16[1536,384]{1,0:T(8,128)(2,1)S(1)}, bf16[1536,384]{1,0:T(8,128)(2,1)S(1)}) custom-call(s32[4]{0:T(128)S(1)} %copy-done.5, bf16[384,3072]{1,0:T(8,128)(2,1)S(1)} %bitcast.14, bf16[384,3072]{1,0:T(8,128)(2,1)} %collective-permute-done.4.refs_1_), custom_call_target="tpu_custom_call" | custom-call | tf_op jit(solution)/shard_map/pallas_call | solution.py:493
  48.2 7.5 %collective-permute-done.6.refs_2_.refs_5_ = bf16[2,256,256]{2,1,0:T(8,128)(2,1)S(1)} collective-permute-done((bf16[2,256,256]{2,1,0:T(8,128)(2,1)S(1)}, bf16[2,256,256]{2,1,0:T(8,128)(2,1)S(1)}, u32[]{:S(2)}, u32[]{:S(2)}) %collective-permute-start.6) | collective-permute-done | bytes 262176 | tf_op jit(solution)/shard_map/ppermute | solution.py:436
  55.7 2.8 %collective-permute-done.7.refs_3_.refs_6_ = bf16[2,256,256]{2,1,0:T(8,128)(2,1)S(1)} collective-permute-done((bf16[2,256,256]{2,1,0:T(8,128)(2,1)S(1)}, bf16[2,256,256]{2,1,0:T(8,128)(2,1)S(1)}, u32[]{:S(2)}, u32[]{:S(2)}) %collective-permute-start.7) | collective-permute-done | bytes 262176 | tf_op jit(solution)/shard_map/ppermute | solution.py:436
  58.5 3.3 %shard_map.81 = (bf16[384,512]{1,0:T(8,128)(2,1)}, bf16[384,512]{1,0:T(8,128)(2,1)S(1)}, f32[32,384]{1,0:T(8,128)S(1)}) custom-call(s32[4]{0:T(128)S(1)} %copy-done.5, bf16[384,1024]{1,0:T(8,128)(2,1)S(1)} %copy-done.2, f32[1,1024]{1,0:T(1,128)S(1)} %get-tuple-element.62.row_prev_ref, f32[8,1024]{1,0:T(8,128)S(1)} %get-tuple-element.114.far_ref, ...), custom_call_target="tpu_custom_call" | custom-call | tf_op jit(solution)/shard_map/pallas_call | solution.py:501
  61.8 0.0 collective-permute-start.9
  61.8 1.4 collective-permute-start.8
  63.3 1.3 collective-permute-start.11
  64.6 1.3 collective-permute-start.10
  65.9 0.0 collective-permute-done.9.refs_3_
  65.9 2.9 %shard_map.82 = (bf16[4,384,512]{2,1,0:T(8,128)(2,1)S(1)}, bf16[2,384,512]{2,1,0:T(8,128)(2,1)S(1)}) custom-call(s32[4]{0:T(128)S(1)} %copy-done.5, bf16[1536,384]{1,0:T(8,128)(2,1)S(1)} %get-tuple-element.79.refs_0_, bf16[1536,384]{1,0:T(8,128)(2,1)S(1)} %get-tuple-element.80.refs_1_, bf16[384,512]{1,0:T(8,128)(2,1)S(1)} %get-tuple-element.83.refs_2_, ...), custom_call_target="tpu_custom_call" | custom-call | tf_op jit(solution)/shard_map/pallas_call | solution.py:511
  68.8 2.3 %collective-permute-done.11.refs_2_ = f32[32,384]{1,0:T(8,128)S(1)} collective-permute-done((f32[32,384]{1,0:T(8,128)S(1)}, f32[32,384]{1,0:T(8,128)S(1)}, u32[]{:S(2)}, u32[]{:S(2)}) %collective-permute-start.11) | collective-permute-done | bytes 49184 | tf_op jit(solution)/shard_map/ppermute | solution.py:426
  71.1 2.0 %collective-permute-done.10.refs_1_ = f32[32,384]{1,0:T(8,128)S(1)} collective-permute-done((f32[32,384]{1,0:T(8,128)S(1)}, f32[32,384]{1,0:T(8,128)S(1)}, u32[]{:S(2)}, u32[]{:S(2)}) %collective-permute-start.10) | collective-permute-done | bytes 49184 | tf_op jit(solution)/shard_map/ppermute | solution.py:426
  73.1 4.2 %shard_map.83 = (bf16[384,512]{1,0:T(8,128)(2,1)S(1)}, bf16[384,512]{1,0:T(8,128)(2,1)S(1)}) custom-call(s32[4]{0:T(128)S(1)} %copy-done.5, bf16[384,1024]{1,0:T(8,128)(2,1)S(1)} %copy-done.4, bf16[384,1024]{1,0:T(8,128)(2,1)S(1)} %copy-done.2, f32[32,384]{1,0:T(8,128)S(1)} %get-tuple-element.81.note_ref, ...), custom_call_target="tpu_custom_call" | custom-call | tf_op jit(solution)/shard_map/pallas_call | solution.py:594
  77.3 0.1 collective-permute-start.12
  77.4 2.3 %collective-permute-start.16 = (bf16[2,384,512]{2,1,0:T(8,128)(2,1)S(1)}, bf16[2,384,512]{2,1,0:T(8,128)(2,1)S(1)}, u32[]{:S(2)}, u32[]{:S(2)}) collective-permute-start(bf16[2,384,512]{2,1,0:T(8,128)(2,1)S(1)} %get-tuple-element.95), channel_id=1, source_target_pairs={{0,8},{24,16},{1,9},{25,17},{2,10},{26,18},{3,11},{27,19},{4,12},{... | collective-permute-start | bytes 2359304 | tf_op jit(solution)/shard_map/ppermute | solution.py:548
  79.7 2.9 %shard_map.84 = (bf16[4,384,512]{2,1,0:T(8,128)(2,1)S(1)}, bf16[2,384,512]{2,1,0:T(8,128)(2,1)S(1)}) custom-call(s32[4]{0:T(128)S(1)} %copy-done.5, bf16[1536,384]{1,0:T(8,128)(2,1)S(1)} %get-tuple-element.79.refs_0_, bf16[1536,384]{1,0:T(8,128)(2,1)S(1)} %get-tuple-element.80.refs_1_, bf16[384,512]{1,0:T(8,128)(2,1)S(1)} %get-tuple-element.89.refs_2_, ...), custom_call_target="tpu_custom_call" | custom-call | tf_op jit(solution)/shard_map/pallas_call | solution.py:511
  82.7 0.3 collective-permute-start.13
  82.9 1.6 collective-permute-start.15
  84.6 2.9 %shard_map.85 = (bf16[4,384,512]{2,1,0:T(8,128)(2,1)S(1)}, bf16[2,384,512]{2,1,0:T(8,128)(2,1)S(1)}) custom-call(s32[4]{0:T(128)S(1)} %copy-done.5, bf16[1536,384]{1,0:T(8,128)(2,1)S(1)} %get-tuple-element.79.refs_0_, bf16[1536,384]{1,0:T(8,128)(2,1)S(1)} %get-tuple-element.80.refs_1_, bf16[384,512]{1,0:T(8,128)(2,1)S(1)} %get-tuple-element.91.refs_2_, ...), custom_call_target="tpu_custom_call" | custom-call | tf_op jit(solution)/shard_map/pallas_call | solution.py:511
  87.5 10.0 %collective-permute-done.16.refs_0_ = bf16[2,384,512]{2,1,0:T(8,128)(2,1)S(1)} collective-permute-done((bf16[2,384,512]{2,1,0:T(8,128)(2,1)S(1)}, bf16[2,384,512]{2,1,0:T(8,128)(2,1)S(1)}, u32[]{:S(2)}, u32[]{:S(2)}) %collective-permute-start.16) | collective-permute-done | bytes 786464 | tf_op jit(solution)/shard_map/ppermute | solution.py:548
  97.5 0.7 shard_map.86
  98.3 0.7 collective-permute-start.17
  98.9 0.7 collective-permute-start.18
  99.6 8.9 %collective-permute-start.14 = (bf16[2,384,512]{2,1,0:T(8,128)(2,1)S(1)}, bf16[2,384,512]{2,1,0:T(8,128)(2,1)S(1)}, u32[]{:S(2)}, u32[]{:S(2)}) collective-permute-start(bf16[2,384,512]{2,1,0:T(8,128)(2,1)S(1)} %get-tuple-element.92), channel_id=1, source_target_pairs={{0,8},{24,16},{1,9},{25,17},{2,10},{26,18},{3,11},{27,19},{4,12},{... | collective-permute-start | bytes 2359304 | tf_op jit(solution)/shard_map/ppermute | solution.py:548
  108.6 5.8 %collective-permute-done.15.refs_0_ = bf16[2,384,512]{2,1,0:T(8,128)(2,1)S(1)} collective-permute-done((bf16[2,384,512]{2,1,0:T(8,128)(2,1)S(1)}, bf16[2,384,512]{2,1,0:T(8,128)(2,1)S(1)}, u32[]{:S(2)}, u32[]{:S(2)}) %collective-permute-start.15) | collective-permute-done | bytes 786464 | tf_op jit(solution)/shard_map/ppermute | solution.py:548
  114.4 0.7 shard_map.87
  115.1 0.7 collective-permute-start.19
  115.8 0.7 collective-permute-start.20
  116.5 0.6 shard_map.89
  117.1 11.5 %collective-permute-start.22 = (bf16[384,512]{1,0:T(8,128)(2,1)S(1)}, bf16[384,512]{1,0:T(8,128)(2,1)S(1)}, u32[]{:S(2)}, u32[]{:S(2)}) collective-permute-start(bf16[384,512]{1,0:T(8,128)(2,1)S(1)} %shard_map.89), channel_id=1, source_target_pairs={{0,8},{8,0},{16,24},{24,16},{1,9},{9,1},{17,25},{25,17},{2,10},{10... | collective-permute-start | bytes 1179656 | tf_op jit(solution)/shard_map/ppermute | solution.py:436
  128.7 2.5 %collective-permute-done.14.refs_0_ = bf16[2,384,512]{2,1,0:T(8,128)(2,1)S(1)} collective-permute-done((bf16[2,384,512]{2,1,0:T(8,128)(2,1)S(1)}, bf16[2,384,512]{2,1,0:T(8,128)(2,1)S(1)}, u32[]{:S(2)}, u32[]{:S(2)}) %collective-permute-start.14) | collective-permute-done | bytes 786464 | tf_op jit(solution)/shard_map/ppermute | solution.py:548
  131.2 0.7 shard_map.88
  132.0 0.7 collective-permute-start.21
  132.7 0.6 shard_map.91
  133.3 12.5 %collective-permute-start.25 = (bf16[384,512]{1,0:T(8,128)(2,1)S(1)}, bf16[384,512]{1,0:T(8,128)(2,1)S(1)}, u32[]{:S(2)}, u32[]{:S(2)}) collective-permute-start(bf16[384,512]{1,0:T(8,128)(2,1)S(1)} %shard_map.91), channel_id=1, source_target_pairs={{0,8},{8,0},{16,24},{24,16},{1,9},{9,1},{17,25},{25,17},{2,10},{10... | collective-permute-start | bytes 1179656 | tf_op jit(solution)/shard_map/ppermute | solution.py:436
  145.8 0.7 collective-permute-start.24
  146.5 0.6 shard_map.90
  147.1 10.1 %collective-permute-start.23 = (bf16[384,512]{1,0:T(8,128)(2,1)S(1)}, bf16[384,512]{1,0:T(8,128)(2,1)S(1)}, u32[]{:S(2)}, u32[]{:S(2)}) collective-permute-start(bf16[384,512]{1,0:T(8,128)(2,1)S(1)} %shard_map.90), channel_id=1, source_target_pairs={{0,8},{8,0},{16,24},{24,16},{1,9},{9,1},{17,25},{25,17},{2,10},{10... | collective-permute-start | bytes 1179656 | tf_op jit(solution)/shard_map/ppermute | solution.py:436
  157.2 1.6 shard_map.92.refs_0_
  158.8 1.6 shard_map.93.refs_0_
  160.4 2.6 %collective-permute-done.23.even_ref = bf16[384,512]{1,0:T(8,128)(2,1)S(1)} collective-permute-done((bf16[384,512]{1,0:T(8,128)(2,1)S(1)}, bf16[384,512]{1,0:T(8,128)(2,1)S(1)}, u32[]{:S(2)}, u32[]{:S(2)}) %collective-permute-start.23) | collective-permute-done | bytes 393248 | tf_op jit(solution)/shard_map/ppermute | solution.py:436
  163.0 1.6 shard_map.94
  (30 shorter events, 0.1 us)
Async XLA Ops:
  0.6 45.1 %collective-permute-start.4 = (bf16[384,3072]{1,0:T(8,128)(2,1)}, bf16[384,3072]{1,0:T(8,128)(2,1)}, u32[]{:S(2)}, u32[]{:S(2)}) collective-permute-start(bf16[384,3072]{1,0:T(8,128)(2,1)} %bitcast.12), channel_id=1, source_target_pairs={{0,4},{4,0},{1,5},{5,1},{2,6},{6,2},{3,7},{7,3},{8,12},{12,8},{9,1... | collective-permute-start | bytes 7077896 | tf_op jit(solution)/shard_map/ppermute | solution.py:439
  1.8 20.1 %copy-start.7 = (f32[2]{0:T(128)S(1)}, f32[2]{0:T(128)}, u32[]{:S(2)}) copy-start(f32[2]{0:T(128)} %param.10) | copy-start | bytes 28
  1.8 31.5 %copy-start.5 = (s32[4]{0:T(128)S(1)}, s32[4]{0:T(128)}, u32[]{:S(2)}) copy-start(s32[4]{0:T(128)} %pad_add_fusion.info_ref) | copy-start | bytes 52
  12.1 33.7 %copy-start = (bf16[1,384,3072]{2,1,0:T(8,128)(2,1)S(1)}, bf16[1,384,3072]{2,1,0:T(8,128)(2,1)}, u32[]{:S(2)}) copy-start(bf16[1,384,3072]{2,1,0:T(8,128)(2,1)} %param.6) | copy-start | bytes 7077892
  12.1 21.1 %collective-permute-start = (bf16[384,1024]{1,0:T(8,128)(2,1)}, bf16[384,1024]{1,0:T(8,128)(2,1)S(1)}, u32[]{:S(2)}, u32[]{:S(2)}) collective-permute-start(bf16[384,1024]{1,0:T(8,128)(2,1)} %get-tuple-element.59), channel_id=1, source_target_pairs={{0,8},{8,0},{16,24},{24,16},{1,9},{9,1},{17,25},{25,17},{2,10},{10... | collective-permute-start | bytes 2359304 | tf_op jit(solution)/shard_map/ppermute | solution.py:436
  14.8 18.4 %collective-permute-start.1 = (bf16[384,1024]{1,0:T(8,128)(2,1)}, bf16[384,1024]{1,0:T(8,128)(2,1)S(1)}, u32[]{:S(2)}, u32[]{:S(2)}) collective-permute-start(bf16[384,1024]{1,0:T(8,128)(2,1)} %get-tuple-element.60), channel_id=1, source_target_pairs={{8,16},{16,8},{9,17},{17,9},{10,18},{18,10},{11,19},{19,11},{12,20... | collective-permute-start | bytes 2359304 | tf_op jit(solution)/shard_map/ppermute | solution.py:436
  15.5 17.1 %collective-permute-start.3 = (f32[1,1024]{1,0:T(1,128)}, f32[1,1024]{1,0:T(1,128)S(1)}, u32[]{:S(2)}, u32[]{:S(2)}) collective-permute-start(f32[1,1024]{1,0:T(1,128)} %get-tuple-element.61.row_ref), channel_id=1, source_target_pairs={{0,24},{1,25},{2,26},{3,27},{4,28},{5,29},{6,30},{7,31}} | collective-permute-start | bytes 12296 | tf_op jit(solution)/shard_map/ppermute | solution.py:426
  20.0 12.7 %collective-permute-start.2 = (f32[1,1024]{1,0:T(1,128)}, f32[1,1024]{1,0:T(1,128)S(1)}, u32[]{:S(2)}, u32[]{:S(2)}) collective-permute-start(f32[1,1024]{1,0:T(1,128)} %get-tuple-element.61.row_ref), channel_id=1, source_target_pairs={{0,16},{8,24},{1,17},{9,25},{2,18},{10,26},{3,19},{11,27},{4,20},{... | collective-permute-start | bytes 12296 | tf_op jit(solution)/shard_map/ppermute | solution.py:426
  33.2 0.7 copy-start.6
  36.0 12.2 %collective-permute-start.5 = (bf16[2,256,256]{2,1,0:T(8,128)(2,1)S(1)}, bf16[2,256,256]{2,1,0:T(8,128)(2,1)S(1)}, u32[]{:S(2)}, u32[]{:S(2)}) collective-permute-start(bf16[2,256,256]{2,1,0:T(8,128)(2,1)S(1)} %get-tuple-element.75), channel_id=1, source_target_pairs={{8,16},{16,8},{9,17},{17,9},{10,18},{18,10},{11,19},{19,11},{12,20... | collective-permute-start | bytes 786440 | tf_op jit(solution)/shard_map/ppermute | solution.py:436
  36.7 19.0 %collective-permute-start.6 = (bf16[2,256,256]{2,1,0:T(8,128)(2,1)S(1)}, bf16[2,256,256]{2,1,0:T(8,128)(2,1)S(1)}, u32[]{:S(2)}, u32[]{:S(2)}) collective-permute-start(bf16[2,256,256]{2,1,0:T(8,128)(2,1)S(1)} %get-tuple-element.76), channel_id=1, source_target_pairs={{16,0},{8,24},{17,1},{9,25},{18,2},{10,26},{19,3},{11,27},{20,4},{... | collective-permute-start | bytes 786440 | tf_op jit(solution)/shard_map/ppermute | solution.py:436
  38.0 20.5 %collective-permute-start.7 = (bf16[2,256,256]{2,1,0:T(8,128)(2,1)S(1)}, bf16[2,256,256]{2,1,0:T(8,128)(2,1)S(1)}, u32[]{:S(2)}, u32[]{:S(2)}) collective-permute-start(bf16[2,256,256]{2,1,0:T(8,128)(2,1)S(1)} %get-tuple-element.77), channel_id=1, source_target_pairs={{8,0},{16,24},{9,1},{17,25},{10,2},{18,26},{11,3},{19,27},{12,4},{... | collective-permute-start | bytes 786440 | tf_op jit(solution)/shard_map/ppermute | solution.py:436
  39.3 1.1 copy-start.1
  40.4 1.1 copy-start.3
  45.8 12.8 %copy-start.2 = (bf16[384,1024]{1,0:T(8,128)(2,1)S(1)}, bf16[384,1024]{1,0:T(8,128)(2,1)}, u32[]{:S(2)}) copy-start(bf16[384,1024]{1,0:T(8,128)(2,1)} %get-tuple-element.58.query_ref) | copy-start | bytes 2359300
  61.8 11.2 %copy-start.4 = (bf16[384,1024]{1,0:T(8,128)(2,1)S(1)}, bf16[384,1024]{1,0:T(8,128)(2,1)}, u32[]{:S(2)}) copy-start(bf16[384,1024]{1,0:T(8,128)(2,1)} %get-tuple-element.63.pair_ref) | copy-start | bytes 2359300
  61.8 4.0 %collective-permute-start.9 = (bf16[384,512]{1,0:T(8,128)(2,1)S(1)}, bf16[384,512]{1,0:T(8,128)(2,1)S(1)}, u32[]{:S(2)}, u32[]{:S(2)}) collective-permute-start(bf16[384,512]{1,0:T(8,128)(2,1)S(1)} %get-tuple-element.83.refs_2_), channel_id=1, source_target_pairs={{0,4},{4,0},{1,5},{5,1},{2,6},{6,2},{3,7},{7,3},{8,12},{12,8},{9,1... | collective-permute-start | bytes 1179656 | tf_op jit(solution)/shard_map/ppermute | solution.py:439
  61.8 7.0 %collective-permute-start.8 = (f32[32,384]{1,0:T(8,128)S(1)}, f32[32,384]{1,0:T(8,128)S(1)}, u32[]{:S(2)}, u32[]{:S(2)}) collective-permute-start(f32[32,384]{1,0:T(8,128)S(1)} %get-tuple-element.81.note_ref), channel_id=1, source_target_pairs={{8,0},{16,8},{24,16},{9,1},{17,9},{25,17},{10,2},{18,10},{26,18},{... | collective-permute-start | bytes 147464 | tf_op jit(solution)/shard_map/ppermute | solution.py:426
  63.3 7.8 %collective-permute-start.11 = (f32[32,384]{1,0:T(8,128)S(1)}, f32[32,384]{1,0:T(8,128)S(1)}, u32[]{:S(2)}, u32[]{:S(2)}) collective-permute-start(f32[32,384]{1,0:T(8,128)S(1)} %get-tuple-element.81.note_ref), channel_id=1, source_target_pairs={{24,0},{25,1},{26,2},{27,3},{28,4},{29,5},{30,6},{31,7}} | collective-permute-start | bytes 147464 | tf_op jit(solution)/shard_map/ppermute | solution.py:426
  64.6 8.5 %collective-permute-start.10 = (f32[32,384]{1,0:T(8,128)S(1)}, f32[32,384]{1,0:T(8,128)S(1)}, u32[]{:S(2)}, u32[]{:S(2)}) collective-permute-start(f32[32,384]{1,0:T(8,128)S(1)} %get-tuple-element.81.note_ref), channel_id=1, source_target_pairs={{16,0},{24,8},{17,1},{25,9},{18,2},{26,10},{19,3},{27,11},{20,4},{... | collective-permute-start | bytes 147464 | tf_op jit(solution)/shard_map/ppermute | solution.py:426
  77.3 2.4 %collective-permute-start.12 = (bf16[384,512]{1,0:T(8,128)(2,1)S(1)}, bf16[384,512]{1,0:T(8,128)(2,1)S(1)}, u32[]{:S(2)}, u32[]{:S(2)}) collective-permute-start(bf16[384,512]{1,0:T(8,128)(2,1)S(1)} %get-tuple-element.89.refs_2_), channel_id=1, source_target_pairs={{0,4},{4,0},{1,5},{5,1},{2,6},{6,2},{3,7},{7,3},{8,12},{12,8},{9,1... | collective-permute-start | bytes 1179656 | tf_op jit(solution)/shard_map/ppermute | solution.py:439
  77.4 20.1 %collective-permute-start.16 = (bf16[2,384,512]{2,1,0:T(8,128)(2,1)S(1)}, bf16[2,384,512]{2,1,0:T(8,128)(2,1)S(1)}, u32[]{:S(2)}, u32[]{:S(2)}) collective-permute-start(bf16[2,384,512]{2,1,0:T(8,128)(2,1)S(1)} %get-tuple-element.95), channel_id=1, source_target_pairs={{0,8},{24,16},{1,9},{25,17},{2,10},{26,18},{3,11},{27,19},{4,12},{... | collective-permute-start | bytes 2359304 | tf_op jit(solution)/shard_map/ppermute | solution.py:548
  82.7 1.9 %collective-permute-start.13 = (bf16[384,512]{1,0:T(8,128)(2,1)S(1)}, bf16[384,512]{1,0:T(8,128)(2,1)S(1)}, u32[]{:S(2)}, u32[]{:S(2)}) collective-permute-start(bf16[384,512]{1,0:T(8,128)(2,1)S(1)} %get-tuple-element.91.refs_2_), channel_id=1, source_target_pairs={{0,4},{4,0},{1,5},{5,1},{2,6},{6,2},{3,7},{7,3},{8,12},{12,8},{9,1... | collective-permute-start | bytes 1179656 | tf_op jit(solution)/shard_map/ppermute | solution.py:439
  82.9 31.4 %collective-permute-start.15 = (bf16[2,384,512]{2,1,0:T(8,128)(2,1)S(1)}, bf16[2,384,512]{2,1,0:T(8,128)(2,1)S(1)}, u32[]{:S(2)}, u32[]{:S(2)}) collective-permute-start(bf16[2,384,512]{2,1,0:T(8,128)(2,1)S(1)} %get-tuple-element.93), channel_id=1, source_target_pairs={{0,8},{24,16},{1,9},{25,17},{2,10},{26,18},{3,11},{27,19},{4,12},{... | collective-permute-start | bytes 2359304 | tf_op jit(solution)/shard_map/ppermute | solution.py:548
  98.3 10.3 %collective-permute-start.17 = (bf16[384,512]{1,0:T(8,128)(2,1)S(1)}, bf16[384,512]{1,0:T(8,128)(2,1)S(1)}, u32[]{:S(2)}, u32[]{:S(2)}) collective-permute-start(bf16[384,512]{1,0:T(8,128)(2,1)S(1)} %get-tuple-element.98), channel_id=1, source_target_pairs={{8,16},{16,8},{9,17},{17,9},{10,18},{18,10},{11,19},{19,11},{12,20... | collective-permute-start | bytes 1179656 | tf_op jit(solution)/shard_map/ppermute | solution.py:436
  98.9 9.6 %collective-permute-start.18 = (bf16[384,512]{1,0:T(8,128)(2,1)S(1)}, bf16[384,512]{1,0:T(8,128)(2,1)S(1)}, u32[]{:S(2)}, u32[]{:S(2)}) collective-permute-start(bf16[384,512]{1,0:T(8,128)(2,1)S(1)} %get-tuple-element.99), channel_id=1, source_target_pairs={{8,16},{16,8},{9,17},{17,9},{10,18},{18,10},{11,19},{19,11},{12,20... | collective-permute-start | bytes 1179656 | tf_op jit(solution)/shard_map/ppermute | solution.py:436
  99.6 31.6 %collective-permute-start.14 = (bf16[2,384,512]{2,1,0:T(8,128)(2,1)S(1)}, bf16[2,384,512]{2,1,0:T(8,128)(2,1)S(1)}, u32[]{:S(2)}, u32[]{:S(2)}) collective-permute-start(bf16[2,384,512]{2,1,0:T(8,128)(2,1)S(1)} %get-tuple-element.92), channel_id=1, source_target_pairs={{0,8},{24,16},{1,9},{25,17},{2,10},{26,18},{3,11},{27,19},{4,12},{... | collective-permute-start | bytes 2359304 | tf_op jit(solution)/shard_map/ppermute | solution.py:548
  115.1 16.1 %collective-permute-start.19 = (bf16[384,512]{1,0:T(8,128)(2,1)S(1)}, bf16[384,512]{1,0:T(8,128)(2,1)S(1)}, u32[]{:S(2)}, u32[]{:S(2)}) collective-permute-start(bf16[384,512]{1,0:T(8,128)(2,1)S(1)} %get-tuple-element.102), channel_id=1, source_target_pairs={{8,16},{16,8},{9,17},{17,9},{10,18},{18,10},{11,19},{19,11},{12,20... | collective-permute-start | bytes 1179656 | tf_op jit(solution)/shard_map/ppermute | solution.py:436
  115.8 15.4 %collective-permute-start.20 = (bf16[384,512]{1,0:T(8,128)(2,1)S(1)}, bf16[384,512]{1,0:T(8,128)(2,1)S(1)}, u32[]{:S(2)}, u32[]{:S(2)}) collective-permute-start(bf16[384,512]{1,0:T(8,128)(2,1)S(1)} %get-tuple-element.103), channel_id=1, source_target_pairs={{8,16},{16,8},{9,17},{17,9},{10,18},{18,10},{11,19},{19,11},{12,20... | collective-permute-start | bytes 1179656 | tf_op jit(solution)/shard_map/ppermute | solution.py:436
  117.1 29.3 %collective-permute-start.22 = (bf16[384,512]{1,0:T(8,128)(2,1)S(1)}, bf16[384,512]{1,0:T(8,128)(2,1)S(1)}, u32[]{:S(2)}, u32[]{:S(2)}) collective-permute-start(bf16[384,512]{1,0:T(8,128)(2,1)S(1)} %shard_map.89), channel_id=1, source_target_pairs={{0,8},{8,0},{16,24},{24,16},{1,9},{9,1},{17,25},{25,17},{2,10},{10... | collective-permute-start | bytes 1179656 | tf_op jit(solution)/shard_map/ppermute | solution.py:436
  132.0 14.5 %collective-permute-start.21 = (bf16[384,512]{1,0:T(8,128)(2,1)S(1)}, bf16[384,512]{1,0:T(8,128)(2,1)S(1)}, u32[]{:S(2)}, u32[]{:S(2)}) collective-permute-start(bf16[384,512]{1,0:T(8,128)(2,1)S(1)} %get-tuple-element.106), channel_id=1, source_target_pairs={{8,16},{16,8},{9,17},{17,9},{10,18},{18,10},{11,19},{19,11},{12,20... | collective-permute-start | bytes 1179656 | tf_op jit(solution)/shard_map/ppermute | solution.py:436
  133.3 25.5 %collective-permute-start.25 = (bf16[384,512]{1,0:T(8,128)(2,1)S(1)}, bf16[384,512]{1,0:T(8,128)(2,1)S(1)}, u32[]{:S(2)}, u32[]{:S(2)}) collective-permute-start(bf16[384,512]{1,0:T(8,128)(2,1)S(1)} %shard_map.91), channel_id=1, source_target_pairs={{0,8},{8,0},{16,24},{24,16},{1,9},{9,1},{17,25},{25,17},{2,10},{10... | collective-permute-start | bytes 1179656 | tf_op jit(solution)/shard_map/ppermute | solution.py:436
  145.8 14.6 %collective-permute-start.24 = (bf16[384,512]{1,0:T(8,128)(2,1)S(1)}, bf16[384,512]{1,0:T(8,128)(2,1)S(1)}, u32[]{:S(2)}, u32[]{:S(2)}) collective-permute-start(bf16[384,512]{1,0:T(8,128)(2,1)S(1)} %get-tuple-element.109), channel_id=1, source_target_pairs={{8,16},{16,8},{9,17},{17,9},{10,18},{18,10},{11,19},{19,11},{12,20... | collective-permute-start | bytes 1179656 | tf_op jit(solution)/shard_map/ppermute | solution.py:436
  147.1 15.9 %collective-permute-start.23 = (bf16[384,512]{1,0:T(8,128)(2,1)S(1)}, bf16[384,512]{1,0:T(8,128)(2,1)S(1)}, u32[]{:S(2)}, u32[]{:S(2)}) collective-permute-start(bf16[384,512]{1,0:T(8,128)(2,1)S(1)} %shard_map.90), channel_id=1, source_target_pairs={{0,8},{8,0},{16,24},{24,16},{1,9},{9,1},{17,25},{25,17},{2,10},{10... | collective-permute-start | bytes 1179656 | tf_op jit(solution)/shard_map/ppermute | solution.py:436

commit v4 on v3

--- a/solution.py
+++ b/solution.py
@@ -8,7 +8,7 @@
 from jax.experimental.pallas import tpu as pltpu
 from jax.sharding import PartitionSpec as P
 
-VMEM_LIMIT = 48 * 1024 * 1024
+VMEM_LIMIT = 32 * 1024 * 1024
 SEQ, EVEN, CORE, PLACE = range(4)
 
 
@@ -267,10 +267,10 @@
 
 
 def key_value_kernel(
-    routes, notes, info_ref, pair_ref, query_ref, note_ref, query_next_ref, mix_ref, *refs
+    routes, notes, orders, info_ref, pair_ref, query_ref, note_ref, query_next_ref, mix_ref, *refs
 ):
     note_refs, grad_key_ref, grad_value_ref = refs[:notes], refs[-2], refs[-1]
-    note_next_ref = note_refs[0]
+    stats_next = note_refs[0][:8]
     seg_len, head_dim = pair_ref.shape[0], pair_ref.shape[1] // 2
     key, value = pair_ref[:, :head_dim], pair_ref[:, head_dim:]
     scale = head_dim ** (-0.5)
@@ -293,12 +293,12 @@
         return part(ref[:, :head_dim], ref[:, head_dim:], stats, causal)
 
     own_key, own_value = both(query_ref, note_ref[:8], True)
-    next_key, next_value = both(query_next_ref, note_next_ref[:8], False)
+    next_key, next_value = both(query_next_ref, stats_next, False)
     key_float = key.astype(jnp.float32)
-    grad_memory = total_from(info_ref, refs[notes:-2], routes, True).astype(jnp.bfloat16)
+    grad_memory = total_from(info_ref, refs[notes : len(refs) - 2 - orders], routes, True).astype(jnp.bfloat16)
     phi_high, phi_low = halves(feature(key_float))
     from_memory = dot_nt(value, grad_memory)
-    norm = note_next_ref[8:9, :head_dim]
+    norm = note_refs[0][8:9, :head_dim]
     for ref in note_refs[1:]:
         norm = norm + ref[8:9, :head_dim]
     from_memory = (from_memory + norm) * feature_slope(key_float)
@@ -335,21 +335,22 @@
         first_ref[place] = total
 
 
-def inner_kernel(arrived_ref, far_ref, near_ref, far_out_ref, near_out_ref):
-    for at, (ref, out_ref) in enumerate(((far_ref, far_out_ref), (near_ref, near_out_ref))):
+def inner_kernel(arrived_ref, far_ref, near_ref, *out_refs):
+    for at, ref in enumerate((far_ref, near_ref)):
         total = arrived_ref[at].astype(jnp.float32) + ref[0].astype(jnp.float32)
-        out_ref[...] = total.astype(jnp.bfloat16)
-
-
-def outer_kernel(info_ref, arrived_ref, terms_ref, out_ref):
+        out_ref = out_refs[at] if len(out_refs) > 1 else out_refs[0]
+        out_ref[at if len(out_refs) == 1 else 0] = total.astype(jnp.bfloat16)
+
+
+def outer_kernel(info_ref, arrived_ref, terms_ref, *refs):
     term = terms_ref[0].astype(jnp.float32)
-    total = term + arrived_ref[...].astype(jnp.float32)
-    out_ref[...] = total.astype(jnp.bfloat16)
+    total = term + arrived_ref[0].astype(jnp.float32)
+    refs[-1][...] = total.astype(jnp.bfloat16)
 
 
 def finish_kernel(scale, info_ref, even_ref, odd_ref, terms_ref, *refs):
     out_ref = refs[-1]
-    total = even_ref[...].astype(jnp.float32) + odd_ref[...].astype(jnp.float32)
+    total = even_ref[...].astype(jnp.float32) + odd_ref[0].astype(jnp.float32)
     out_ref[0] = (total + terms_ref[0].astype(jnp.float32)) * scale
 
 
@@ -382,6 +383,8 @@
     def spec(kind):
         if kind == "f":
             return SMEM_SPEC
+        if kind == "x":
+            return HBM_SPEC
         if kind == "m":
             return pl.BlockSpec(blocks[kind], lambda h: (h, 0, 0))
         if kind in "sn":
@@ -434,6 +437,9 @@
                 if seq_count - 1 - (i + distance) >= lowest:
                     pairs.append((i + distance, i))
         return lax.ppermute(x, "seq", pairs) if pairs else None
+
+    def nudge(x):
+        return from_core(x.reshape(-1, x.shape[-1])[:16, :128], 1)
 
     def from_core(x, step):
         return lax.ppermute(x, "dp", [(i, (i + step) % dp_count) for i in range(dp_count)])
@@ -456,7 +462,7 @@
             pltpu.VMEM((seg_len, columns), bf16),
             pltpu.SemaphoreType.DMA((4 * pieces + 1,)),
         ],
-        **limits(62 * 1024 * 1024),
+        **limits(48 * 1024 * 1024),
     )(info, tokens, w_key, w_value, w_query, cot)
     even_arrived = swapped(even_message, 1, 0)
     odd_arrived = swapped(odd_message, 1, 1)
@@ -506,8 +512,10 @@
     )(info, query, row_prev, far, mix, local_out, grad_att, stats, memory, *arrived)
     notes = [shifted(note, -step) for step in range(1, seq_count)]
 
-    def row_blocks(grad):
-        grads = [grad] + [from_core(grad, step) for step in range(1, dp_count)]
+    def of_cores(grad):
+        return [grad] + [from_core(grad, step) for step in range(1, dp_count)]
+
+    def row_blocks(grads):
         return pl.pallas_call(
             row_blocks_kernel,
             grid=(seq_count,),
@@ -529,6 +537,7 @@
     block = (part_rows, columns)
     part_shape = jax.ShapeDtypeStruct(block, bf16)
     whole = pl.BlockSpec(block, lambda i, info: (0, 0))
+    first = pl.BlockSpec((1,) + block, lambda i, info: (0, 0, 0))
 
     def on_terms(kernel, ins, outs, out_shape, **more):
         return pl.pallas_call(
@@ -547,56 +556,57 @@
         last = seq_count - 1
         return lax.ppermute(first, "seq", [(0, 1), (last, last - 1)])
 
-    def inner_messages(terms, arrived):
+    def inner_messages(terms, arrived, arrays, *order):
         def inner(info_ref, *refs):
-            inner_kernel(*refs)
-
+            inner_kernel(*refs[:3], *refs[-arrays:])
+
+        size = (2 // arrays,) + block
         return on_terms(
             inner,
             [
                 pl.BlockSpec((2,) + block, lambda i, info: (0, 0, 0)),
                 at_block(lambda z: jnp.where(z < 2, 3, 0)),
                 at_block(lambda z: jnp.where(z < 2, 2, 1)),
-            ],
-            [whole, whole],
-            [part_shape] * 2,
-        )(info, arrived, terms, terms)
-
-    def over_middle(terms, arrived):
-        return [swapped(message, 1, 1) for message in inner_messages(terms, arrived)]
-
-    def end_message(terms, far):
+            ]
+            + [HBM_SPEC] * len(order),
+            [pl.BlockSpec(size, lambda i, info: (0, 0, 0))] * arrays,
+            [jax.ShapeDtypeStruct(size, bf16)] * arrays,
+        )(info, arrived, terms, terms, *order)
+
+    def end_message(terms, far, *order):
         return on_terms(
             outer_kernel,
-            [whole, at_block(lambda z: lax.bitwise_xor(z, 1))],
+            [first, at_block(lambda z: lax.bitwise_xor(z, 1))] + [HBM_SPEC] * len(order),
             whole,
             part_shape,
-        )(info, far, terms)
-
-    def to_ends(terms, far):
-        return swapped(end_message(terms, far), 1, 0)
+        )(info, far, terms, *order)
 
     def finish(terms, even, odd, which, into=()):
+        last = odd.shape[0] - 1
+        odd_block = pl.BlockSpec((1,) + block, lambda i, info: (last, 0, 0))
         return on_terms(
             functools.partial(finish_kernel, grad_scale),
-            [whole, whole, at_block(lambda z: z)] + [HBM_SPEC] * len(into),
+            [whole, odd_block, at_block(lambda z: z)] + [HBM_SPEC] * len(into),
             pl.BlockSpec((1,) + block, lambda i, info: (which, 0, 0)),
             jax.ShapeDtypeStruct((3,) + block, f32),
             input_output_aliases={4: 0} if into else {},
         )(info, even, odd, terms, *into)
 
     if by_swaps:
-        query_terms, query_first = row_blocks(grad_query)
+        query_terms, query_first = row_blocks(of_cores(grad_query))
         notes[0], query_terms, query_first = lax.optimization_barrier(
             (notes[0], query_terms, query_first)
         )
         query_ends = swapped_ends(query_first)
+        order = [nudge(query_first)]
+    else:
+        order = []
     grad_key, grad_value = call(
-        functools.partial(key_value_kernel, routes, len(notes)),
+        functools.partial(key_value_kernel, routes, len(notes), len(order)),
         sizes,
-        "fppnpr" + "n" * len(notes) + over + "m",
+        "fppnpr" + "n" * len(notes) + over + "m" + "x" * len(order),
         (("c", bf16), ("c", bf16)),
-    )(info, pair, query, note, query_next, mix, *notes, grad_memory, *arrived)
+    )(info, pair, query, note, query_next, mix, *notes, grad_memory, *arrived, *order)
     if not by_swaps:
         contract = (((0,), (0,)), ((), ()))
 
@@ -636,25 +646,27 @@
         rows = summed(jnp.concatenate([grad_query, grad_key, grad_value], 1)) * grad_scale
         return (blended[None], rows.reshape(part_rows, 3, columns))
 
-    value_terms, value_first = row_blocks(grad_value)
+    values, keys = lax.optimization_barrier((of_cores(grad_value), of_cores(grad_key)))
+    value_terms, value_first = row_blocks(values)
     value_ends = swapped_ends(value_first)
-    grad_key, value_terms = lax.optimization_barrier((grad_key, value_terms))
-    key_terms, key_first = row_blocks(grad_key)
+    keys, value_terms = lax.optimization_barrier((keys, value_terms))
+    key_terms, key_first = row_blocks(keys)
     key_ends = swapped_ends(key_first)
-    key_terms, query_ends = lax.optimization_barrier((key_terms, query_ends))
-    query_far, query_near = over_middle(query_terms, query_ends)
-    value_ends, query_far, query_near = lax.optimization_barrier(
-        (value_ends, query_far, query_near)
-    )
-    query_even = to_ends(query_terms, query_far)
-    value_far, value_near = over_middle(value_terms, value_ends)
-    key_ends, value_far, value_near = lax.optimization_barrier((key_ends, value_far, value_near))
-    value_even = to_ends(value_terms, value_far)
-    key_far, key_near = over_middle(key_terms, key_ends)
-    key_far, query_even = lax.optimization_barrier((key_far, query_even))
-    key_even = to_ends(key_terms, key_far)
-    grad_weights = finish(query_terms, query_even, query_near, 0)
-    grad_weights = finish(value_terms, value_even, value_near, 2, (grad_weights,))
+
+    (message,) = inner_messages(query_terms, query_ends, 1, key_terms)
+    query_odd = swapped(message, 1, 1)
+    (message,) = inner_messages(value_terms, value_ends, 1, message)
+    value_odd = swapped(message, 1, 1)
+    message = end_message(query_terms, query_odd, message)
+    query_even = swapped(message, 1, 0)
+    messages = inner_messages(key_terms, key_ends, 2, message)
+    key_far, key_near = [swapped(message, 1, 1) for message in messages]
+    message = end_message(value_terms, value_odd, query_even, *messages)
+    value_even = swapped(message, 1, 0)
+    message = end_message(key_terms, key_far, message)
+    key_even = swapped(message, 1, 0)
+    grad_weights = finish(query_terms, query_even, query_odd, 0)
+    grad_weights = finish(value_terms, value_even, value_odd, 2, (grad_weights,))
     grad_weights = finish(key_terms, key_even, key_near, 1, (grad_weights,))
     return (blended[None], jnp.transpose(grad_weights, (1, 0, 2)))
 

time: 165 us -> 160 us (0.970)
  starting transfers between devices: 69 us -> 45.5 us
  waiting for transfers between devices: 46.6 us -> 69.8 us
  Pallas kernels: 44.1 us -> 40.3 us
    ppermute x14 -> x12, starting transfers between devices: 44.9 us -> 23.5 us  [swapped(): return lax.ppermute(x, 'seq', pairs) if pairs else None]
    ppermute x14 -> x12, waiting for transfers between devices: 13.4 us -> 27.4 us  [swapped(): return lax.ppermute(x, 'seq', pairs) if pairs else None]
    ppermute x3, waiting for transfers between devices: 18.4 us -> 28.2 us  [swapped_ends(): return lax.ppermute(first, 'seq', [(0, 1), (last, last - 1)])]
    ppermute x3, starting transfers between devices: 12.9 us -> 9.52 us  [swapped_ends(): return lax.ppermute(first, 'seq', [(0, 1), (last, last - 1)])]
    pallas_call x1, Pallas kernels: 10.3 us -> 7.75 us  [local(): pl.pallas_call(functools.partial(project_kernel, heads), in_specs=[SMEM_S...]
  transfers between devices with their start and end apart: 26 -> 25, of which waited for: 10 -> 13; matrix products, arithmetic and copies ran while one was open for 1% -> 0% of each run, Pallas kernels for 21% -> 20%
where the time goes in v4:
time: 160 us
  waiting for transfers between devices  69.8 us (44%)
  starting transfers between devices  45.5 us (28%)
  Pallas kernels  40.3 us (25%)
  local copies, waits for them, and re-layouts  2.83 us (2%)
    ppermute x3, waiting for transfers between devices, swapped_ends(): return lax.ppermute(first, 'seq', [(0, 1), (last, last - 1)])  28.2 us
    ppermute x12, waiting for transfers between devices, swapped(): return lax.ppermute(x, 'seq', pairs) if pairs else None  27.4 us
    ppermute x12, starting transfers between devices, swapped(): return lax.ppermute(x, 'seq', pairs) if pairs else None  23.5 us
    ppermute x5, waiting for transfers between devices, shifted(): return lax.ppermute(x, 'seq', pairs)  13.9 us
    ppermute x5, starting transfers between devices, shifted(): return lax.ppermute(x, 'seq', pairs)  10.9 us
    ppermute x3, starting transfers between devices, swapped_ends(): return lax.ppermute(first, 'seq', [(0, 1), (last, last - 1)])  9.52 us
    pallas_call x3, Pallas kernels, row_blocks(): pl.pallas_call(row_blocks_kernel, grid=(seq_count,), in_specs=[SMEM_SPEC]...  8.72 us
    pallas_call x1, Pallas kernels, local(): pl.pallas_call(functools.partial(project_kernel, heads), in_specs=[SMEM_S...  7.75 us
  transfers between devices with their start and end apart: 25, of which 13 were waited for; matrix products, arithmetic and copies ran while one was open for 0% of the time, Pallas kernels for 20%

profile of v4, /device:TPU:0, one launch (start us, length us, event | category | flops | bytes accessed | tf_op | source)
XLA Modules:
  0.0 159.7 jit_solution(5495035381435264597)
XLA Ops:
  0.6 0.5 collective-permute-start.4
  1.1 0.1 pad_add_fusion.info_ref
  1.2 1.7 %copy-done = bf16[1,384,3072]{2,1,0:T(8,128)(2,1)S(1)} copy-done((bf16[1,384,3072]{2,1,0:T(8,128)(2,1)S(1)}, bf16[1,384,3072]{2,1,0:T(8,128)(2,1)}, u32[]{:S(2)}) %copy-start) | copy-done | bytes 2359320
  2.9 1.0 copy-done.1
  3.9 7.8 %shard_map.77 = (bf16[384,1024]{1,0:T(8,128)(2,1)S(1)}, bf16[384,1024]{1,0:T(8,128)(2,1)S(1)}, bf16[384,1024]{1,0:T(8,128)(2,1)S(1)}, bf16[384,1024]{1,0:T(8,128)(2,1)S(1)}, f32[1,1024]{1,0:T(1,128)S(1)}) custom-call(s32[4]{0:T(128)S(1)} %pad_add_fusion.info_ref, bf16[384,3072]{1,0:T(8,128)(2,1)S(1)} %bitcast.14, bf16[3072,512]{1,0:T(8,128)(2,1)} %w_key_ref.1, ...), custom_call_target="tpu_custom_call" | custom-call | tf_op jit(solution)/shard_map/pallas_call | solution.py:454
  11.7 2.7 %collective-permute-start = (bf16[384,1024]{1,0:T(8,128)(2,1)S(1)}, bf16[384,1024]{1,0:T(8,128)(2,1)S(1)}, u32[]{:S(2)}, u32[]{:S(2)}) collective-permute-start(bf16[384,1024]{1,0:T(8,128)(2,1)S(1)} %get-tuple-element.50), channel_id=1, source_target_pairs={{0,8},{8,0},{16,24},{24,16},{1,9},{9,1},{17,25},{25,17},{2,10},{10... | collective-permute-start | bytes 2359304 | tf_op jit(solution)/shard_map/ppermute | solution.py:439
  14.4 0.7 collective-permute-start.1
  15.1 5.7 %collective-permute-start.2 = (f32[1,1024]{1,0:T(1,128)S(1)}, f32[1,1024]{1,0:T(1,128)S(1)}, u32[]{:S(2)}, u32[]{:S(2)}) collective-permute-start(f32[1,1024]{1,0:T(1,128)S(1)} %get-tuple-element.52.row_ref), channel_id=1, source_target_pairs={{0,16},{8,24},{1,17},{9,25},{2,18},{10,26},{3,19},{11,27},{4,20},{... | collective-permute-start | bytes 12296 | tf_op jit(solution)/shard_map/ppermute | solution.py:429
  20.8 1.3 collective-permute-start.3
  22.1 0.1 broadcast_bitcast_fusion
  22.2 0.1 pad.7.clone
  22.3 9.7 %collective-permute-done.2 = f32[1,1024]{1,0:T(1,128)S(1)} collective-permute-done((f32[1,1024]{1,0:T(1,128)S(1)}, f32[1,1024]{1,0:T(1,128)S(1)}, u32[]{:S(2)}, u32[]{:S(2)}) %collective-permute-start.2) | collective-permute-done | bytes 4128 | tf_op jit(solution)/shard_map/ppermute | solution.py:429
  32.0 0.0 collective-permute-done.3
  32.0 0.1 fusion.1
  32.1 0.5 collective-permute-done.even_ref
  32.6 0.0 collective-permute-done.1.odd_ref
  32.6 2.1 %shard_map.78 = (bf16[384,1024]{1,0:T(8,128)(2,1)S(1)}, bf16[384,1024]{1,0:T(8,128)(2,1)S(1)}, bf16[2,256,256]{2,1,0:T(8,128)(2,1)S(1)}, bf16[2,256,256]{2,1,0:T...) custom-call(s32[4]{0:T(128)S(1)} %pad_add_fusion.info_ref, ...), custom_call_target="tpu_custom_call" | custom-call | tf_op jit(solution)/shard_map/pallas_call | solution.py:486
  34.7 0.7 collective-permute-start.5
  35.4 1.3 collective-permute-start.6
  36.7 1.3 collective-permute-start.7
  38.0 4.2 %shard_map.79 = (f32[384,512]{1,0:T(8,128)S(1)}, f32[384,512]{1,0:T(8,128)S(1)}, f32[16,384]{1,0:T(8,128)S(1)}) custom-call(s32[4]{0:T(128)S(1)} %pad_add_fusion.info_ref, bf16[384,1024]{1,0:T(8,128)(2,1)S(1)} %get-tuple-element.49.query_ref, bf16[384,1024]{1,0:T(8,128)(2,1)S(1)} %get-tuple-element.54.pair_ref, ...), custom_call_target="tpu_custom_call" | custom-call | tf_op jit(solution)/shard_map/pallas_call | solution.py:493
  42.2 0.0 collective-permute-done.4.refs_1_
  42.2 1.2 shard_map.80
  43.4 11.0 %collective-permute-done.6.refs_2_.refs_5_ = bf16[2,256,256]{2,1,0:T(8,128)(2,1)S(1)} collective-permute-done((bf16[2,256,256]{2,1,0:T(8,128)(2,1)S(1)}, bf16[2,256,256]{2,1,0:T(8,128)(2,1)S(1)}, u32[]{:S(2)}, u32[]{:S(2)}) %collective-permute-start.6) | collective-permute-done | bytes 262176 | tf_op jit(solution)/shard_map/ppermute | solution.py:439
  54.4 2.8 %collective-permute-done.7.refs_3_.refs_6_ = bf16[2,256,256]{2,1,0:T(8,128)(2,1)S(1)} collective-permute-done((bf16[2,256,256]{2,1,0:T(8,128)(2,1)S(1)}, bf16[2,256,256]{2,1,0:T(8,128)(2,1)S(1)}, u32[]{:S(2)}, u32[]{:S(2)}) %collective-permute-start.7) | collective-permute-done | bytes 262176 | tf_op jit(solution)/shard_map/ppermute | solution.py:439
  57.2 3.3 %shard_map.81 = (bf16[384,512]{1,0:T(8,128)(2,1)}, bf16[384,512]{1,0:T(8,128)(2,1)S(1)}, f32[32,384]{1,0:T(8,128)S(1)}) custom-call(s32[4]{0:T(128)S(1)} %pad_add_fusion.info_ref, bf16[384,1024]{1,0:T(8,128)(2,1)S(1)} %get-tuple-element.49.query_ref, f32[1,1024]{1,0:T(1,128)S(1)} %get-tuple-element.53.row_prev_ref, f32[8,1024]{1,0:T(8,128)S(1)} %get-tuple-element.96.far_ref, ...), custom_call_target="tpu_custom_call" | custom-call | tf_op jit(solution)/shard_map/pallas_call | solution.py:507
  60.5 1.3 collective-permute-start.8
  61.8 1.3 collective-permute-start.10
  63.1 1.3 collective-permute-start.11
  64.4 2.9 %shard_map.82 = (bf16[4,384,512]{2,1,0:T(8,128)(2,1)S(1)}, bf16[2,384,512]{2,1,0:T(8,128)(2,1)S(1)}) custom-call(s32[4]{0:T(128)S(1)} %pad_add_fusion.info_ref, bf16[1536,384]{1,0:T(8,128)(2,1)S(1)} %get-tuple-element.70.refs_0_, bf16[1536,384]{1,0:T(8,128)(2,1)S(1)} %get-tuple-element.71.refs_1_, bf16[384,512]{1,0:T(8,128)(2,1)S(1)} %get-tuple-element.74.refs_2_, ...), custom_call_target="tpu_custom_call" | custom-call | tf_op jit(solution)/shard_map/pallas_call | solution.py:519
  67.4 0.6 collective-permute-start.12
  68.0 0.8 collective-permute-done.10.refs_1_
  68.8 3.3 %collective-permute-done.11.refs_2_ = f32[32,384]{1,0:T(8,128)S(1)} collective-permute-done((f32[32,384]{1,0:T(8,128)S(1)}, f32[32,384]{1,0:T(8,128)S(1)}, u32[]{:S(2)}, u32[]{:S(2)}) %collective-permute-start.11) | collective-permute-done | bytes 49184 | tf_op jit(solution)/shard_map/ppermute | solution.py:429
  72.1 4.2 %shard_map.83 = (bf16[384,512]{1,0:T(8,128)(2,1)S(1)}, bf16[384,512]{1,0:T(8,128)(2,1)S(1)}) custom-call(s32[4]{0:T(128)S(1)} %pad_add_fusion.info_ref, bf16[384,1024]{1,0:T(8,128)(2,1)S(1)} %get-tuple-element.54.pair_ref, bf16[384,1024]{1,0:T(8,128)(2,1)S(1)} %get-tuple-element.49.query_ref, f32[32,384]{1,0:T(8,128)S(1)} %get-tuple-element.72.note_ref, ...), custom_call_target="tpu_custom_call" | custom-call | tf_op jit(solution)/shard_map/pallas_call | solution.py:604
  76.3 0.1 collective-permute-start.13
  76.4 0.5 collective-permute-start.14
  76.9 1.3 collective-permute-start.16
  78.2 0.4 collective-permute-done.14.refs_3_
  78.7 2.9 %shard_map.84 = (bf16[4,384,512]{2,1,0:T(8,128)(2,1)S(1)}, bf16[2,384,512]{2,1,0:T(8,128)(2,1)S(1)}) custom-call(s32[4]{0:T(128)S(1)} %pad_add_fusion.info_ref, bf16[1536,384]{1,0:T(8,128)(2,1)S(1)} %get-tuple-element.70.refs_0_, bf16[1536,384]{1,0:T(8,128)(2,1)S(1)} %get-tuple-element.71.refs_1_, bf16[384,512]{1,0:T(8,128)(2,1)S(1)} %get-tuple-element.84.refs_2_, ...), custom_call_target="tpu_custom_call" | custom-call | tf_op jit(solution)/shard_map/pallas_call | solution.py:519
  81.6 1.3 collective-permute-start.18
  82.9 2.9 %shard_map.85 = (bf16[4,384,512]{2,1,0:T(8,128)(2,1)S(1)}, bf16[2,384,512]{2,1,0:T(8,128)(2,1)S(1)}) custom-call(s32[4]{0:T(128)S(1)} %pad_add_fusion.info_ref, bf16[1536,384]{1,0:T(8,128)(2,1)S(1)} %get-tuple-element.70.refs_0_, bf16[1536,384]{1,0:T(8,128)(2,1)S(1)} %get-tuple-element.71.refs_1_, bf16[384,512]{1,0:T(8,128)(2,1)S(1)} %get-tuple-element.87.refs_2_, ...), custom_call_target="tpu_custom_call" | custom-call | tf_op jit(solution)/shard_map/pallas_call | solution.py:519
  85.8 10.2 %collective-permute-done.16.refs_0_ = bf16[2,384,512]{2,1,0:T(8,128)(2,1)S(1)} collective-permute-done((bf16[2,384,512]{2,1,0:T(8,128)(2,1)S(1)}, bf16[2,384,512]{2,1,0:T(8,128)(2,1)S(1)}, u32[]{:S(2)}, u32[]{:S(2)}) %collective-permute-start.16) | collective-permute-done | bytes 786464 | tf_op jit(solution)/shard_map/ppermute | solution.py:557
  96.0 0.7 shard_map.86.refs_3_
  96.8 0.7 collective-permute-start.17
  97.5 6.9 %collective-permute-start.15 = (bf16[2,384,512]{2,1,0:T(8,128)(2,1)S(1)}, bf16[2,384,512]{2,1,0:T(8,128)(2,1)S(1)}, u32[]{:S(2)}, u32[]{:S(2)}) collective-permute-start(bf16[2,384,512]{2,1,0:T(8,128)(2,1)S(1)} %get-tuple-element.89), channel_id=1, source_target_pairs={{0,8},{24,16},{1,9},{25,17},{2,10},{26,18},{3,11},{27,19},{4,12},{... | collective-permute-start | bytes 2359304 | tf_op jit(solution)/shard_map/ppermute | solution.py:557
  104.4 8.5 %collective-permute-done.18.refs_0_ = bf16[2,384,512]{2,1,0:T(8,128)(2,1)S(1)} collective-permute-done((bf16[2,384,512]{2,1,0:T(8,128)(2,1)S(1)}, bf16[2,384,512]{2,1,0:T(8,128)(2,1)S(1)}, u32[]{:S(2)}, u32[]{:S(2)}) %collective-permute-start.18) | collective-permute-done | bytes 786464 | tf_op jit(solution)/shard_map/ppermute | solution.py:557
  112.9 0.7 shard_map.87.refs_0_
  113.6 0.7 collective-permute-start.20
  114.4 0.6 shard_map.88.refs_3_
  115.0 5.3 %collective-permute-start.21 = (bf16[384,512]{1,0:T(8,128)(2,1)S(1)}, bf16[384,512]{1,0:T(8,128)(2,1)S(1)}, u32[]{:S(2)}, u32[]{:S(2)}) collective-permute-start(bf16[384,512]{1,0:T(8,128)(2,1)S(1)} %shard_map.88.refs_3_), channel_id=1, source_target_pairs={{0,8},{8,0},{16,24},{24,16},{1,9},{9,1},{17,25},{25,17},{2,10},{10... | collective-permute-start | bytes 1179656 | tf_op jit(solution)/shard_map/ppermute | solution.py:439
  120.3 9.4 %collective-permute-done.15.refs_0_ = bf16[2,384,512]{2,1,0:T(8,128)(2,1)S(1)} collective-permute-done((bf16[2,384,512]{2,1,0:T(8,128)(2,1)S(1)}, bf16[2,384,512]{2,1,0:T(8,128)(2,1)S(1)}, u32[]{:S(2)}, u32[]{:S(2)}) %collective-permute-start.15) | collective-permute-done | bytes 786464 | tf_op jit(solution)/shard_map/ppermute | solution.py:557
  129.8 0.7 shard_map.89
  130.5 0.7 collective-permute-start.19
  131.2 0.7 collective-permute-start.23
  131.9 5.8 %collective-permute-done.21.refs_0_.even_ref = bf16[384,512]{1,0:T(8,128)(2,1)S(1)} collective-permute-done((bf16[384,512]{1,0:T(8,128)(2,1)S(1)}, bf16[384,512]{1,0:T(8,128)(2,1)S(1)}, u32[]{:S(2)}, u32[]{:S(2)}) %collective-permute-start.21) | collective-permute-done | bytes 393248 | tf_op jit(solution)/shard_map/ppermute | solution.py:439
  137.6 0.6 shard_map.90.refs_0_
  138.3 2.5 %collective-permute-start.24 = (bf16[384,512]{1,0:T(8,128)(2,1)S(1)}, bf16[384,512]{1,0:T(8,128)(2,1)S(1)}, u32[]{:S(2)}, u32[]{:S(2)}) collective-permute-start(bf16[384,512]{1,0:T(8,128)(2,1)S(1)} %shard_map.90.refs_0_), channel_id=1, source_target_pairs={{0,8},{8,0},{16,24},{24,16},{1,9},{9,1},{17,25},{25,17},{2,10},{10... | collective-permute-start | bytes 1179656 | tf_op jit(solution)/shard_map/ppermute | solution.py:439
  140.8 0.6 shard_map.91
  141.5 6.2 %collective-permute-start.22 = (bf16[384,512]{1,0:T(8,128)(2,1)S(1)}, bf16[384,512]{1,0:T(8,128)(2,1)S(1)}, u32[]{:S(2)}, u32[]{:S(2)}) collective-permute-start(bf16[384,512]{1,0:T(8,128)(2,1)S(1)} %shard_map.91), channel_id=1, source_target_pairs={{0,8},{8,0},{16,24},{24,16},{1,9},{9,1},{17,25},{25,17},{2,10},{10... | collective-permute-start | bytes 1179656 | tf_op jit(solution)/shard_map/ppermute | solution.py:439
  147.6 1.6 shard_map.92.refs_0_
  149.2 1.6 %collective-permute-done.24.even_ref = bf16[384,512]{1,0:T(8,128)(2,1)S(1)} collective-permute-done((bf16[384,512]{1,0:T(8,128)(2,1)S(1)}, bf16[384,512]{1,0:T(8,128)(2,1)S(1)}, u32[]{:S(2)}, u32[]{:S(2)}) %collective-permute-start.24) | collective-permute-done | bytes 393248 | tf_op jit(solution)/shard_map/ppermute | solution.py:439
  150.8 1.6 shard_map.93.refs_0_
  152.4 5.7 %collective-permute-done.22.even_ref = bf16[384,512]{1,0:T(8,128)(2,1)S(1)} collective-permute-done((bf16[384,512]{1,0:T(8,128)(2,1)S(1)}, bf16[384,512]{1,0:T(8,128)(2,1)S(1)}, u32[]{:S(2)}, u32[]{:S(2)}) %collective-permute-start.22) | collective-permute-done | bytes 393248 | tf_op jit(solution)/shard_map/ppermute | solution.py:439
  158.1 1.6 shard_map.94
  (19 shorter events, 0.1 us)
Async XLA Ops:
  0.6 41.6 %collective-permute-start.4 = (bf16[384,3072]{1,0:T(8,128)(2,1)}, bf16[384,3072]{1,0:T(8,128)(2,1)S(1)}, u32[]{:S(2)}, u32[]{:S(2)}) collective-permute-start(bf16[384,3072]{1,0:T(8,128)(2,1)} %bitcast.13), channel_id=1, source_target_pairs={{0,4},{4,0},{1,5},{5,1},{2,6},{6,2},{3,7},{7,3},{8,12},{12,8},{9,1... | collective-permute-start | bytes 7077896 | tf_op jit(solution)/shard_map/ppermute | solution.py:445
  1.2 1.7 %copy-start = (bf16[1,384,3072]{2,1,0:T(8,128)(2,1)S(1)}, bf16[1,384,3072]{2,1,0:T(8,128)(2,1)}, u32[]{:S(2)}) copy-start(bf16[1,384,3072]{2,1,0:T(8,128)(2,1)} %param.6) | copy-start | bytes 7077892
  2.9 1.0 copy-start.1
  3.9 18.2 %copy-start.2 = (f32[2]{0:T(128)S(1)}, f32[2]{0:T(128)}, u32[]{:S(2)}) copy-start(f32[2]{0:T(128)} %param.10) | copy-start | bytes 28
  11.7 20.9 %collective-permute-start = (bf16[384,1024]{1,0:T(8,128)(2,1)S(1)}, bf16[384,1024]{1,0:T(8,128)(2,1)S(1)}, u32[]{:S(2)}, u32[]{:S(2)}) collective-permute-start(bf16[384,1024]{1,0:T(8,128)(2,1)S(1)} %get-tuple-element.50), channel_id=1, source_target_pairs={{0,8},{8,0},{16,24},{24,16},{1,9},{9,1},{17,25},{25,17},{2,10},{10... | collective-permute-start | bytes 2359304 | tf_op jit(solution)/shard_map/ppermute | solution.py:439
  14.4 18.2 %collective-permute-start.1 = (bf16[384,1024]{1,0:T(8,128)(2,1)S(1)}, bf16[384,1024]{1,0:T(8,128)(2,1)S(1)}, u32[]{:S(2)}, u32[]{:S(2)}) collective-permute-start(bf16[384,1024]{1,0:T(8,128)(2,1)S(1)} %get-tuple-element.51), channel_id=1, source_target_pairs={{8,16},{16,8},{9,17},{17,9},{10,18},{18,10},{11,19},{19,11},{12,20... | collective-permute-start | bytes 2359304 | tf_op jit(solution)/shard_map/ppermute | solution.py:439
  15.1 16.9 %collective-permute-start.2 = (f32[1,1024]{1,0:T(1,128)S(1)}, f32[1,1024]{1,0:T(1,128)S(1)}, u32[]{:S(2)}, u32[]{:S(2)}) collective-permute-start(f32[1,1024]{1,0:T(1,128)S(1)} %get-tuple-element.52.row_ref), channel_id=1, source_target_pairs={{0,16},{8,24},{1,17},{9,25},{2,18},{10,26},{3,19},{11,27},{4,20},{... | collective-permute-start | bytes 12296 | tf_op jit(solution)/shard_map/ppermute | solution.py:429
  20.8 11.2 %collective-permute-start.3 = (f32[1,1024]{1,0:T(1,128)S(1)}, f32[1,1024]{1,0:T(1,128)S(1)}, u32[]{:S(2)}, u32[]{:S(2)}) collective-permute-start(f32[1,1024]{1,0:T(1,128)S(1)} %get-tuple-element.52.row_ref), channel_id=1, source_target_pairs={{0,24},{1,25},{2,26},{3,27},{4,28},{5,29},{6,30},{7,31}} | collective-permute-start | bytes 12296 | tf_op jit(solution)/shard_map/ppermute | solution.py:429
  34.7 8.7 %collective-permute-start.5 = (bf16[2,256,256]{2,1,0:T(8,128)(2,1)S(1)}, bf16[2,256,256]{2,1,0:T(8,128)(2,1)S(1)}, u32[]{:S(2)}, u32[]{:S(2)}) collective-permute-start(bf16[2,256,256]{2,1,0:T(8,128)(2,1)S(1)} %get-tuple-element.66), channel_id=1, source_target_pairs={{8,16},{16,8},{9,17},{17,9},{10,18},{18,10},{11,19},{19,11},{12,20... | collective-permute-start | bytes 786440 | tf_op jit(solution)/shard_map/ppermute | solution.py:439
  35.4 19.0 %collective-permute-start.6 = (bf16[2,256,256]{2,1,0:T(8,128)(2,1)S(1)}, bf16[2,256,256]{2,1,0:T(8,128)(2,1)S(1)}, u32[]{:S(2)}, u32[]{:S(2)}) collective-permute-start(bf16[2,256,256]{2,1,0:T(8,128)(2,1)S(1)} %get-tuple-element.67), channel_id=1, source_target_pairs={{16,0},{8,24},{17,1},{9,25},{18,2},{10,26},{19,3},{11,27},{20,4},{... | collective-permute-start | bytes 786440 | tf_op jit(solution)/shard_map/ppermute | solution.py:439
  36.7 20.6 %collective-permute-start.7 = (bf16[2,256,256]{2,1,0:T(8,128)(2,1)S(1)}, bf16[2,256,256]{2,1,0:T(8,128)(2,1)S(1)}, u32[]{:S(2)}, u32[]{:S(2)}) collective-permute-start(bf16[2,256,256]{2,1,0:T(8,128)(2,1)S(1)} %get-tuple-element.68), channel_id=1, source_target_pairs={{8,0},{16,24},{9,1},{17,25},{10,2},{18,26},{11,3},{19,27},{12,4},{... | collective-permute-start | bytes 786440 | tf_op jit(solution)/shard_map/ppermute | solution.py:439
  60.5 3.9 %collective-permute-start.9 = (bf16[384,512]{1,0:T(8,128)(2,1)S(1)}, bf16[384,512]{1,0:T(8,128)(2,1)S(1)}, u32[]{:S(2)}, u32[]{:S(2)}) collective-permute-start(bf16[384,512]{1,0:T(8,128)(2,1)S(1)} %get-tuple-element.74.refs_2_), channel_id=1, source_target_pairs={{0,4},{4,0},{1,5},{5,1},{2,6},{6,2},{3,7},{7,3},{8,12},{12,8},{9,1... | collective-permute-start | bytes 1179656 | tf_op jit(solution)/shard_map/ppermute | solution.py:445
  60.5 6.8 %collective-permute-start.8 = (f32[32,384]{1,0:T(8,128)S(1)}, f32[32,384]{1,0:T(8,128)S(1)}, u32[]{:S(2)}, u32[]{:S(2)}) collective-permute-start(f32[32,384]{1,0:T(8,128)S(1)} %get-tuple-element.72.note_ref), channel_id=1, source_target_pairs={{8,0},{16,8},{24,16},{9,1},{17,9},{25,17},{10,2},{18,10},{26,18},{... | collective-permute-start | bytes 147464 | tf_op jit(solution)/shard_map/ppermute | solution.py:429
  61.8 6.9 %collective-permute-start.10 = (f32[32,384]{1,0:T(8,128)S(1)}, f32[32,384]{1,0:T(8,128)S(1)}, u32[]{:S(2)}, u32[]{:S(2)}) collective-permute-start(f32[32,384]{1,0:T(8,128)S(1)} %get-tuple-element.72.note_ref), channel_id=1, source_target_pairs={{16,0},{24,8},{17,1},{25,9},{18,2},{26,10},{19,3},{27,11},{20,4},{... | collective-permute-start | bytes 147464 | tf_op jit(solution)/shard_map/ppermute | solution.py:429
  63.1 9.0 %collective-permute-start.11 = (f32[32,384]{1,0:T(8,128)S(1)}, f32[32,384]{1,0:T(8,128)S(1)}, u32[]{:S(2)}, u32[]{:S(2)}) collective-permute-start(f32[32,384]{1,0:T(8,128)S(1)} %get-tuple-element.72.note_ref), channel_id=1, source_target_pairs={{24,0},{25,1},{26,2},{27,3},{28,4},{29,5},{30,6},{31,7}} | collective-permute-start | bytes 147464 | tf_op jit(solution)/shard_map/ppermute | solution.py:429
  67.4 4.7 %collective-permute-start.12 = (bf16[16,128]{1,0:T(8,128)(2,1)S(1)}, bf16[16,128]{1,0:T(8,128)(2,1)S(1)}, u32[]{:S(2)}, u32[]{:S(2)}) collective-permute-start(bf16[16,128]{1,0:T(8,128)(2,1)S(1)} %slice.4), channel_id=1, source_target_pairs={{0,4},{4,0},{1,5},{5,1},{2,6},{6,2},{3,7},{7,3},{8,12},{12,8},{9,1... | collective-permute-start | bytes 12296 | tf_op jit(solution)/shard_map/ppermute | solution.py:445
  76.3 1.9 %collective-permute-start.13 = (bf16[384,512]{1,0:T(8,128)(2,1)S(1)}, bf16[384,512]{1,0:T(8,128)(2,1)S(1)}, u32[]{:S(2)}, u32[]{:S(2)}) collective-permute-start(bf16[384,512]{1,0:T(8,128)(2,1)S(1)} %get-tuple-element.84.refs_2_), channel_id=1, source_target_pairs={{0,4},{4,0},{1,5},{5,1},{2,6},{6,2},{3,7},{7,3},{8,12},{12,8},{9,1... | collective-permute-start | bytes 1179656 | tf_op jit(solution)/shard_map/ppermute | solution.py:445
  76.4 2.3 %collective-permute-start.14 = (bf16[384,512]{1,0:T(8,128)(2,1)S(1)}, bf16[384,512]{1,0:T(8,128)(2,1)S(1)}, u32[]{:S(2)}, u32[]{:S(2)}) collective-permute-start(bf16[384,512]{1,0:T(8,128)(2,1)S(1)} %get-tuple-element.87.refs_2_), channel_id=1, source_target_pairs={{0,4},{4,0},{1,5},{5,1},{2,6},{6,2},{3,7},{7,3},{8,12},{12,8},{9,1... | collective-permute-start | bytes 1179656 | tf_op jit(solution)/shard_map/ppermute | solution.py:445
  76.9 19.1 %collective-permute-start.16 = (bf16[2,384,512]{2,1,0:T(8,128)(2,1)S(1)}, bf16[2,384,512]{2,1,0:T(8,128)(2,1)S(1)}, u32[]{:S(2)}, u32[]{:S(2)}) collective-permute-start(bf16[2,384,512]{2,1,0:T(8,128)(2,1)S(1)} %get-tuple-element.79), channel_id=1, source_target_pairs={{0,8},{24,16},{1,9},{25,17},{2,10},{26,18},{3,11},{27,19},{4,12},{... | collective-permute-start | bytes 2359304 | tf_op jit(solution)/shard_map/ppermute | solution.py:557
  81.6 31.3 %collective-permute-start.18 = (bf16[2,384,512]{2,1,0:T(8,128)(2,1)S(1)}, bf16[2,384,512]{2,1,0:T(8,128)(2,1)S(1)}, u32[]{:S(2)}, u32[]{:S(2)}) collective-permute-start(bf16[2,384,512]{2,1,0:T(8,128)(2,1)S(1)} %get-tuple-element.92), channel_id=1, source_target_pairs={{0,8},{24,16},{1,9},{25,17},{2,10},{26,18},{3,11},{27,19},{4,12},{... | collective-permute-start | bytes 2359304 | tf_op jit(solution)/shard_map/ppermute | solution.py:557
  96.8 17.6 %collective-permute-start.17 = (bf16[2,384,512]{2,1,0:T(8,128)(2,1)S(1)}, bf16[2,384,512]{2,1,0:T(8,128)(2,1)S(1)}, u32[]{:S(2)}, u32[]{:S(2)}) collective-permute-start(bf16[2,384,512]{2,1,0:T(8,128)(2,1)S(1)} %shard_map.86.refs_3_), channel_id=1, source_target_pairs={{8,16},{16,8},{9,17},{17,9},{10,18},{18,10},{11,19},{19,11},{12,20... | collective-permute-start | bytes 2359304 | tf_op jit(solution)/shard_map/ppermute | solution.py:439
  97.5 32.3 %collective-permute-start.15 = (bf16[2,384,512]{2,1,0:T(8,128)(2,1)S(1)}, bf16[2,384,512]{2,1,0:T(8,128)(2,1)S(1)}, u32[]{:S(2)}, u32[]{:S(2)}) collective-permute-start(bf16[2,384,512]{2,1,0:T(8,128)(2,1)S(1)} %get-tuple-element.89), channel_id=1, source_target_pairs={{0,8},{24,16},{1,9},{25,17},{2,10},{26,18},{3,11},{27,19},{4,12},{... | collective-permute-start | bytes 2359304 | tf_op jit(solution)/shard_map/ppermute | solution.py:557
  113.6 24.0 %collective-permute-start.20 = (bf16[2,384,512]{2,1,0:T(8,128)(2,1)S(1)}, bf16[2,384,512]{2,1,0:T(8,128)(2,1)S(1)}, u32[]{:S(2)}, u32[]{:S(2)}) collective-permute-start(bf16[2,384,512]{2,1,0:T(8,128)(2,1)S(1)} %shard_map.87.refs_0_), channel_id=1, source_target_pairs={{8,16},{16,8},{9,17},{17,9},{10,18},{18,10},{11,19},{19,11},{12,20... | collective-permute-start | bytes 2359304 | tf_op jit(solution)/shard_map/ppermute | solution.py:439
  115.0 22.6 %collective-permute-start.21 = (bf16[384,512]{1,0:T(8,128)(2,1)S(1)}, bf16[384,512]{1,0:T(8,128)(2,1)S(1)}, u32[]{:S(2)}, u32[]{:S(2)}) collective-permute-start(bf16[384,512]{1,0:T(8,128)(2,1)S(1)} %shard_map.88.refs_3_), channel_id=1, source_target_pairs={{0,8},{8,0},{16,24},{24,16},{1,9},{9,1},{17,25},{25,17},{2,10},{10... | collective-permute-start | bytes 1179656 | tf_op jit(solution)/shard_map/ppermute | solution.py:439
  130.5 10.3 %collective-permute-start.19 = (bf16[1,384,512]{2,1,0:T(8,128)(2,1)S(1)}, bf16[1,384,512]{2,1,0:T(8,128)(2,1)S(1)}, u32[]{:S(2)}, u32[]{:S(2)}) collective-permute-start(bf16[1,384,512]{2,1,0:T(8,128)(2,1)S(1)} %get-tuple-element.94.refs_1_), channel_id=1, source_target_pairs={{8,16},{16,8},{9,17},{17,9},{10,18},{18,10},{11,19},{19,11},{12,20... | collective-permute-start | bytes 1179656 | tf_op jit(solution)/shard_map/ppermute | solution.py:439
  131.2 21.2 %collective-permute-start.23 = (bf16[1,384,512]{2,1,0:T(8,128)(2,1)S(1)}, bf16[1,384,512]{2,1,0:T(8,128)(2,1)S(1)}, u32[]{:S(2)}, u32[]{:S(2)}) collective-permute-start(bf16[1,384,512]{2,1,0:T(8,128)(2,1)S(1)} %get-tuple-element.95.refs_2_), channel_id=1, source_target_pairs={{8,16},{16,8},{9,17},{17,9},{10,18},{18,10},{11,19},{19,11},{12,20... | collective-permute-start | bytes 1179656 | tf_op jit(solution)/shard_map/ppermute | solution.py:439
  138.3 12.5 %collective-permute-start.24 = (bf16[384,512]{1,0:T(8,128)(2,1)S(1)}, bf16[384,512]{1,0:T(8,128)(2,1)S(1)}, u32[]{:S(2)}, u32[]{:S(2)}) collective-permute-start(bf16[384,512]{1,0:T(8,128)(2,1)S(1)} %shard_map.90.refs_0_), channel_id=1, source_target_pairs={{0,8},{8,0},{16,24},{24,16},{1,9},{9,1},{17,25},{25,17},{2,10},{10... | collective-permute-start | bytes 1179656 | tf_op jit(solution)/shard_map/ppermute | solution.py:439
  141.5 16.6 %collective-permute-start.22 = (bf16[384,512]{1,0:T(8,128)(2,1)S(1)}, bf16[384,512]{1,0:T(8,128)(2,1)S(1)}, u32[]{:S(2)}, u32[]{:S(2)}) collective-permute-start(bf16[384,512]{1,0:T(8,128)(2,1)S(1)} %shard_map.91), channel_id=1, source_target_pairs={{0,8},{8,0},{16,24},{24,16},{1,9},{9,1},{17,25},{25,17},{2,10},{10... | collective-permute-start | bytes 1179656 | tf_op jit(solution)/shard_map/ppermute | solution.py:439

commit v5 on v4

--- a/solution.py
+++ b/solution.py
@@ -72,15 +72,20 @@
             weight_copy(which, piece).start()
 
     def product(which):
-        total = None
         for piece in range(pieces):
             if which == 0:
                 token_copy(piece).wait()
             weight_copy(which, piece).wait()
-            at = slice(piece * depth, (piece + 1) * depth)
-            term = dot_nn(tokens[:, at], weights[which, piece])
-            total = term if total is None else total + term
-        return total.astype(jnp.bfloat16)
+        parts = []
+        half = weights.shape[3] // 2
+        for columns in (slice(0, half), slice(half, 2 * half)):
+            total = None
+            for piece in range(pieces):
+                at = slice(piece * depth, (piece + 1) * depth)
+                term = dot_nn(tokens[:, at], weights[which, piece, :, columns])
+                total = term if total is None else total + term
+            parts.append(total.astype(jnp.bfloat16))
+        return jnp.concatenate(parts, 1)
 
     return product
 
@@ -267,7 +272,7 @@
 
 
 def key_value_kernel(
-    routes, notes, orders, info_ref, pair_ref, query_ref, note_ref, query_next_ref, mix_ref, *refs
+    routes, notes, info_ref, pair_ref, query_ref, note_ref, query_next_ref, mix_ref, *refs
 ):
     note_refs, grad_key_ref, grad_value_ref = refs[:notes], refs[-2], refs[-1]
     stats_next = note_refs[0][:8]
@@ -295,7 +300,7 @@
     own_key, own_value = both(query_ref, note_ref[:8], True)
     next_key, next_value = both(query_next_ref, stats_next, False)
     key_float = key.astype(jnp.float32)
-    grad_memory = total_from(info_ref, refs[notes : len(refs) - 2 - orders], routes, True).astype(jnp.bfloat16)
+    grad_memory = total_from(info_ref, refs[notes:-2], routes, True).astype(jnp.bfloat16)
     phi_high, phi_low = halves(feature(key_float))
     from_memory = dot_nt(value, grad_memory)
     norm = note_refs[0][8:9, :head_dim]
@@ -321,18 +326,19 @@
 def row_blocks_kernel(info_ref, *refs):
     *refs, out_ref, first_ref = refs
     count = len(refs) // 2
-    total = dot_nn(refs[0][...], refs[count][...])
-    for rows, grad in zip(refs[1:count], refs[count + 1 :]):
-        total = total + dot_nn(rows[...], grad[...])
-    total = total.astype(jnp.bfloat16)
-    out_ref[0] = total
-    block = pl.program_id(0)
-    last = pl.num_programs(0) - 1
-    place = jnp.where(info_ref[SEQ] == 0, last - block, block)
-
-    @pl.when(place < 2)
-    def _():
-        first_ref[place] = total
+    blocks, part_rows = out_ref.shape[:2]
+    for block in range(blocks):
+        rows = slice(block * part_rows, (block + 1) * part_rows)
+        total = dot_nn(refs[0][rows], refs[count][...])
+        for columns, grad in zip(refs[1:count], refs[count + 1 :]):
+            total = total + dot_nn(columns[rows], grad[...])
+        total = total.astype(jnp.bfloat16)
+        out_ref[block] = total
+        place = jnp.where(info_ref[SEQ] == 0, blocks - 1 - block, block)
+
+        @pl.when(place < 2)
+        def _(place=place, total=total):
+            first_ref[place] = total
 
 
 def inner_kernel(arrived_ref, far_ref, near_ref, *out_refs):
@@ -380,28 +386,29 @@
         "n": (16, max(seg_len, head_dim)),
     }
 
-    def spec(kind):
-        if kind == "f":
-            return SMEM_SPEC
-        if kind == "x":
-            return HBM_SPEC
-        if kind == "m":
-            return pl.BlockSpec(blocks[kind], lambda h: (h, 0, 0))
-        if kind in "sn":
-            return pl.BlockSpec(blocks[kind], lambda h: (h, 0))
-        return pl.BlockSpec(blocks[kind], lambda h: (0, h))
-
     def shape(kind):
         block = blocks[kind]
         if kind in "msn":
             return (heads * block[0],) + block[1:]
         return (block[0], heads * block[1])
 
+    def of_head(kind, ref, head):
+        if kind == "f":
+            return ref
+        block = blocks[kind]
+        if kind in "msn":
+            return ref.at[pl.ds(head * block[0], block[0])]
+        return ref.at[:, pl.ds(head * block[1], block[1])]
+
+    def all_heads(*refs):
+        kinds = list(ins) + [kind for kind, _ in outs]
+        for head in range(heads):
+            kernel(*[of_head(kind, ref, head) for kind, ref in zip(kinds, refs)])
+
     return pl.pallas_call(
-        kernel,
-        grid=(heads,),
-        in_specs=[spec(kind) for kind in ins],
-        out_specs=[spec(kind) for kind, _ in outs],
+        all_heads,
+        in_specs=[SMEM_SPEC if kind == "f" else VMEM_SPEC for kind in ins],
+        out_specs=[VMEM_SPEC] * len(outs),
         out_shape=[jax.ShapeDtypeStruct(shape(kind), dtype) for kind, dtype in outs],
         **limits(),
     )
@@ -437,9 +444,6 @@
                 if seq_count - 1 - (i + distance) >= lowest:
                     pairs.append((i + distance, i))
         return lax.ppermute(x, "seq", pairs) if pairs else None
-
-    def nudge(x):
-        return from_core(x.reshape(-1, x.shape[-1])[:16, :128], 1)
 
     def from_core(x, step):
         return lax.ppermute(x, "dp", [(i, (i + step) % dp_count) for i in range(dp_count)])
@@ -467,6 +471,7 @@
     even_arrived = swapped(even_message, 1, 0)
     odd_arrived = swapped(odd_message, 1, 1)
     far_rows = [shifted(row, step) for step in range(2, seq_count)]
+    odd_arrived, far_rows = lax.optimization_barrier((odd_arrived, far_rows))
     free = jnp.zeros_like(row)
     pad = jnp.zeros((count - seq_count + 1, 2 * columns), f32)
     near = jnp.concatenate([free] + far_rows[:-1] + [free, pad], 0)
@@ -518,14 +523,8 @@
     def row_blocks(grads):
         return pl.pallas_call(
             row_blocks_kernel,
-            grid=(seq_count,),
-            in_specs=[SMEM_SPEC]
-            + [pl.BlockSpec((part_rows, seg_len), lambda b: (b, 0))] * dp_count
-            + [pl.BlockSpec((seg_len, columns), lambda b: (0, 0))] * dp_count,
-            out_specs=[
-                pl.BlockSpec((1, part_rows, columns), lambda b: (b, 0, 0)),
-                pl.BlockSpec((2, part_rows, columns), lambda b: (0, 0, 0)),
-            ],
+            in_specs=[SMEM_SPEC] + [VMEM_SPEC] * (2 * dp_count),
+            out_specs=[VMEM_SPEC] * 2,
             out_shape=[
                 jax.ShapeDtypeStruct((seq_count, part_rows, columns), bf16),
                 jax.ShapeDtypeStruct((2, part_rows, columns), bf16),
@@ -598,15 +597,12 @@
             (notes[0], query_terms, query_first)
         )
         query_ends = swapped_ends(query_first)
-        order = [nudge(query_first)]
-    else:
-        order = []
     grad_key, grad_value = call(
-        functools.partial(key_value_kernel, routes, len(notes), len(order)),
+        functools.partial(key_value_kernel, routes, len(notes)),
         sizes,
-        "fppnpr" + "n" * len(notes) + over + "m" + "x" * len(order),
+        "fppnpr" + "n" * len(notes) + over + "m",
         (("c", bf16), ("c", bf16)),
-    )(info, pair, query, note, query_next, mix, *notes, grad_memory, *arrived, *order)
+    )(info, pair, query, note, query_next, mix, *notes, grad_memory, *arrived)
     if not by_swaps:
         contract = (((0,), (0,)), ((), ()))
 

time: 160 us -> 158 us (0.988)
  Pallas kernels: 40.3 us -> 37.7 us
  waiting for transfers between devices: 69.8 us -> 71.8 us
    ppermute x5, waiting for transfers between devices: 13.9 us -> 17.2 us  [shifted(): return lax.ppermute(x, 'seq', pairs)]
    ppermute x12, starting transfers between devices: 23.5 us -> 26.2 us  [swapped(): return lax.ppermute(x, 'seq', pairs) if pairs else None]
    ppermute x12, waiting for transfers between devices: 27.4 us -> 24.8 us  [swapped(): return lax.ppermute(x, 'seq', pairs) if pairs else None]
    ppermute x5, starting transfers between devices: 10.9 us -> 8.46 us  [shifted(): return lax.ppermute(x, 'seq', pairs)]
  transfers between devices with their start and end apart: 25 -> 24, of which waited for: 13 -> 13; matrix products, arithmetic and copies ran while one was open for 0% -> 0% of each run, Pallas kernels for 20% -> 19%
where the time goes in v5:
time: 158 us
  waiting for transfers between devices  71.8 us (45%)
  starting transfers between devices  44.2 us (28%)
  Pallas kernels  37.7 us (24%)
  local copies, waits for them, and re-layouts  2.82 us (2%)
    ppermute x3, waiting for transfers between devices, swapped_ends(): return lax.ppermute(first, 'seq', [(0, 1), (last, last - 1)])  29.4 us
    ppermute x12, starting transfers between devices, swapped(): return lax.ppermute(x, 'seq', pairs) if pairs else None  26.2 us
    ppermute x12, waiting for transfers between devices, swapped(): return lax.ppermute(x, 'seq', pairs) if pairs else None  24.8 us
    ppermute x5, waiting for transfers between devices, shifted(): return lax.ppermute(x, 'seq', pairs)  17.2 us
    pallas_call x3, Pallas kernels, row_blocks(): pl.pallas_call(row_blocks_kernel, in_specs=[SMEM_SPEC] + [VMEM_SPEC] * (2...  8.72 us
    ppermute x5, starting transfers between devices, shifted(): return lax.ppermute(x, 'seq', pairs)  8.46 us
    ppermute x3, starting transfers between devices, swapped_ends(): return lax.ppermute(first, 'seq', [(0, 1), (last, last - 1)])  8.43 us
    pallas_call x1, Pallas kernels, local(): pl.pallas_call(functools.partial(project_kernel, heads), in_specs=[SMEM_S...  7.39 us
  transfers between devices with their start and end apart: 24, of which 13 were waited for; matrix products, arithmetic and copies ran while one was open for 0% of the time, Pallas kernels for 19%

profile of v5, /device:TPU:0, one launch (start us, length us, event | category | flops | bytes accessed | tf_op | source)
XLA Modules:
  0.0 157.6 jit_solution(3867925579624051514)
XLA Ops:
  0.6 0.5 collective-permute-start.4
  1.1 0.1 pad_add_fusion.info_ref.refs_0_
  1.2 1.7 %copy-done = bf16[1,384,3072]{2,1,0:T(8,128)(2,1)S(1)} copy-done((bf16[1,384,3072]{2,1,0:T(8,128)(2,1)S(1)}, bf16[1,384,3072]{2,1,0:T(8,128)(2,1)}, u32[]{:S(2)}) %copy-start) | copy-done | bytes 2359320
  2.9 1.0 copy-done.1
  3.9 7.4 %shard_map.77 = (bf16[384,1024]{1,0:T(8,128)(2,1)S(1)}, bf16[384,1024]{1,0:T(8,128)(2,1)S(1)}, bf16[384,1024]{1,0:T(8,128)(2,1)S(1)}, bf16[384,1024]{1,0:T(8,128)(2,1)S(1)}, f32[1,1024]{1,0:T(1,128)S(1)}) custom-call(s32[4]{0:T(128)S(1)} %pad_add_fusion.info_ref.refs_0_, bf16[384,3072]{1,0:T(8,128)(2,1)S(1)} %bitcast.13, bf16[3072,512]{1,0:T(8,128)(2,1)} %w_key_ref.1, ...), custom_call_target="tpu_custom_call" | custom-call | tf_op jit(solution)/shard_map/pallas_call | solution.py:458
  11.3 0.7 collective-permute-start.1
  12.0 5.4 %collective-permute-start = (bf16[384,1024]{1,0:T(8,128)(2,1)S(1)}, bf16[384,1024]{1,0:T(8,128)(2,1)S(1)}, u32[]{:S(2)}, u32[]{:S(2)}) collective-permute-start(bf16[384,1024]{1,0:T(8,128)(2,1)S(1)} %get-tuple-element.53), channel_id=1, source_target_pairs={{0,8},{8,0},{16,24},{24,16},{1,9},{9,1},{17,25},{25,17},{2,10},{10... | collective-permute-start | bytes 2359304 | tf_op jit(solution)/shard_map/ppermute | solution.py:446
  17.4 1.9 %collective-permute-start.2 = (f32[1,1024]{1,0:T(1,128)S(1)}, f32[1,1024]{1,0:T(1,128)S(1)}, u32[]{:S(2)}, u32[]{:S(2)}) collective-permute-start(f32[1,1024]{1,0:T(1,128)S(1)} %get-tuple-element.55.refs_4_), channel_id=1, source_target_pairs={{0,16},{8,24},{1,17},{9,25},{2,18},{10,26},{3,19},{11,27},{4,20},{... | collective-permute-start | bytes 12296 | tf_op jit(solution)/shard_map/ppermute | solution.py:436
  19.3 2.7 %collective-permute-start.3 = (f32[1,1024]{1,0:T(1,128)S(1)}, f32[1,1024]{1,0:T(1,128)S(1)}, u32[]{:S(2)}, u32[]{:S(2)}) collective-permute-start(f32[1,1024]{1,0:T(1,128)S(1)} %get-tuple-element.55.refs_4_), channel_id=1, source_target_pairs={{0,24},{1,25},{2,26},{3,27},{4,28},{5,29},{6,30},{7,31}} | collective-permute-start | bytes 12296 | tf_op jit(solution)/shard_map/ppermute | solution.py:436
  22.1 0.1 broadcast_bitcast_fusion
  22.2 0.1 pad.7.clone
  22.2 12.5 %collective-permute-done.2 = f32[1,1024]{1,0:T(1,128)S(1)} collective-permute-done((f32[1,1024]{1,0:T(1,128)S(1)}, f32[1,1024]{1,0:T(1,128)S(1)}, u32[]{:S(2)}, u32[]{:S(2)}) %collective-permute-start.2) | collective-permute-done | bytes 4128 | tf_op jit(solution)/shard_map/ppermute | solution.py:436
  34.7 0.0 collective-permute-done.3
  34.8 0.0 collective-permute-done.1.refs_2_
  34.8 0.1 fusion.1
  34.9 0.5 collective-permute-done.refs_1_
  35.4 1.8 %shard_map.78 = (bf16[384,1024]{1,0:T(8,128)(2,1)S(1)}, bf16[384,1024]{1,0:T(8,128)(2,1)S(1)}, bf16[2,256,256]{2,1,0:T(8,128)(2,1)S(1)}, bf16[2,256,256]{2,1,0:T...) custom-call(s32[4]{0:T(128)S(1)} %pad_add_fusion.info_ref.refs_0_, ...), custom_call_target="tpu_custom_call" | custom-call | tf_op jit(solution)/shard_map/pallas_call | solution.py:491
  37.1 0.7 collective-permute-start.5
  37.8 1.3 collective-permute-start.6
  39.1 1.3 collective-permute-start.7
  40.4 3.4 %shard_map.79 = (f32[384,512]{1,0:T(8,128)S(1)}, f32[384,512]{1,0:T(8,128)S(1)}, f32[16,384]{1,0:T(8,128)S(1)}) custom-call(s32[4]{0:T(128)S(1)} %pad_add_fusion.info_ref.refs_0_, bf16[384,1024]{1,0:T(8,128)(2,1)S(1)} %get-tuple-element.52.refs_1_.refs_2_, bf16[384,1024]{1,0:T(8,128)(2,1)S(1)} %get-tuple-element.60.refs_2_.refs_1_, ...), custom_call_target="tpu_custom_call" | custom-call | tf_op jit(solution)/shard_map/pallas_call | solution.py:498
  43.8 1.2 shard_map.80
  45.0 8.5 %collective-permute-done.6.refs_10_.refs_11_ = bf16[2,256,256]{2,1,0:T(8,128)(2,1)S(1)} collective-permute-done((bf16[2,256,256]{2,1,0:T(8,128)(2,1)S(1)}, bf16[2,256,256]{2,1,0:T(8,128)(2,1)S(1)}, u32[]{:S(2)}, u32[]{:S(2)}) %collective-permute-start.6) | collective-permute-done | bytes 262176 | tf_op jit(solution)/shard_map/ppermute | solution.py:446
  53.5 2.8 %collective-permute-done.7.refs_11_.refs_12_ = bf16[2,256,256]{2,1,0:T(8,128)(2,1)S(1)} collective-permute-done((bf16[2,256,256]{2,1,0:T(8,128)(2,1)S(1)}, bf16[2,256,256]{2,1,0:T(8,128)(2,1)S(1)}, u32[]{:S(2)}, u32[]{:S(2)}) %collective-permute-start.7) | collective-permute-done | bytes 262176 | tf_op jit(solution)/shard_map/ppermute | solution.py:446
  56.3 3.0 %shard_map.81 = (bf16[384,512]{1,0:T(8,128)(2,1)}, bf16[384,512]{1,0:T(8,128)(2,1)S(1)}, f32[32,384]{1,0:T(8,128)S(1)}) custom-call(s32[4]{0:T(128)S(1)} %pad_add_fusion.info_ref.refs_0_, bf16[384,1024]{1,0:T(8,128)(2,1)S(1)} %get-tuple-element.52.refs_1_.refs_2_, f32[1,1024]{1,0:T(1,128)S(1)} %get-tuple-element.58.refs_2_, ...), custom_call_target="tpu_custom_call" | custom-call | tf_op jit(solution)/shard_map/pallas_call | solution.py:512
  59.3 0.0 collective-permute-start.9
  59.3 1.3 collective-permute-start.8
  60.5 1.3 collective-permute-start.10
  61.8 1.3 collective-permute-start.11
  63.1 0.0 collective-permute-done.9.refs_3_
  63.2 3.0 %shard_map.82 = (bf16[4,384,512]{2,1,0:T(8,128)(2,1)S(1)}, bf16[2,384,512]{2,1,0:T(8,128)(2,1)S(1)}) custom-call(s32[4]{0:T(128)S(1)} %pad_add_fusion.info_ref.refs_0_, bf16[1536,384]{1,0:T(8,128)(2,1)S(1)} %get-tuple-element.76.refs_0_, bf16[1536,384]{1,0:T(8,128)(2,1)S(1)} %get-tuple-element.77.refs_1_, bf16[384,512]{1,0:T(8,128)(2,1)S(1)} %get-tuple-element.80.refs_2_, ...), custom_call_target="tpu_custom_call" | custom-call | tf_op jit(solution)/shard_map/pallas_call | solution.py:524
  66.2 1.3 collective-permute-done.10.refs_7_
  67.5 3.3 %collective-permute-done.11.refs_8_ = f32[32,384]{1,0:T(8,128)S(1)} collective-permute-done((f32[32,384]{1,0:T(8,128)S(1)}, f32[32,384]{1,0:T(8,128)S(1)}, u32[]{:S(2)}, u32[]{:S(2)}) %collective-permute-start.11) | collective-permute-done | bytes 49184 | tf_op jit(solution)/shard_map/ppermute | solution.py:436
  70.8 3.5 %shard_map.83 = (bf16[384,512]{1,0:T(8,128)(2,1)S(1)}, bf16[384,512]{1,0:T(8,128)(2,1)S(1)}) custom-call(s32[4]{0:T(128)S(1)} %pad_add_fusion.info_ref.refs_0_, bf16[384,1024]{1,0:T(8,128)(2,1)S(1)} %get-tuple-element.60.refs_2_.refs_1_, bf16[384,1024]{1,0:T(8,128)(2,1)S(1)} %get-tuple-element.52.refs_1_.refs_2_, f32[32,384]{1,0:T(8,128)S(1)} %get-tuple-element.78.refs_3_, ...), custom_call_target="tpu_custom_call" | custom-call | tf_op jit(solution)/shard_map/pallas_call | solution.py:600
  74.3 0.1 collective-permute-start.12
  74.4 0.5 collective-permute-start.13
  74.9 1.3 collective-permute-start.15
  76.2 0.4 collective-permute-done.13.refs_3_
  76.7 2.8 %shard_map.84 = (bf16[4,384,512]{2,1,0:T(8,128)(2,1)S(1)}, bf16[2,384,512]{2,1,0:T(8,128)(2,1)S(1)}) custom-call(s32[4]{0:T(128)S(1)} %pad_add_fusion.info_ref.refs_0_, bf16[1536,384]{1,0:T(8,128)(2,1)S(1)} %get-tuple-element.76.refs_0_, bf16[1536,384]{1,0:T(8,128)(2,1)S(1)} %get-tuple-element.77.refs_1_, bf16[384,512]{1,0:T(8,128)(2,1)S(1)} %get-tuple-element.89.refs_2_, ...), custom_call_target="tpu_custom_call" | custom-call | tf_op jit(solution)/shard_map/pallas_call | solution.py:524
  79.5 1.3 collective-permute-start.17
  80.9 2.9 %shard_map.85 = (bf16[4,384,512]{2,1,0:T(8,128)(2,1)S(1)}, bf16[2,384,512]{2,1,0:T(8,128)(2,1)S(1)}) custom-call(s32[4]{0:T(128)S(1)} %pad_add_fusion.info_ref.refs_0_, bf16[1536,384]{1,0:T(8,128)(2,1)S(1)} %get-tuple-element.76.refs_0_, bf16[1536,384]{1,0:T(8,128)(2,1)S(1)} %get-tuple-element.77.refs_1_, bf16[384,512]{1,0:T(8,128)(2,1)S(1)} %get-tuple-element.92.refs_2_, ...), custom_call_target="tpu_custom_call" | custom-call | tf_op jit(solution)/shard_map/pallas_call | solution.py:524
  83.7 10.3 %collective-permute-done.15.refs_0_ = bf16[2,384,512]{2,1,0:T(8,128)(2,1)S(1)} collective-permute-done((bf16[2,384,512]{2,1,0:T(8,128)(2,1)S(1)}, bf16[2,384,512]{2,1,0:T(8,128)(2,1)S(1)}, u32[]{:S(2)}, u32[]{:S(2)}) %collective-permute-start.15) | collective-permute-done | bytes 786464 | tf_op jit(solution)/shard_map/ppermute | solution.py:556
  94.0 0.7 shard_map.86.refs_3_
  94.8 0.7 collective-permute-start.16
  95.5 5.8 %collective-permute-start.14 = (bf16[2,384,512]{2,1,0:T(8,128)(2,1)S(1)}, bf16[2,384,512]{2,1,0:T(8,128)(2,1)S(1)}, u32[]{:S(2)}, u32[]{:S(2)}) collective-permute-start(bf16[2,384,512]{2,1,0:T(8,128)(2,1)S(1)} %get-tuple-element.94), channel_id=1, source_target_pairs={{0,8},{24,16},{1,9},{25,17},{2,10},{26,18},{3,11},{27,19},{4,12},{... | collective-permute-start | bytes 2359304 | tf_op jit(solution)/shard_map/ppermute | solution.py:556
  101.3 9.6 %collective-permute-done.17.refs_0_ = bf16[2,384,512]{2,1,0:T(8,128)(2,1)S(1)} collective-permute-done((bf16[2,384,512]{2,1,0:T(8,128)(2,1)S(1)}, bf16[2,384,512]{2,1,0:T(8,128)(2,1)S(1)}, u32[]{:S(2)}, u32[]{:S(2)}) %collective-permute-start.17) | collective-permute-done | bytes 786464 | tf_op jit(solution)/shard_map/ppermute | solution.py:556
  110.9 0.7 shard_map.87.refs_0_
  111.6 0.7 collective-permute-start.19
  112.3 0.6 shard_map.88.refs_3_
  113.0 5.3 %collective-permute-start.20 = (bf16[384,512]{1,0:T(8,128)(2,1)S(1)}, bf16[384,512]{1,0:T(8,128)(2,1)S(1)}, u32[]{:S(2)}, u32[]{:S(2)}) collective-permute-start(bf16[384,512]{1,0:T(8,128)(2,1)S(1)} %shard_map.88.refs_3_), channel_id=1, source_target_pairs={{0,8},{8,0},{16,24},{24,16},{1,9},{9,1},{17,25},{25,17},{2,10},{10... | collective-permute-start | bytes 1179656 | tf_op jit(solution)/shard_map/ppermute | solution.py:446
  118.3 9.4 %collective-permute-done.14.refs_0_ = bf16[2,384,512]{2,1,0:T(8,128)(2,1)S(1)} collective-permute-done((bf16[2,384,512]{2,1,0:T(8,128)(2,1)S(1)}, bf16[2,384,512]{2,1,0:T(8,128)(2,1)S(1)}, u32[]{:S(2)}, u32[]{:S(2)}) %collective-permute-start.14) | collective-permute-done | bytes 786464 | tf_op jit(solution)/shard_map/ppermute | solution.py:556
  127.7 0.7 shard_map.89
  128.5 0.7 collective-permute-start.18
  129.2 0.7 collective-permute-start.22
  129.9 5.7 %collective-permute-done.20.refs_0_.even_ref = bf16[384,512]{1,0:T(8,128)(2,1)S(1)} collective-permute-done((bf16[384,512]{1,0:T(8,128)(2,1)S(1)}, bf16[384,512]{1,0:T(8,128)(2,1)S(1)}, u32[]{:S(2)}, u32[]{:S(2)}) %collective-permute-start.20) | collective-permute-done | bytes 393248 | tf_op jit(solution)/shard_map/ppermute | solution.py:446
  135.6 0.6 shard_map.90.refs_0_
  136.2 2.5 %collective-permute-start.23 = (bf16[384,512]{1,0:T(8,128)(2,1)S(1)}, bf16[384,512]{1,0:T(8,128)(2,1)S(1)}, u32[]{:S(2)}, u32[]{:S(2)}) collective-permute-start(bf16[384,512]{1,0:T(8,128)(2,1)S(1)} %shard_map.90.refs_0_), channel_id=1, source_target_pairs={{0,8},{8,0},{16,24},{24,16},{1,9},{9,1},{17,25},{25,17},{2,10},{10... | collective-permute-start | bytes 1179656 | tf_op jit(solution)/shard_map/ppermute | solution.py:446
  138.8 0.6 shard_map.91
  139.4 6.2 %collective-permute-start.21 = (bf16[384,512]{1,0:T(8,128)(2,1)S(1)}, bf16[384,512]{1,0:T(8,128)(2,1)S(1)}, u32[]{:S(2)}, u32[]{:S(2)}) collective-permute-start(bf16[384,512]{1,0:T(8,128)(2,1)S(1)} %shard_map.91), channel_id=1, source_target_pairs={{0,8},{8,0},{16,24},{24,16},{1,9},{9,1},{17,25},{25,17},{2,10},{10... | collective-permute-start | bytes 1179656 | tf_op jit(solution)/shard_map/ppermute | solution.py:446
  145.6 1.6 shard_map.92.refs_0_
  147.2 1.6 %collective-permute-done.23.even_ref = bf16[384,512]{1,0:T(8,128)(2,1)S(1)} collective-permute-done((bf16[384,512]{1,0:T(8,128)(2,1)S(1)}, bf16[384,512]{1,0:T(8,128)(2,1)S(1)}, u32[]{:S(2)}, u32[]{:S(2)}) %collective-permute-start.23) | collective-permute-done | bytes 393248 | tf_op jit(solution)/shard_map/ppermute | solution.py:446
  148.8 1.6 shard_map.93.refs_0_
  150.4 5.7 %collective-permute-done.21.even_ref = bf16[384,512]{1,0:T(8,128)(2,1)S(1)} collective-permute-done((bf16[384,512]{1,0:T(8,128)(2,1)S(1)}, bf16[384,512]{1,0:T(8,128)(2,1)S(1)}, u32[]{:S(2)}, u32[]{:S(2)}) %collective-permute-start.21) | collective-permute-done | bytes 393248 | tf_op jit(solution)/shard_map/ppermute | solution.py:446
  156.1 1.6 shard_map.94
  (16 shorter events, 0.0 us)
Async XLA Ops:
  0.6 43.2 %collective-permute-start.4 = (bf16[384,3072]{1,0:T(8,128)(2,1)}, bf16[384,3072]{1,0:T(8,128)(2,1)S(1)}, u32[]{:S(2)}, u32[]{:S(2)}) collective-permute-start(bf16[384,3072]{1,0:T(8,128)(2,1)} %bitcast.12), channel_id=1, source_target_pairs={{0,4},{4,0},{1,5},{5,1},{2,6},{6,2},{3,7},{7,3},{8,12},{12,8},{9,1... | collective-permute-start | bytes 7077896 | tf_op jit(solution)/shard_map/ppermute | solution.py:449
  1.2 1.7 %copy-start = (bf16[1,384,3072]{2,1,0:T(8,128)(2,1)S(1)}, bf16[1,384,3072]{2,1,0:T(8,128)(2,1)}, u32[]{:S(2)}) copy-start(bf16[1,384,3072]{2,1,0:T(8,128)(2,1)} %param.6) | copy-start | bytes 7077892
  2.9 1.0 copy-start.1
  3.9 18.2 %copy-start.2 = (f32[2]{0:T(128)S(1)}, f32[2]{0:T(128)}, u32[]{:S(2)}) copy-start(f32[2]{0:T(128)} %param.10) | copy-start | bytes 28
  11.3 23.5 %collective-permute-start.1 = (bf16[384,1024]{1,0:T(8,128)(2,1)S(1)}, bf16[384,1024]{1,0:T(8,128)(2,1)S(1)}, u32[]{:S(2)}, u32[]{:S(2)}) collective-permute-start(bf16[384,1024]{1,0:T(8,128)(2,1)S(1)} %get-tuple-element.54), channel_id=1, source_target_pairs={{8,16},{16,8},{9,17},{17,9},{10,18},{18,10},{11,19},{19,11},{12,20... | collective-permute-start | bytes 2359304 | tf_op jit(solution)/shard_map/ppermute | solution.py:446
  12.0 23.3 %collective-permute-start = (bf16[384,1024]{1,0:T(8,128)(2,1)S(1)}, bf16[384,1024]{1,0:T(8,128)(2,1)S(1)}, u32[]{:S(2)}, u32[]{:S(2)}) collective-permute-start(bf16[384,1024]{1,0:T(8,128)(2,1)S(1)} %get-tuple-element.53), channel_id=1, source_target_pairs={{0,8},{8,0},{16,24},{24,16},{1,9},{9,1},{17,25},{25,17},{2,10},{10... | collective-permute-start | bytes 2359304 | tf_op jit(solution)/shard_map/ppermute | solution.py:446
  17.4 17.3 %collective-permute-start.2 = (f32[1,1024]{1,0:T(1,128)S(1)}, f32[1,1024]{1,0:T(1,128)S(1)}, u32[]{:S(2)}, u32[]{:S(2)}) collective-permute-start(f32[1,1024]{1,0:T(1,128)S(1)} %get-tuple-element.55.refs_4_), channel_id=1, source_target_pairs={{0,16},{8,24},{1,17},{9,25},{2,18},{10,26},{3,19},{11,27},{4,20},{... | collective-permute-start | bytes 12296 | tf_op jit(solution)/shard_map/ppermute | solution.py:436
  19.3 15.5 %collective-permute-start.3 = (f32[1,1024]{1,0:T(1,128)S(1)}, f32[1,1024]{1,0:T(1,128)S(1)}, u32[]{:S(2)}, u32[]{:S(2)}) collective-permute-start(f32[1,1024]{1,0:T(1,128)S(1)} %get-tuple-element.55.refs_4_), channel_id=1, source_target_pairs={{0,24},{1,25},{2,26},{3,27},{4,28},{5,29},{6,30},{7,31}} | collective-permute-start | bytes 12296 | tf_op jit(solution)/shard_map/ppermute | solution.py:436
  37.1 7.9 %collective-permute-start.5 = (bf16[2,256,256]{2,1,0:T(8,128)(2,1)S(1)}, bf16[2,256,256]{2,1,0:T(8,128)(2,1)S(1)}, u32[]{:S(2)}, u32[]{:S(2)}) collective-permute-start(bf16[2,256,256]{2,1,0:T(8,128)(2,1)S(1)} %get-tuple-element.72), channel_id=1, source_target_pairs={{8,16},{16,8},{9,17},{17,9},{10,18},{18,10},{11,19},{19,11},{12,20... | collective-permute-start | bytes 786440 | tf_op jit(solution)/shard_map/ppermute | solution.py:446
  37.8 15.7 %collective-permute-start.6 = (bf16[2,256,256]{2,1,0:T(8,128)(2,1)S(1)}, bf16[2,256,256]{2,1,0:T(8,128)(2,1)S(1)}, u32[]{:S(2)}, u32[]{:S(2)}) collective-permute-start(bf16[2,256,256]{2,1,0:T(8,128)(2,1)S(1)} %get-tuple-element.73), channel_id=1, source_target_pairs={{16,0},{8,24},{17,1},{9,25},{18,2},{10,26},{19,3},{11,27},{20,4},{... | collective-permute-start | bytes 786440 | tf_op jit(solution)/shard_map/ppermute | solution.py:446
  39.1 17.2 %collective-permute-start.7 = (bf16[2,256,256]{2,1,0:T(8,128)(2,1)S(1)}, bf16[2,256,256]{2,1,0:T(8,128)(2,1)S(1)}, u32[]{:S(2)}, u32[]{:S(2)}) collective-permute-start(bf16[2,256,256]{2,1,0:T(8,128)(2,1)S(1)} %get-tuple-element.74), channel_id=1, source_target_pairs={{8,0},{16,24},{9,1},{17,25},{10,2},{18,26},{11,3},{19,27},{12,4},{... | collective-permute-start | bytes 786440 | tf_op jit(solution)/shard_map/ppermute | solution.py:446
  59.3 3.9 %collective-permute-start.9 = (bf16[384,512]{1,0:T(8,128)(2,1)S(1)}, bf16[384,512]{1,0:T(8,128)(2,1)S(1)}, u32[]{:S(2)}, u32[]{:S(2)}) collective-permute-start(bf16[384,512]{1,0:T(8,128)(2,1)S(1)} %get-tuple-element.80.refs_2_), channel_id=1, source_target_pairs={{0,4},{4,0},{1,5},{5,1},{2,6},{6,2},{3,7},{7,3},{8,12},{12,8},{9,1... | collective-permute-start | bytes 1179656 | tf_op jit(solution)/shard_map/ppermute | solution.py:449
  59.3 6.9 %collective-permute-start.8 = (f32[32,384]{1,0:T(8,128)S(1)}, f32[32,384]{1,0:T(8,128)S(1)}, u32[]{:S(2)}, u32[]{:S(2)}) collective-permute-start(f32[32,384]{1,0:T(8,128)S(1)} %get-tuple-element.78.refs_3_), channel_id=1, source_target_pairs={{8,0},{16,8},{24,16},{9,1},{17,9},{25,17},{10,2},{18,10},{26,18},{... | collective-permute-start | bytes 147464 | tf_op jit(solution)/shard_map/ppermute | solution.py:436
  60.5 6.9 %collective-permute-start.10 = (f32[32,384]{1,0:T(8,128)S(1)}, f32[32,384]{1,0:T(8,128)S(1)}, u32[]{:S(2)}, u32[]{:S(2)}) collective-permute-start(f32[32,384]{1,0:T(8,128)S(1)} %get-tuple-element.78.refs_3_), channel_id=1, source_target_pairs={{16,0},{24,8},{17,1},{25,9},{18,2},{26,10},{19,3},{27,11},{20,4},{... | collective-permute-start | bytes 147464 | tf_op jit(solution)/shard_map/ppermute | solution.py:436
  61.8 9.0 %collective-permute-start.11 = (f32[32,384]{1,0:T(8,128)S(1)}, f32[32,384]{1,0:T(8,128)S(1)}, u32[]{:S(2)}, u32[]{:S(2)}) collective-permute-start(f32[32,384]{1,0:T(8,128)S(1)} %get-tuple-element.78.refs_3_), channel_id=1, source_target_pairs={{24,0},{25,1},{26,2},{27,3},{28,4},{29,5},{30,6},{31,7}} | collective-permute-start | bytes 147464 | tf_op jit(solution)/shard_map/ppermute | solution.py:436
  74.3 1.9 %collective-permute-start.12 = (bf16[384,512]{1,0:T(8,128)(2,1)S(1)}, bf16[384,512]{1,0:T(8,128)(2,1)S(1)}, u32[]{:S(2)}, u32[]{:S(2)}) collective-permute-start(bf16[384,512]{1,0:T(8,128)(2,1)S(1)} %get-tuple-element.89.refs_2_), channel_id=1, source_target_pairs={{0,4},{4,0},{1,5},{5,1},{2,6},{6,2},{3,7},{7,3},{8,12},{12,8},{9,1... | collective-permute-start | bytes 1179656 | tf_op jit(solution)/shard_map/ppermute | solution.py:449
  74.4 2.3 %collective-permute-start.13 = (bf16[384,512]{1,0:T(8,128)(2,1)S(1)}, bf16[384,512]{1,0:T(8,128)(2,1)S(1)}, u32[]{:S(2)}, u32[]{:S(2)}) collective-permute-start(bf16[384,512]{1,0:T(8,128)(2,1)S(1)} %get-tuple-element.92.refs_2_), channel_id=1, source_target_pairs={{0,4},{4,0},{1,5},{5,1},{2,6},{6,2},{3,7},{7,3},{8,12},{12,8},{9,1... | collective-permute-start | bytes 1179656 | tf_op jit(solution)/shard_map/ppermute | solution.py:449
  74.9 19.1 %collective-permute-start.15 = (bf16[2,384,512]{2,1,0:T(8,128)(2,1)S(1)}, bf16[2,384,512]{2,1,0:T(8,128)(2,1)S(1)}, u32[]{:S(2)}, u32[]{:S(2)}) collective-permute-start(bf16[2,384,512]{2,1,0:T(8,128)(2,1)S(1)} %get-tuple-element.96), channel_id=1, source_target_pairs={{0,8},{24,16},{1,9},{25,17},{2,10},{26,18},{3,11},{27,19},{4,12},{... | collective-permute-start | bytes 2359304 | tf_op jit(solution)/shard_map/ppermute | solution.py:556
  79.5 31.4 %collective-permute-start.17 = (bf16[2,384,512]{2,1,0:T(8,128)(2,1)S(1)}, bf16[2,384,512]{2,1,0:T(8,128)(2,1)S(1)}, u32[]{:S(2)}, u32[]{:S(2)}) collective-permute-start(bf16[2,384,512]{2,1,0:T(8,128)(2,1)S(1)} %get-tuple-element.98), channel_id=1, source_target_pairs={{0,8},{24,16},{1,9},{25,17},{2,10},{26,18},{3,11},{27,19},{4,12},{... | collective-permute-start | bytes 2359304 | tf_op jit(solution)/shard_map/ppermute | solution.py:556
  94.8 17.6 %collective-permute-start.16 = (bf16[2,384,512]{2,1,0:T(8,128)(2,1)S(1)}, bf16[2,384,512]{2,1,0:T(8,128)(2,1)S(1)}, u32[]{:S(2)}, u32[]{:S(2)}) collective-permute-start(bf16[2,384,512]{2,1,0:T(8,128)(2,1)S(1)} %shard_map.86.refs_3_), channel_id=1, source_target_pairs={{8,16},{16,8},{9,17},{17,9},{10,18},{18,10},{11,19},{19,11},{12,20... | collective-permute-start | bytes 2359304 | tf_op jit(solution)/shard_map/ppermute | solution.py:446
  95.5 32.3 %collective-permute-start.14 = (bf16[2,384,512]{2,1,0:T(8,128)(2,1)S(1)}, bf16[2,384,512]{2,1,0:T(8,128)(2,1)S(1)}, u32[]{:S(2)}, u32[]{:S(2)}) collective-permute-start(bf16[2,384,512]{2,1,0:T(8,128)(2,1)S(1)} %get-tuple-element.94), channel_id=1, source_target_pairs={{0,8},{24,16},{1,9},{25,17},{2,10},{26,18},{3,11},{27,19},{4,12},{... | collective-permute-start | bytes 2359304 | tf_op jit(solution)/shard_map/ppermute | solution.py:556
  111.6 18.2 %collective-permute-start.19 = (bf16[2,384,512]{2,1,0:T(8,128)(2,1)S(1)}, bf16[2,384,512]{2,1,0:T(8,128)(2,1)S(1)}, u32[]{:S(2)}, u32[]{:S(2)}) collective-permute-start(bf16[2,384,512]{2,1,0:T(8,128)(2,1)S(1)} %shard_map.87.refs_0_), channel_id=1, source_target_pairs={{8,16},{16,8},{9,17},{17,9},{10,18},{18,10},{11,19},{19,11},{12,20... | collective-permute-start | bytes 2359304 | tf_op jit(solution)/shard_map/ppermute | solution.py:446
  113.0 22.6 %collective-permute-start.20 = (bf16[384,512]{1,0:T(8,128)(2,1)S(1)}, bf16[384,512]{1,0:T(8,128)(2,1)S(1)}, u32[]{:S(2)}, u32[]{:S(2)}) collective-permute-start(bf16[384,512]{1,0:T(8,128)(2,1)S(1)} %shard_map.88.refs_3_), channel_id=1, source_target_pairs={{0,8},{8,0},{16,24},{24,16},{1,9},{9,1},{17,25},{25,17},{2,10},{10... | collective-permute-start | bytes 1179656 | tf_op jit(solution)/shard_map/ppermute | solution.py:446
  128.5 10.3 %collective-permute-start.18 = (bf16[1,384,512]{2,1,0:T(8,128)(2,1)S(1)}, bf16[1,384,512]{2,1,0:T(8,128)(2,1)S(1)}, u32[]{:S(2)}, u32[]{:S(2)}) collective-permute-start(bf16[1,384,512]{2,1,0:T(8,128)(2,1)S(1)} %get-tuple-element.100.refs_1_), channel_id=1, source_target_pairs={{8,16},{16,8},{9,17},{17,9},{10,18},{18,10},{11,19},{19,11},{12,20... | collective-permute-start | bytes 1179656 | tf_op jit(solution)/shard_map/ppermute | solution.py:446
  129.2 21.2 %collective-permute-start.22 = (bf16[1,384,512]{2,1,0:T(8,128)(2,1)S(1)}, bf16[1,384,512]{2,1,0:T(8,128)(2,1)S(1)}, u32[]{:S(2)}, u32[]{:S(2)}) collective-permute-start(bf16[1,384,512]{2,1,0:T(8,128)(2,1)S(1)} %get-tuple-element.101.refs_2_), channel_id=1, source_target_pairs={{8,16},{16,8},{9,17},{17,9},{10,18},{18,10},{11,19},{19,11},{12,20... | collective-permute-start | bytes 1179656 | tf_op jit(solution)/shard_map/ppermute | solution.py:446
  136.2 12.5 %collective-permute-start.23 = (bf16[384,512]{1,0:T(8,128)(2,1)S(1)}, bf16[384,512]{1,0:T(8,128)(2,1)S(1)}, u32[]{:S(2)}, u32[]{:S(2)}) collective-permute-start(bf16[384,512]{1,0:T(8,128)(2,1)S(1)} %shard_map.90.refs_0_), channel_id=1, source_target_pairs={{0,8},{8,0},{16,24},{24,16},{1,9},{9,1},{17,25},{25,17},{2,10},{10... | collective-permute-start | bytes 1179656 | tf_op jit(solution)/shard_map/ppermute | solution.py:446
  139.4 16.6 %collective-permute-start.21 = (bf16[384,512]{1,0:T(8,128)(2,1)S(1)}, bf16[384,512]{1,0:T(8,128)(2,1)S(1)}, u32[]{:S(2)}, u32[]{:S(2)}) collective-permute-start(bf16[384,512]{1,0:T(8,128)(2,1)S(1)} %shard_map.91), channel_id=1, source_target_pairs={{0,8},{8,0},{16,24},{24,16},{1,9},{9,1},{17,25},{25,17},{2,10},{10... | collective-permute-start | bytes 1179656 | tf_op jit(solution)/shard_map/ppermute | solution.py:446

commit v6 on v5

--- a/solution.py
+++ b/solution.py
@@ -307,9 +307,22 @@
     for ref in note_refs[1:]:
         norm = norm + ref[8:9, :head_dim]
     from_memory = (from_memory + norm) * feature_slope(key_float)
-    grad_key_ref[...] = (own_key + next_key + from_memory).astype(jnp.bfloat16)
+    grad_key_ref[...] = own_key + next_key + from_memory
     to_value = dot_nn(phi_high, grad_memory) + dot_nn(phi_low, grad_memory)
     grad_value_ref[...] = (own_value + next_value + to_value).astype(jnp.bfloat16)
+
+
+def join_kernel(heads, pair_ref, rest_ref, *refs):
+    note_refs, out_ref = refs[:-1], refs[-1]
+    head_dim = pair_ref.shape[1] // (2 * heads)
+    for head in range(heads):
+        of_head = slice(head * head_dim, (head + 1) * head_dim)
+        key = pair_ref[:, 2 * head * head_dim : (2 * head + 1) * head_dim].astype(jnp.float32)
+        norm = jnp.zeros((1, head_dim), jnp.float32)
+        for ref in note_refs:
+            norm = norm + ref[16 * head + 8 : 16 * head + 9, :head_dim]
+        grad_key = rest_ref[:, of_head] + norm * feature_slope(key)
+        out_ref[:, of_head] = grad_key.astype(jnp.bfloat16)
 
 
 def pack_kernel(seq_count, dp_count, info_ref, *refs):
@@ -596,13 +609,19 @@
         notes[0], query_terms, query_first = lax.optimization_barrier(
             (notes[0], query_terms, query_first)
         )
+        notes[1:], query_first = lax.optimization_barrier((notes[1:], query_first))
         query_ends = swapped_ends(query_first)
-    grad_key, grad_value = call(
-        functools.partial(key_value_kernel, routes, len(notes)),
+    key_rest, grad_value = call(
+        functools.partial(key_value_kernel, routes, 1),
         sizes,
-        "fppnpr" + "n" * len(notes) + over + "m",
-        (("c", bf16), ("c", bf16)),
-    )(info, pair, query, note, query_next, mix, *notes, grad_memory, *arrived)
+        "fppnprn" + over + "m",
+        (("c", f32), ("c", bf16)),
+    )(info, pair, query, note, query_next, mix, notes[0], grad_memory, *arrived)
+    grad_key = pl.pallas_call(
+        functools.partial(join_kernel, heads),
+        out_shape=jax.ShapeDtypeStruct((seg_len, columns), bf16),
+        **limits(),
+    )(pair, key_rest, *notes[1:])
     if not by_swaps:
         contract = (((0,), (0,)), ((), ()))
 
@@ -642,7 +661,8 @@
         rows = summed(jnp.concatenate([grad_query, grad_key, grad_value], 1)) * grad_scale
         return (blended[None], rows.reshape(part_rows, 3, columns))
 
-    values, keys = lax.optimization_barrier((of_cores(grad_value), of_cores(grad_key)))
+    values, grad_key = lax.optimization_barrier((of_cores(grad_value), grad_key))
+    keys = of_cores(grad_key)
     value_terms, value_first = row_blocks(values)
     value_ends = swapped_ends(value_first)
     keys, value_terms = lax.optimization_barrier((keys, value_terms))

time: 158 us -> 156 us (0.987)
  waiting for transfers between devices: 71.8 us -> 64.3 us
  starting transfers between devices: 44.2 us -> 49.1 us
    ppermute x5, waiting for transfers between devices: 17.2 us -> 13.1 us  [shifted(): return lax.ppermute(x, 'seq', pairs)]
    ppermute x3, starting transfers between devices: 8.43 us -> 12.3 us  [swapped_ends(): return lax.ppermute(first, 'seq', [(0, 1), (last, last - 1)])]
    ppermute x3, waiting for transfers between devices: 29.4 us -> 26.5 us  [swapped_ends(): return lax.ppermute(first, 'seq', [(0, 1), (last, last - 1)])]
    pallas_call x1 -> x2, Pallas kernels: 3.49 us -> 3.71 us  [the longest x1 3.48 us: local(): call(functools.partial(key_value_kernel, routes, 1), sizes, 'fppnprn' + o...]
  transfers between devices with their start and end apart: 24 -> 24, of which waited for: 13 -> 11; matrix products, arithmetic and copies ran while one was open for 0% -> 0% of each run, Pallas kernels for 19% -> 22%
where the time goes in v6:
time: 156 us; the launch traced here: 155 us
  waiting for transfers between devices  64.3 us (41%)
  starting transfers between devices  49.1 us (31%)
  Pallas kernels  37.9 us (24%)
  local copies, waits for them, and re-layouts  2.82 us (2%)
    ppermute x12, starting transfers between devices, swapped(): return lax.ppermute(x, 'seq', pairs) if pairs else None  27.1 us
    ppermute x3, waiting for transfers between devices, swapped_ends(): return lax.ppermute(first, 'seq', [(0, 1), (last, last - 1)])  26.5 us
    ppermute x12, waiting for transfers between devices, swapped(): return lax.ppermute(x, 'seq', pairs) if pairs else None  24.7 us
    ppermute x5, waiting for transfers between devices, shifted(): return lax.ppermute(x, 'seq', pairs)  13.1 us
    ppermute x3, starting transfers between devices, swapped_ends(): return lax.ppermute(first, 'seq', [(0, 1), (last, last - 1)])  12.3 us
    pallas_call x3, Pallas kernels, row_blocks(): pl.pallas_call(row_blocks_kernel, in_specs=[SMEM_SPEC] + [VMEM_SPEC] * (2...  8.73 us
    ppermute x5, starting transfers between devices, shifted(): return lax.ppermute(x, 'seq', pairs)  8.48 us
    pallas_call x1, Pallas kernels, local(): pl.pallas_call(functools.partial(project_kernel, heads), in_specs=[SMEM_S...  7.38 us
  transfers between devices with their start and end apart: 24, of which 11 were waited for; matrix products, arithmetic and copies ran while one was open for 0% of the time, Pallas kernels for 22%

profile of v6, /device:TPU:0, one launch (start us, length us, event | category | flops | bytes accessed | tf_op | source)
XLA Modules:
  0.0 155.2 jit_solution(15768174526758543617)
XLA Ops:
  0.6 0.5 collective-permute-start.4
  1.1 0.1 pad_add_fusion.info_ref.refs_0_
  1.2 1.7 %copy-done = bf16[1,384,3072]{2,1,0:T(8,128)(2,1)S(1)} copy-done((bf16[1,384,3072]{2,1,0:T(8,128)(2,1)S(1)}, bf16[1,384,3072]{2,1,0:T(8,128)(2,1)}, u32[]{:S(2)}) %copy-start) | copy-done | bytes 2359320
  2.9 1.0 copy-done.1
  3.9 7.4 %shard_map.77 = (bf16[384,1024]{1,0:T(8,128)(2,1)S(1)}, bf16[384,1024]{1,0:T(8,128)(2,1)S(1)}, bf16[384,1024]{1,0:T(8,128)(2,1)S(1)}, bf16[384,1024]{1,0:T(8,128)(2,1)S(1)}, f32[1,1024]{1,0:T(1,128)S(1)}) custom-call(s32[4]{0:T(128)S(1)} %pad_add_fusion.info_ref.refs_0_, bf16[384,3072]{1,0:T(8,128)(2,1)S(1)} %bitcast.13, bf16[3072,512]{1,0:T(8,128)(2,1)} %w_key_ref.1, ...), custom_call_target="tpu_custom_call" | custom-call | tf_op jit(solution)/shard_map/pallas_call | solution.py:471
  11.3 0.7 collective-permute-start.1
  12.0 5.4 %collective-permute-start = (bf16[384,1024]{1,0:T(8,128)(2,1)S(1)}, bf16[384,1024]{1,0:T(8,128)(2,1)S(1)}, u32[]{:S(2)}, u32[]{:S(2)}) collective-permute-start(bf16[384,1024]{1,0:T(8,128)(2,1)S(1)} %get-tuple-element.55), channel_id=1, source_target_pairs={{0,8},{8,0},{16,24},{24,16},{1,9},{9,1},{17,25},{25,17},{2,10},{10... | collective-permute-start | bytes 2359304 | tf_op jit(solution)/shard_map/ppermute | solution.py:459
  17.4 1.9 %collective-permute-start.2 = (f32[1,1024]{1,0:T(1,128)S(1)}, f32[1,1024]{1,0:T(1,128)S(1)}, u32[]{:S(2)}, u32[]{:S(2)}) collective-permute-start(f32[1,1024]{1,0:T(1,128)S(1)} %get-tuple-element.57.refs_4_), channel_id=1, source_target_pairs={{0,16},{8,24},{1,17},{9,25},{2,18},{10,26},{3,19},{11,27},{4,20},{... | collective-permute-start | bytes 12296 | tf_op jit(solution)/shard_map/ppermute | solution.py:449
  19.3 2.7 %collective-permute-start.3 = (f32[1,1024]{1,0:T(1,128)S(1)}, f32[1,1024]{1,0:T(1,128)S(1)}, u32[]{:S(2)}, u32[]{:S(2)}) collective-permute-start(f32[1,1024]{1,0:T(1,128)S(1)} %get-tuple-element.57.refs_4_), channel_id=1, source_target_pairs={{0,24},{1,25},{2,26},{3,27},{4,28},{5,29},{6,30},{7,31}} | collective-permute-start | bytes 12296 | tf_op jit(solution)/shard_map/ppermute | solution.py:449
  22.1 0.1 broadcast_bitcast_fusion
  22.2 0.1 pad.7.clone
  22.2 12.5 %collective-permute-done.2 = f32[1,1024]{1,0:T(1,128)S(1)} collective-permute-done((f32[1,1024]{1,0:T(1,128)S(1)}, f32[1,1024]{1,0:T(1,128)S(1)}, u32[]{:S(2)}, u32[]{:S(2)}) %collective-permute-start.2) | collective-permute-done | bytes 4128 | tf_op jit(solution)/shard_map/ppermute | solution.py:449
  34.7 0.0 collective-permute-done.3
  34.8 0.0 collective-permute-done.1.refs_2_
  34.8 0.1 fusion.1
  34.9 0.5 collective-permute-done.refs_1_
  35.3 1.8 %shard_map.78 = (bf16[384,1024]{1,0:T(8,128)(2,1)S(1)}, bf16[384,1024]{1,0:T(8,128)(2,1)S(1)}, bf16[2,256,256]{2,1,0:T(8,128)(2,1)S(1)}, bf16[2,256,256]{2,1,0:T...) custom-call(s32[4]{0:T(128)S(1)} %pad_add_fusion.info_ref.refs_0_, ...), custom_call_target="tpu_custom_call" | custom-call | tf_op jit(solution)/shard_map/pallas_call | solution.py:504
  37.1 0.7 collective-permute-start.5
  37.8 1.3 collective-permute-start.6
  39.1 1.3 collective-permute-start.7
  40.4 3.4 %shard_map.79 = (f32[384,512]{1,0:T(8,128)S(1)}, f32[384,512]{1,0:T(8,128)S(1)}, f32[16,384]{1,0:T(8,128)S(1)}) custom-call(s32[4]{0:T(128)S(1)} %pad_add_fusion.info_ref.refs_0_, bf16[384,1024]{1,0:T(8,128)(2,1)S(1)} %get-tuple-element.54.refs_1_.refs_2_, bf16[384,1024]{1,0:T(8,128)(2,1)S(1)} %get-tuple-element.62.refs_2_.refs_1_.pair_ref, ...), custom_call_target="tpu_custom_call" | custom-call | tf_op jit(solution)/shard_map/pallas_call | solution.py:511
  43.8 0.0 collective-permute-done.4.refs_1_
  43.8 1.2 shard_map.80
  45.0 0.0 collective-permute-done.5.refs_9_.refs_8_
  45.0 8.5 %collective-permute-done.6.refs_10_.refs_9_ = bf16[2,256,256]{2,1,0:T(8,128)(2,1)S(1)} collective-permute-done((bf16[2,256,256]{2,1,0:T(8,128)(2,1)S(1)}, bf16[2,256,256]{2,1,0:T(8,128)(2,1)S(1)}, u32[]{:S(2)}, u32[]{:S(2)}) %collective-permute-start.6) | collective-permute-done | bytes 262176 | tf_op jit(solution)/shard_map/ppermute | solution.py:459
  53.5 2.8 %collective-permute-done.7.refs_11_.refs_10_ = bf16[2,256,256]{2,1,0:T(8,128)(2,1)S(1)} collective-permute-done((bf16[2,256,256]{2,1,0:T(8,128)(2,1)S(1)}, bf16[2,256,256]{2,1,0:T(8,128)(2,1)S(1)}, u32[]{:S(2)}, u32[]{:S(2)}) %collective-permute-start.7) | collective-permute-done | bytes 262176 | tf_op jit(solution)/shard_map/ppermute | solution.py:459
  56.3 3.0 %shard_map.81 = (bf16[384,512]{1,0:T(8,128)(2,1)}, bf16[384,512]{1,0:T(8,128)(2,1)S(1)}, f32[32,384]{1,0:T(8,128)S(1)}) custom-call(s32[4]{0:T(128)S(1)} %pad_add_fusion.info_ref.refs_0_, bf16[384,1024]{1,0:T(8,128)(2,1)S(1)} %get-tuple-element.54.refs_1_.refs_2_, f32[1,1024]{1,0:T(1,128)S(1)} %get-tuple-element.60.refs_2_, ...), custom_call_target="tpu_custom_call" | custom-call | tf_op jit(solution)/shard_map/pallas_call | solution.py:525
  59.2 1.3 collective-permute-start.8
  60.5 1.3 collective-permute-start.11
  61.8 1.3 collective-permute-start.12
  63.1 3.0 %shard_map.82 = (bf16[4,384,512]{2,1,0:T(8,128)(2,1)S(1)}, bf16[2,384,512]{2,1,0:T(8,128)(2,1)S(1)}) custom-call(s32[4]{0:T(128)S(1)} %pad_add_fusion.info_ref.refs_0_, bf16[1536,384]{1,0:T(8,128)(2,1)S(1)} %get-tuple-element.78.refs_0_, bf16[1536,384]{1,0:T(8,128)(2,1)S(1)} %get-tuple-element.79.refs_1_, bf16[384,512]{1,0:T(8,128)(2,1)S(1)} %get-tuple-element.82.refs_2_, ...), custom_call_target="tpu_custom_call" | custom-call | tf_op jit(solution)/shard_map/pallas_call | solution.py:537
  66.1 0.0 collective-permute-done.8.refs_6_
  66.2 3.5 %shard_map.83 = (f32[384,512]{1,0:T(8,128)S(1)}, bf16[384,512]{1,0:T(8,128)(2,1)S(1)}) custom-call(s32[4]{0:T(128)S(1)} %pad_add_fusion.info_ref.refs_0_, bf16[384,1024]{1,0:T(8,128)(2,1)S(1)} %get-tuple-element.62.refs_2_.refs_1_.pair_ref, bf16[384,1024]{1,0:T(8,128)(2,1)S(1)} %get-tuple-element.54.refs_1_.refs_2_, ...), custom_call_target="tpu_custom_call" | custom-call | tf_op jit(solution)/shard_map/pallas_call | solution.py:614
  69.7 0.6 collective-permute-start.10
  70.2 0.5 collective-permute-done.12.refs_1_
  70.8 3.1 %collective-permute-start.15 = (bf16[2,384,512]{2,1,0:T(8,128)(2,1)S(1)}, bf16[2,384,512]{2,1,0:T(8,128)(2,1)S(1)}, u32[]{:S(2)}, u32[]{:S(2)}) collective-permute-start(bf16[2,384,512]{2,1,0:T(8,128)(2,1)S(1)} %get-tuple-element.100), channel_id=1, source_target_pairs={{0,8},{24,16},{1,9},{25,17},{2,10},{26,18},{3,11},{27,19},{4,12},{... | collective-permute-start | bytes 2359304 | tf_op jit(solution)/shard_map/ppermute | solution.py:569
  73.9 0.2 shard_map.84.refs_2_
  74.2 0.1 collective-permute-start.13
  74.2 2.9 %shard_map.85 = (bf16[4,384,512]{2,1,0:T(8,128)(2,1)S(1)}, bf16[2,384,512]{2,1,0:T(8,128)(2,1)S(1)}) custom-call(s32[4]{0:T(128)S(1)} %pad_add_fusion.info_ref.refs_0_, bf16[1536,384]{1,0:T(8,128)(2,1)S(1)} %get-tuple-element.78.refs_0_, bf16[1536,384]{1,0:T(8,128)(2,1)S(1)} %get-tuple-element.79.refs_1_, bf16[384,512]{1,0:T(8,128)(2,1)S(1)} %get-tuple-element.93.refs_2_, ...), custom_call_target="tpu_custom_call" | custom-call | tf_op jit(solution)/shard_map/pallas_call | solution.py:537
  77.1 1.6 %collective-permute-start.17 = (bf16[2,384,512]{2,1,0:T(8,128)(2,1)S(1)}, bf16[2,384,512]{2,1,0:T(8,128)(2,1)S(1)}, u32[]{:S(2)}, u32[]{:S(2)}) collective-permute-start(bf16[2,384,512]{2,1,0:T(8,128)(2,1)S(1)} %get-tuple-element.102), channel_id=1, source_target_pairs={{0,8},{24,16},{1,9},{25,17},{2,10},{26,18},{3,11},{27,19},{4,12},{... | collective-permute-start | bytes 2359304 | tf_op jit(solution)/shard_map/ppermute | solution.py:569
  78.7 2.9 %shard_map.86 = (bf16[4,384,512]{2,1,0:T(8,128)(2,1)S(1)}, bf16[2,384,512]{2,1,0:T(8,128)(2,1)S(1)}) custom-call(s32[4]{0:T(128)S(1)} %pad_add_fusion.info_ref.refs_0_, bf16[1536,384]{1,0:T(8,128)(2,1)S(1)} %get-tuple-element.78.refs_0_, bf16[1536,384]{1,0:T(8,128)(2,1)S(1)} %get-tuple-element.79.refs_1_, bf16[384,512]{1,0:T(8,128)(2,1)S(1)} %shard_map.84.refs_2_, ...), custom_call_target="tpu_custom_call" | custom-call | tf_op jit(solution)/shard_map/pallas_call | solution.py:537
  81.6 10.2 %collective-permute-done.15.refs_0_ = bf16[2,384,512]{2,1,0:T(8,128)(2,1)S(1)} collective-permute-done((bf16[2,384,512]{2,1,0:T(8,128)(2,1)S(1)}, bf16[2,384,512]{2,1,0:T(8,128)(2,1)S(1)}, u32[]{:S(2)}, u32[]{:S(2)}) %collective-permute-start.15) | collective-permute-done | bytes 786464 | tf_op jit(solution)/shard_map/ppermute | solution.py:569
  91.7 0.7 shard_map.87.refs_3_
  92.5 0.7 collective-permute-start.16
  93.2 7.6 %collective-permute-start.14 = (bf16[2,384,512]{2,1,0:T(8,128)(2,1)S(1)}, bf16[2,384,512]{2,1,0:T(8,128)(2,1)S(1)}, u32[]{:S(2)}, u32[]{:S(2)}) collective-permute-start(bf16[2,384,512]{2,1,0:T(8,128)(2,1)S(1)} %get-tuple-element.98), channel_id=1, source_target_pairs={{0,8},{24,16},{1,9},{25,17},{2,10},{26,18},{3,11},{27,19},{4,12},{... | collective-permute-start | bytes 2359304 | tf_op jit(solution)/shard_map/ppermute | solution.py:569
  100.8 7.8 %collective-permute-done.17.refs_0_ = bf16[2,384,512]{2,1,0:T(8,128)(2,1)S(1)} collective-permute-done((bf16[2,384,512]{2,1,0:T(8,128)(2,1)S(1)}, bf16[2,384,512]{2,1,0:T(8,128)(2,1)S(1)}, u32[]{:S(2)}, u32[]{:S(2)}) %collective-permute-start.17) | collective-permute-done | bytes 786464 | tf_op jit(solution)/shard_map/ppermute | solution.py:569
  108.6 0.7 shard_map.88.refs_0_
  109.3 0.7 collective-permute-start.19
  110.0 0.6 shard_map.89.refs_3_
  110.7 6.2 %collective-permute-start.20 = (bf16[384,512]{1,0:T(8,128)(2,1)S(1)}, bf16[384,512]{1,0:T(8,128)(2,1)S(1)}, u32[]{:S(2)}, u32[]{:S(2)}) collective-permute-start(bf16[384,512]{1,0:T(8,128)(2,1)S(1)} %shard_map.89.refs_3_), channel_id=1, source_target_pairs={{0,8},{8,0},{16,24},{24,16},{1,9},{9,1},{17,25},{25,17},{2,10},{10... | collective-permute-start | bytes 1179656 | tf_op jit(solution)/shard_map/ppermute | solution.py:459
  116.9 8.5 %collective-permute-done.14.refs_0_ = bf16[2,384,512]{2,1,0:T(8,128)(2,1)S(1)} collective-permute-done((bf16[2,384,512]{2,1,0:T(8,128)(2,1)S(1)}, bf16[2,384,512]{2,1,0:T(8,128)(2,1)S(1)}, u32[]{:S(2)}, u32[]{:S(2)}) %collective-permute-start.14) | collective-permute-done | bytes 786464 | tf_op jit(solution)/shard_map/ppermute | solution.py:569
  125.4 0.7 shard_map.90
  126.2 0.7 collective-permute-start.18
  126.9 0.7 collective-permute-start.22
  127.6 5.7 %collective-permute-done.20.refs_0_.even_ref = bf16[384,512]{1,0:T(8,128)(2,1)S(1)} collective-permute-done((bf16[384,512]{1,0:T(8,128)(2,1)S(1)}, bf16[384,512]{1,0:T(8,128)(2,1)S(1)}, u32[]{:S(2)}, u32[]{:S(2)}) %collective-permute-start.20) | collective-permute-done | bytes 393248 | tf_op jit(solution)/shard_map/ppermute | solution.py:459
  133.2 0.6 shard_map.91.refs_0_
  133.9 2.5 %collective-permute-start.23 = (bf16[384,512]{1,0:T(8,128)(2,1)S(1)}, bf16[384,512]{1,0:T(8,128)(2,1)S(1)}, u32[]{:S(2)}, u32[]{:S(2)}) collective-permute-start(bf16[384,512]{1,0:T(8,128)(2,1)S(1)} %shard_map.91.refs_0_), channel_id=1, source_target_pairs={{0,8},{8,0},{16,24},{24,16},{1,9},{9,1},{17,25},{25,17},{2,10},{10... | collective-permute-start | bytes 1179656 | tf_op jit(solution)/shard_map/ppermute | solution.py:459
  136.4 0.6 shard_map.92
  137.1 6.2 %collective-permute-start.21 = (bf16[384,512]{1,0:T(8,128)(2,1)S(1)}, bf16[384,512]{1,0:T(8,128)(2,1)S(1)}, u32[]{:S(2)}, u32[]{:S(2)}) collective-permute-start(bf16[384,512]{1,0:T(8,128)(2,1)S(1)} %shard_map.92), channel_id=1, source_target_pairs={{0,8},{8,0},{16,24},{24,16},{1,9},{9,1},{17,25},{25,17},{2,10},{10... | collective-permute-start | bytes 1179656 | tf_op jit(solution)/shard_map/ppermute | solution.py:459
  143.3 1.6 %shard_map.93.refs_0_ = f32[3,384,512]{2,1,0:T(8,128)} custom-call(s32[4]{0:T(128)S(1)} %pad_add_fusion.info_ref.refs_0_, bf16[384,512]{1,0:T(8,128)(2,1)S(1)} %collective-permute-done.20.refs_0_.even_ref, bf16[2,384,512]{2,1,0:T(8,128)(2,1)S(1)} %collective-permute-done.16.arrived_ref.odd_ref, ...), custom_call_target="tpu_custom_call" | custom-call | tf_op jit(solution)/shard_map/pallas_call | solution.py:599
  144.8 1.6 %collective-permute-done.23.even_ref = bf16[384,512]{1,0:T(8,128)(2,1)S(1)} collective-permute-done((bf16[384,512]{1,0:T(8,128)(2,1)S(1)}, bf16[384,512]{1,0:T(8,128)(2,1)S(1)}, u32[]{:S(2)}, u32[]{:S(2)}) %collective-permute-start.23) | collective-permute-done | bytes 393248 | tf_op jit(solution)/shard_map/ppermute | solution.py:459
  146.4 1.6 %shard_map.94.refs_0_ = f32[3,384,512]{2,1,0:T(8,128)} custom-call(s32[4]{0:T(128)S(1)} %pad_add_fusion.info_ref.refs_0_, bf16[384,512]{1,0:T(8,128)(2,1)S(1)} %collective-permute-done.23.even_ref, bf16[2,384,512]{2,1,0:T(8,128)(2,1)S(1)} %collective-permute-done.19.arrived_ref.odd_ref, ...), custom_call_target="tpu_custom_call", output_to_operand_aliasing={{}: (4, {})} | custom-call | tf_op jit(solution)/shard_map/pallas_call | solution.py:599
  148.0 5.6 %collective-permute-done.21.even_ref = bf16[384,512]{1,0:T(8,128)(2,1)S(1)} collective-permute-done((bf16[384,512]{1,0:T(8,128)(2,1)S(1)}, bf16[384,512]{1,0:T(8,128)(2,1)S(1)}, u32[]{:S(2)}, u32[]{:S(2)}) %collective-permute-start.21) | collective-permute-done | bytes 393248 | tf_op jit(solution)/shard_map/ppermute | solution.py:459
  153.6 1.6 %shard_map.95 = f32[3,384,512]{2,1,0:T(8,128)} custom-call(s32[4]{0:T(128)S(1)} %pad_add_fusion.info_ref.refs_0_, bf16[384,512]{1,0:T(8,128)(2,1)S(1)} %collective-permute-done.21.even_ref, bf16[1,384,512]{2,1,0:T(8,128)(2,1)S(1)} %collective-permute-done.22.odd_ref, ...), custom_call_target="tpu_custom_call", output_to_operand_aliasing={{}: (4, {})} | custom-call | tf_op jit(solution)/shard_map/pallas_call | solution.py:599
  (17 shorter events, 0.0 us)
Async XLA Ops:
  0.6 43.2 %collective-permute-start.4 = (bf16[384,3072]{1,0:T(8,128)(2,1)}, bf16[384,3072]{1,0:T(8,128)(2,1)S(1)}, u32[]{:S(2)}, u32[]{:S(2)}) collective-permute-start(bf16[384,3072]{1,0:T(8,128)(2,1)} %bitcast.12), channel_id=1, source_target_pairs={{0,4},{4,0},{1,5},{5,1},{2,6},{6,2},{3,7},{7,3},{8,12},{12,8},{9,1... | collective-permute-start | bytes 7077896 | tf_op jit(solution)/shard_map/ppermute | solution.py:462
  1.2 1.7 %copy-start = (bf16[1,384,3072]{2,1,0:T(8,128)(2,1)S(1)}, bf16[1,384,3072]{2,1,0:T(8,128)(2,1)}, u32[]{:S(2)}) copy-start(bf16[1,384,3072]{2,1,0:T(8,128)(2,1)} %param.6) | copy-start | bytes 7077892
  2.9 1.0 copy-start.1
  3.9 18.2 %copy-start.2 = (f32[2]{0:T(128)S(1)}, f32[2]{0:T(128)}, u32[]{:S(2)}) copy-start(f32[2]{0:T(128)} %param.10) | copy-start | bytes 28
  11.3 23.5 %collective-permute-start.1 = (bf16[384,1024]{1,0:T(8,128)(2,1)S(1)}, bf16[384,1024]{1,0:T(8,128)(2,1)S(1)}, u32[]{:S(2)}, u32[]{:S(2)}) collective-permute-start(bf16[384,1024]{1,0:T(8,128)(2,1)S(1)} %get-tuple-element.56), channel_id=1, source_target_pairs={{8,16},{16,8},{9,17},{17,9},{10,18},{18,10},{11,19},{19,11},{12,20... | collective-permute-start | bytes 2359304 | tf_op jit(solution)/shard_map/ppermute | solution.py:459
  12.0 23.3 %collective-permute-start = (bf16[384,1024]{1,0:T(8,128)(2,1)S(1)}, bf16[384,1024]{1,0:T(8,128)(2,1)S(1)}, u32[]{:S(2)}, u32[]{:S(2)}) collective-permute-start(bf16[384,1024]{1,0:T(8,128)(2,1)S(1)} %get-tuple-element.55), channel_id=1, source_target_pairs={{0,8},{8,0},{16,24},{24,16},{1,9},{9,1},{17,25},{25,17},{2,10},{10... | collective-permute-start | bytes 2359304 | tf_op jit(solution)/shard_map/ppermute | solution.py:459
  17.4 17.3 %collective-permute-start.2 = (f32[1,1024]{1,0:T(1,128)S(1)}, f32[1,1024]{1,0:T(1,128)S(1)}, u32[]{:S(2)}, u32[]{:S(2)}) collective-permute-start(f32[1,1024]{1,0:T(1,128)S(1)} %get-tuple-element.57.refs_4_), channel_id=1, source_target_pairs={{0,16},{8,24},{1,17},{9,25},{2,18},{10,26},{3,19},{11,27},{4,20},{... | collective-permute-start | bytes 12296 | tf_op jit(solution)/shard_map/ppermute | solution.py:449
  19.3 15.4 %collective-permute-start.3 = (f32[1,1024]{1,0:T(1,128)S(1)}, f32[1,1024]{1,0:T(1,128)S(1)}, u32[]{:S(2)}, u32[]{:S(2)}) collective-permute-start(f32[1,1024]{1,0:T(1,128)S(1)} %get-tuple-element.57.refs_4_), channel_id=1, source_target_pairs={{0,24},{1,25},{2,26},{3,27},{4,28},{5,29},{6,30},{7,31}} | collective-permute-start | bytes 12296 | tf_op jit(solution)/shard_map/ppermute | solution.py:449
  37.1 7.9 %collective-permute-start.5 = (bf16[2,256,256]{2,1,0:T(8,128)(2,1)S(1)}, bf16[2,256,256]{2,1,0:T(8,128)(2,1)S(1)}, u32[]{:S(2)}, u32[]{:S(2)}) collective-permute-start(bf16[2,256,256]{2,1,0:T(8,128)(2,1)S(1)} %get-tuple-element.74), channel_id=1, source_target_pairs={{8,16},{16,8},{9,17},{17,9},{10,18},{18,10},{11,19},{19,11},{12,20... | collective-permute-start | bytes 786440 | tf_op jit(solution)/shard_map/ppermute | solution.py:459
  37.8 15.7 %collective-permute-start.6 = (bf16[2,256,256]{2,1,0:T(8,128)(2,1)S(1)}, bf16[2,256,256]{2,1,0:T(8,128)(2,1)S(1)}, u32[]{:S(2)}, u32[]{:S(2)}) collective-permute-start(bf16[2,256,256]{2,1,0:T(8,128)(2,1)S(1)} %get-tuple-element.75), channel_id=1, source_target_pairs={{16,0},{8,24},{17,1},{9,25},{18,2},{10,26},{19,3},{11,27},{20,4},{... | collective-permute-start | bytes 786440 | tf_op jit(solution)/shard_map/ppermute | solution.py:459
  39.1 17.2 %collective-permute-start.7 = (bf16[2,256,256]{2,1,0:T(8,128)(2,1)S(1)}, bf16[2,256,256]{2,1,0:T(8,128)(2,1)S(1)}, u32[]{:S(2)}, u32[]{:S(2)}) collective-permute-start(bf16[2,256,256]{2,1,0:T(8,128)(2,1)S(1)} %get-tuple-element.76), channel_id=1, source_target_pairs={{8,0},{16,24},{9,1},{17,25},{10,2},{18,26},{11,3},{19,27},{12,4},{... | collective-permute-start | bytes 786440 | tf_op jit(solution)/shard_map/ppermute | solution.py:459
  59.2 3.9 %collective-permute-start.9 = (bf16[384,512]{1,0:T(8,128)(2,1)S(1)}, bf16[384,512]{1,0:T(8,128)(2,1)S(1)}, u32[]{:S(2)}, u32[]{:S(2)}) collective-permute-start(bf16[384,512]{1,0:T(8,128)(2,1)S(1)} %get-tuple-element.82.refs_2_), channel_id=1, source_target_pairs={{0,4},{4,0},{1,5},{5,1},{2,6},{6,2},{3,7},{7,3},{8,12},{12,8},{9,1... | collective-permute-start | bytes 1179656 | tf_op jit(solution)/shard_map/ppermute | solution.py:462
  59.2 6.9 %collective-permute-start.8 = (f32[32,384]{1,0:T(8,128)S(1)}, f32[32,384]{1,0:T(8,128)S(1)}, u32[]{:S(2)}, u32[]{:S(2)}) collective-permute-start(f32[32,384]{1,0:T(8,128)S(1)} %get-tuple-element.80.refs_3_), channel_id=1, source_target_pairs={{8,0},{16,8},{24,16},{9,1},{17,9},{25,17},{10,2},{18,10},{26,18},{... | collective-permute-start | bytes 147464 | tf_op jit(solution)/shard_map/ppermute | solution.py:449
  60.5 9.7 %collective-permute-start.11 = (f32[32,384]{1,0:T(8,128)S(1)}, f32[32,384]{1,0:T(8,128)S(1)}, u32[]{:S(2)}, u32[]{:S(2)}) collective-permute-start(f32[32,384]{1,0:T(8,128)S(1)} %get-tuple-element.80.refs_3_), channel_id=1, source_target_pairs={{16,0},{24,8},{17,1},{25,9},{18,2},{26,10},{19,3},{27,11},{20,4},{... | collective-permute-start | bytes 147464 | tf_op jit(solution)/shard_map/ppermute | solution.py:449
  61.8 9.0 %collective-permute-start.12 = (f32[32,384]{1,0:T(8,128)S(1)}, f32[32,384]{1,0:T(8,128)S(1)}, u32[]{:S(2)}, u32[]{:S(2)}) collective-permute-start(f32[32,384]{1,0:T(8,128)S(1)} %get-tuple-element.80.refs_3_), channel_id=1, source_target_pairs={{24,0},{25,1},{26,2},{27,3},{28,4},{29,5},{30,6},{31,7}} | collective-permute-start | bytes 147464 | tf_op jit(solution)/shard_map/ppermute | solution.py:449
  69.7 4.5 %collective-permute-start.10 = (bf16[384,512]{1,0:T(8,128)(2,1)S(1)}, bf16[384,512]{1,0:T(8,128)(2,1)S(1)}, u32[]{:S(2)}, u32[]{:S(2)}) collective-permute-start(bf16[384,512]{1,0:T(8,128)(2,1)S(1)} %get-tuple-element.93.refs_2_), channel_id=1, source_target_pairs={{0,4},{4,0},{1,5},{5,1},{2,6},{6,2},{3,7},{7,3},{8,12},{12,8},{9,1... | collective-permute-start | bytes 1179656 | tf_op jit(solution)/shard_map/ppermute | solution.py:462
  70.8 21.0 %collective-permute-start.15 = (bf16[2,384,512]{2,1,0:T(8,128)(2,1)S(1)}, bf16[2,384,512]{2,1,0:T(8,128)(2,1)S(1)}, u32[]{:S(2)}, u32[]{:S(2)}) collective-permute-start(bf16[2,384,512]{2,1,0:T(8,128)(2,1)S(1)} %get-tuple-element.100), channel_id=1, source_target_pairs={{0,8},{24,16},{1,9},{25,17},{2,10},{26,18},{3,11},{27,19},{4,12},{... | collective-permute-start | bytes 2359304 | tf_op jit(solution)/shard_map/ppermute | solution.py:569
  74.2 4.5 %collective-permute-start.13 = (bf16[384,512]{1,0:T(8,128)(2,1)S(1)}, bf16[384,512]{1,0:T(8,128)(2,1)S(1)}, u32[]{:S(2)}, u32[]{:S(2)}) collective-permute-start(bf16[384,512]{1,0:T(8,128)(2,1)S(1)} %shard_map.84.refs_2_), channel_id=1, source_target_pairs={{0,4},{4,0},{1,5},{5,1},{2,6},{6,2},{3,7},{7,3},{8,12},{12,8},{9,1... | collective-permute-start | bytes 1179656 | tf_op jit(solution)/shard_map/ppermute | solution.py:462
  77.1 31.5 %collective-permute-start.17 = (bf16[2,384,512]{2,1,0:T(8,128)(2,1)S(1)}, bf16[2,384,512]{2,1,0:T(8,128)(2,1)S(1)}, u32[]{:S(2)}, u32[]{:S(2)}) collective-permute-start(bf16[2,384,512]{2,1,0:T(8,128)(2,1)S(1)} %get-tuple-element.102), channel_id=1, source_target_pairs={{0,8},{24,16},{1,9},{25,17},{2,10},{26,18},{3,11},{27,19},{4,12},{... | collective-permute-start | bytes 2359304 | tf_op jit(solution)/shard_map/ppermute | solution.py:569
  92.5 17.6 %collective-permute-start.16 = (bf16[2,384,512]{2,1,0:T(8,128)(2,1)S(1)}, bf16[2,384,512]{2,1,0:T(8,128)(2,1)S(1)}, u32[]{:S(2)}, u32[]{:S(2)}) collective-permute-start(bf16[2,384,512]{2,1,0:T(8,128)(2,1)S(1)} %shard_map.87.refs_3_), channel_id=1, source_target_pairs={{8,16},{16,8},{9,17},{17,9},{10,18},{18,10},{11,19},{19,11},{12,20... | collective-permute-start | bytes 2359304 | tf_op jit(solution)/shard_map/ppermute | solution.py:459
  93.2 32.3 %collective-permute-start.14 = (bf16[2,384,512]{2,1,0:T(8,128)(2,1)S(1)}, bf16[2,384,512]{2,1,0:T(8,128)(2,1)S(1)}, u32[]{:S(2)}, u32[]{:S(2)}) collective-permute-start(bf16[2,384,512]{2,1,0:T(8,128)(2,1)S(1)} %get-tuple-element.98), channel_id=1, source_target_pairs={{0,8},{24,16},{1,9},{25,17},{2,10},{26,18},{3,11},{27,19},{4,12},{... | collective-permute-start | bytes 2359304 | tf_op jit(solution)/shard_map/ppermute | solution.py:569
  109.3 18.2 %collective-permute-start.19 = (bf16[2,384,512]{2,1,0:T(8,128)(2,1)S(1)}, bf16[2,384,512]{2,1,0:T(8,128)(2,1)S(1)}, u32[]{:S(2)}, u32[]{:S(2)}) collective-permute-start(bf16[2,384,512]{2,1,0:T(8,128)(2,1)S(1)} %shard_map.88.refs_0_), channel_id=1, source_target_pairs={{8,16},{16,8},{9,17},{17,9},{10,18},{18,10},{11,19},{19,11},{12,20... | collective-permute-start | bytes 2359304 | tf_op jit(solution)/shard_map/ppermute | solution.py:459
  110.7 22.6 %collective-permute-start.20 = (bf16[384,512]{1,0:T(8,128)(2,1)S(1)}, bf16[384,512]{1,0:T(8,128)(2,1)S(1)}, u32[]{:S(2)}, u32[]{:S(2)}) collective-permute-start(bf16[384,512]{1,0:T(8,128)(2,1)S(1)} %shard_map.89.refs_3_), channel_id=1, source_target_pairs={{0,8},{8,0},{16,24},{24,16},{1,9},{9,1},{17,25},{25,17},{2,10},{10... | collective-permute-start | bytes 1179656 | tf_op jit(solution)/shard_map/ppermute | solution.py:459
  126.2 10.3 %collective-permute-start.18 = (bf16[1,384,512]{2,1,0:T(8,128)(2,1)S(1)}, bf16[1,384,512]{2,1,0:T(8,128)(2,1)S(1)}, u32[]{:S(2)}, u32[]{:S(2)}) collective-permute-start(bf16[1,384,512]{2,1,0:T(8,128)(2,1)S(1)} %get-tuple-element.104.refs_1_), channel_id=1, source_target_pairs={{8,16},{16,8},{9,17},{17,9},{10,18},{18,10},{11,19},{19,11},{12,20... | collective-permute-start | bytes 1179656 | tf_op jit(solution)/shard_map/ppermute | solution.py:459
  126.9 21.1 %collective-permute-start.22 = (bf16[1,384,512]{2,1,0:T(8,128)(2,1)S(1)}, bf16[1,384,512]{2,1,0:T(8,128)(2,1)S(1)}, u32[]{:S(2)}, u32[]{:S(2)}) collective-permute-start(bf16[1,384,512]{2,1,0:T(8,128)(2,1)S(1)} %get-tuple-element.105.refs_2_), channel_id=1, source_target_pairs={{8,16},{16,8},{9,17},{17,9},{10,18},{18,10},{11,19},{19,11},{12,20... | collective-permute-start | bytes 1179656 | tf_op jit(solution)/shard_map/ppermute | solution.py:459
  133.9 12.5 %collective-permute-start.23 = (bf16[384,512]{1,0:T(8,128)(2,1)S(1)}, bf16[384,512]{1,0:T(8,128)(2,1)S(1)}, u32[]{:S(2)}, u32[]{:S(2)}) collective-permute-start(bf16[384,512]{1,0:T(8,128)(2,1)S(1)} %shard_map.91.refs_0_), channel_id=1, source_target_pairs={{0,8},{8,0},{16,24},{24,16},{1,9},{9,1},{17,25},{25,17},{2,10},{10... | collective-permute-start | bytes 1179656 | tf_op jit(solution)/shard_map/ppermute | solution.py:459
  137.1 16.6 %collective-permute-start.21 = (bf16[384,512]{1,0:T(8,128)(2,1)S(1)}, bf16[384,512]{1,0:T(8,128)(2,1)S(1)}, u32[]{:S(2)}, u32[]{:S(2)}) collective-permute-start(bf16[384,512]{1,0:T(8,128)(2,1)S(1)} %shard_map.92), channel_id=1, source_target_pairs={{0,8},{8,0},{16,24},{24,16},{1,9},{9,1},{17,25},{25,17},{2,10},{10... | collective-permute-start | bytes 1179656 | tf_op jit(solution)/shard_map/ppermute | solution.py:459

commit v7 on v6

--- a/solution.py
+++ b/solution.py
@@ -288,7 +288,7 @@
             rows = lax.broadcasted_iota(jnp.int32, score.shape, 0)
             cols = lax.broadcasted_iota(jnp.int32, score.shape, 1)
             score = jnp.where(rows <= cols, score, -1e30)
-        soft = jnp.exp(score - stats[0:1]) * stats[1:2]
+        soft = jnp.exp(jnp.minimum(score - stats[0:1], 0.0)) * stats[1:2]
         grad_value = dot_nn(soft.astype(jnp.bfloat16), grad_local)
         grad_soft = dot_nt(value, grad_local)
         score_grad = (soft * (grad_soft - stats[2:3]) * scale).astype(jnp.bfloat16)

time: 156 us -> 156 us (level)
  no operation moved by 1% of the time
where the time goes in v7:
time: 156 us; the launch traced here: 155 us
  waiting for transfers between devices  64.3 us (41%)
  starting transfers between devices  49.1 us (31%)
  Pallas kernels  37.9 us (24%)
  local copies, waits for them, and re-layouts  2.82 us (2%)
    ppermute x12, starting transfers between devices, swapped(): return lax.ppermute(x, 'seq', pairs) if pairs else None  27.1 us
    ppermute x3, waiting for transfers between devices, swapped_ends(): return lax.ppermute(first, 'seq', [(0, 1), (last, last - 1)])  26.5 us
    ppermute x12, waiting for transfers between devices, swapped(): return lax.ppermute(x, 'seq', pairs) if pairs else None  24.6 us
    ppermute x5, waiting for transfers between devices, shifted(): return lax.ppermute(x, 'seq', pairs)  13.1 us
    ppermute x3, starting transfers between devices, swapped_ends(): return lax.ppermute(first, 'seq', [(0, 1), (last, last - 1)])  12.3 us
    pallas_call x3, Pallas kernels, row_blocks(): pl.pallas_call(row_blocks_kernel, in_specs=[SMEM_SPEC] + [VMEM_SPEC] * (2...  8.73 us
    ppermute x5, starting transfers between devices, shifted(): return lax.ppermute(x, 'seq', pairs)  8.48 us
    pallas_call x1, Pallas kernels, local(): pl.pallas_call(functools.partial(project_kernel, heads), in_specs=[SMEM_S...  7.38 us
  transfers between devices with their start and end apart: 24, of which 11 were waited for; matrix products, arithmetic and copies ran while one was open for 0% of the time, Pallas kernels for 22%

profile of v7, /device:TPU:0, one launch (start us, length us, event | category | flops | bytes accessed | tf_op | source)
XLA Modules:
  0.0 155.2 jit_solution(4129273024315665520)
XLA Ops:
  0.6 0.5 collective-permute-start.4
  1.1 0.1 pad_add_fusion.info_ref.refs_0_
  1.2 1.7 %copy-done = bf16[1,384,3072]{2,1,0:T(8,128)(2,1)S(1)} copy-done((bf16[1,384,3072]{2,1,0:T(8,128)(2,1)S(1)}, bf16[1,384,3072]{2,1,0:T(8,128)(2,1)}, u32[]{:S(2)}) %copy-start) | copy-done | bytes 2359320
  2.9 1.0 copy-done.1
  3.9 7.4 %shard_map.77 = (bf16[384,1024]{1,0:T(8,128)(2,1)S(1)}, bf16[384,1024]{1,0:T(8,128)(2,1)S(1)}, bf16[384,1024]{1,0:T(8,128)(2,1)S(1)}, bf16[384,1024]{1,0:T(8,128)(2,1)S(1)}, f32[1,1024]{1,0:T(1,128)S(1)}) custom-call(s32[4]{0:T(128)S(1)} %pad_add_fusion.info_ref.refs_0_, bf16[384,3072]{1,0:T(8,128)(2,1)S(1)} %bitcast.13, bf16[3072,512]{1,0:T(8,128)(2,1)} %w_key_ref.1, ...), custom_call_target="tpu_custom_call" | custom-call | tf_op jit(solution)/shard_map/pallas_call | solution.py:471
  11.3 0.7 collective-permute-start.1
  12.0 5.4 %collective-permute-start = (bf16[384,1024]{1,0:T(8,128)(2,1)S(1)}, bf16[384,1024]{1,0:T(8,128)(2,1)S(1)}, u32[]{:S(2)}, u32[]{:S(2)}) collective-permute-start(bf16[384,1024]{1,0:T(8,128)(2,1)S(1)} %get-tuple-element.55), channel_id=1, source_target_pairs={{0,8},{8,0},{16,24},{24,16},{1,9},{9,1},{17,25},{25,17},{2,10},{10... | collective-permute-start | bytes 2359304 | tf_op jit(solution)/shard_map/ppermute | solution.py:459
  17.4 1.9 %collective-permute-start.2 = (f32[1,1024]{1,0:T(1,128)S(1)}, f32[1,1024]{1,0:T(1,128)S(1)}, u32[]{:S(2)}, u32[]{:S(2)}) collective-permute-start(f32[1,1024]{1,0:T(1,128)S(1)} %get-tuple-element.57.refs_4_), channel_id=1, source_target_pairs={{0,16},{8,24},{1,17},{9,25},{2,18},{10,26},{3,19},{11,27},{4,20},{... | collective-permute-start | bytes 12296 | tf_op jit(solution)/shard_map/ppermute | solution.py:449
  19.3 2.7 %collective-permute-start.3 = (f32[1,1024]{1,0:T(1,128)S(1)}, f32[1,1024]{1,0:T(1,128)S(1)}, u32[]{:S(2)}, u32[]{:S(2)}) collective-permute-start(f32[1,1024]{1,0:T(1,128)S(1)} %get-tuple-element.57.refs_4_), channel_id=1, source_target_pairs={{0,24},{1,25},{2,26},{3,27},{4,28},{5,29},{6,30},{7,31}} | collective-permute-start | bytes 12296 | tf_op jit(solution)/shard_map/ppermute | solution.py:449
  22.1 0.1 broadcast_bitcast_fusion
  22.2 0.1 pad.7.clone
  22.2 12.5 %collective-permute-done.2 = f32[1,1024]{1,0:T(1,128)S(1)} collective-permute-done((f32[1,1024]{1,0:T(1,128)S(1)}, f32[1,1024]{1,0:T(1,128)S(1)}, u32[]{:S(2)}, u32[]{:S(2)}) %collective-permute-start.2) | collective-permute-done | bytes 4128 | tf_op jit(solution)/shard_map/ppermute | solution.py:449
  34.7 0.0 collective-permute-done.3
  34.8 0.0 collective-permute-done.1.refs_2_
  34.8 0.1 fusion.1
  34.9 0.5 collective-permute-done.refs_1_
  35.3 1.8 %shard_map.78 = (bf16[384,1024]{1,0:T(8,128)(2,1)S(1)}, bf16[384,1024]{1,0:T(8,128)(2,1)S(1)}, bf16[2,256,256]{2,1,0:T(8,128)(2,1)S(1)}, bf16[2,256,256]{2,1,0:T...) custom-call(s32[4]{0:T(128)S(1)} %pad_add_fusion.info_ref.refs_0_, ...), custom_call_target="tpu_custom_call" | custom-call | tf_op jit(solution)/shard_map/pallas_call | solution.py:504
  37.1 0.7 collective-permute-start.5
  37.8 1.3 collective-permute-start.6
  39.1 1.3 collective-permute-start.7
  40.4 3.4 %shard_map.79 = (f32[384,512]{1,0:T(8,128)S(1)}, f32[384,512]{1,0:T(8,128)S(1)}, f32[16,384]{1,0:T(8,128)S(1)}) custom-call(s32[4]{0:T(128)S(1)} %pad_add_fusion.info_ref.refs_0_, bf16[384,1024]{1,0:T(8,128)(2,1)S(1)} %get-tuple-element.54.refs_1_.refs_2_, bf16[384,1024]{1,0:T(8,128)(2,1)S(1)} %get-tuple-element.62.refs_2_.refs_1_.pair_ref, ...), custom_call_target="tpu_custom_call" | custom-call | tf_op jit(solution)/shard_map/pallas_call | solution.py:511
  43.8 0.0 collective-permute-done.4.refs_1_
  43.8 1.2 shard_map.80
  45.0 0.0 collective-permute-done.5.refs_9_.refs_8_
  45.0 8.5 %collective-permute-done.6.refs_10_.refs_9_ = bf16[2,256,256]{2,1,0:T(8,128)(2,1)S(1)} collective-permute-done((bf16[2,256,256]{2,1,0:T(8,128)(2,1)S(1)}, bf16[2,256,256]{2,1,0:T(8,128)(2,1)S(1)}, u32[]{:S(2)}, u32[]{:S(2)}) %collective-permute-start.6) | collective-permute-done | bytes 262176 | tf_op jit(solution)/shard_map/ppermute | solution.py:459
  53.5 2.8 %collective-permute-done.7.refs_11_.refs_10_ = bf16[2,256,256]{2,1,0:T(8,128)(2,1)S(1)} collective-permute-done((bf16[2,256,256]{2,1,0:T(8,128)(2,1)S(1)}, bf16[2,256,256]{2,1,0:T(8,128)(2,1)S(1)}, u32[]{:S(2)}, u32[]{:S(2)}) %collective-permute-start.7) | collective-permute-done | bytes 262176 | tf_op jit(solution)/shard_map/ppermute | solution.py:459
  56.3 3.0 %shard_map.81 = (bf16[384,512]{1,0:T(8,128)(2,1)}, bf16[384,512]{1,0:T(8,128)(2,1)S(1)}, f32[32,384]{1,0:T(8,128)S(1)}) custom-call(s32[4]{0:T(128)S(1)} %pad_add_fusion.info_ref.refs_0_, bf16[384,1024]{1,0:T(8,128)(2,1)S(1)} %get-tuple-element.54.refs_1_.refs_2_, f32[1,1024]{1,0:T(1,128)S(1)} %get-tuple-element.60.refs_2_, ...), custom_call_target="tpu_custom_call" | custom-call | tf_op jit(solution)/shard_map/pallas_call | solution.py:525
  59.2 1.3 collective-permute-start.8
  60.5 1.3 collective-permute-start.11
  61.8 1.3 collective-permute-start.12
  63.1 3.0 %shard_map.82 = (bf16[4,384,512]{2,1,0:T(8,128)(2,1)S(1)}, bf16[2,384,512]{2,1,0:T(8,128)(2,1)S(1)}) custom-call(s32[4]{0:T(128)S(1)} %pad_add_fusion.info_ref.refs_0_, bf16[1536,384]{1,0:T(8,128)(2,1)S(1)} %get-tuple-element.78.refs_0_, bf16[1536,384]{1,0:T(8,128)(2,1)S(1)} %get-tuple-element.79.refs_1_, bf16[384,512]{1,0:T(8,128)(2,1)S(1)} %get-tuple-element.82.refs_2_, ...), custom_call_target="tpu_custom_call" | custom-call | tf_op jit(solution)/shard_map/pallas_call | solution.py:537
  66.1 0.0 collective-permute-done.8.refs_6_
  66.2 3.5 %shard_map.83 = (f32[384,512]{1,0:T(8,128)S(1)}, bf16[384,512]{1,0:T(8,128)(2,1)S(1)}) custom-call(s32[4]{0:T(128)S(1)} %pad_add_fusion.info_ref.refs_0_, bf16[384,1024]{1,0:T(8,128)(2,1)S(1)} %get-tuple-element.62.refs_2_.refs_1_.pair_ref, bf16[384,1024]{1,0:T(8,128)(2,1)S(1)} %get-tuple-element.54.refs_1_.refs_2_, ...), custom_call_target="tpu_custom_call" | custom-call | tf_op jit(solution)/shard_map/pallas_call | solution.py:614
  69.7 0.6 collective-permute-start.10
  70.2 0.5 collective-permute-done.12.refs_1_
  70.8 3.1 %collective-permute-start.15 = (bf16[2,384,512]{2,1,0:T(8,128)(2,1)S(1)}, bf16[2,384,512]{2,1,0:T(8,128)(2,1)S(1)}, u32[]{:S(2)}, u32[]{:S(2)}) collective-permute-start(bf16[2,384,512]{2,1,0:T(8,128)(2,1)S(1)} %get-tuple-element.100), channel_id=1, source_target_pairs={{0,8},{24,16},{1,9},{25,17},{2,10},{26,18},{3,11},{27,19},{4,12},{... | collective-permute-start | bytes 2359304 | tf_op jit(solution)/shard_map/ppermute | solution.py:569
  73.9 0.2 shard_map.84.refs_2_
  74.2 0.1 collective-permute-start.13
  74.3 2.9 %shard_map.85 = (bf16[4,384,512]{2,1,0:T(8,128)(2,1)S(1)}, bf16[2,384,512]{2,1,0:T(8,128)(2,1)S(1)}) custom-call(s32[4]{0:T(128)S(1)} %pad_add_fusion.info_ref.refs_0_, bf16[1536,384]{1,0:T(8,128)(2,1)S(1)} %get-tuple-element.78.refs_0_, bf16[1536,384]{1,0:T(8,128)(2,1)S(1)} %get-tuple-element.79.refs_1_, bf16[384,512]{1,0:T(8,128)(2,1)S(1)} %get-tuple-element.93.refs_2_, ...), custom_call_target="tpu_custom_call" | custom-call | tf_op jit(solution)/shard_map/pallas_call | solution.py:537
  77.1 1.6 %collective-permute-start.17 = (bf16[2,384,512]{2,1,0:T(8,128)(2,1)S(1)}, bf16[2,384,512]{2,1,0:T(8,128)(2,1)S(1)}, u32[]{:S(2)}, u32[]{:S(2)}) collective-permute-start(bf16[2,384,512]{2,1,0:T(8,128)(2,1)S(1)} %get-tuple-element.102), channel_id=1, source_target_pairs={{0,8},{24,16},{1,9},{25,17},{2,10},{26,18},{3,11},{27,19},{4,12},{... | collective-permute-start | bytes 2359304 | tf_op jit(solution)/shard_map/ppermute | solution.py:569
  78.7 2.9 %shard_map.86 = (bf16[4,384,512]{2,1,0:T(8,128)(2,1)S(1)}, bf16[2,384,512]{2,1,0:T(8,128)(2,1)S(1)}) custom-call(s32[4]{0:T(128)S(1)} %pad_add_fusion.info_ref.refs_0_, bf16[1536,384]{1,0:T(8,128)(2,1)S(1)} %get-tuple-element.78.refs_0_, bf16[1536,384]{1,0:T(8,128)(2,1)S(1)} %get-tuple-element.79.refs_1_, bf16[384,512]{1,0:T(8,128)(2,1)S(1)} %shard_map.84.refs_2_, ...), custom_call_target="tpu_custom_call" | custom-call | tf_op jit(solution)/shard_map/pallas_call | solution.py:537
  81.6 10.2 %collective-permute-done.15.refs_0_ = bf16[2,384,512]{2,1,0:T(8,128)(2,1)S(1)} collective-permute-done((bf16[2,384,512]{2,1,0:T(8,128)(2,1)S(1)}, bf16[2,384,512]{2,1,0:T(8,128)(2,1)S(1)}, u32[]{:S(2)}, u32[]{:S(2)}) %collective-permute-start.15) | collective-permute-done | bytes 786464 | tf_op jit(solution)/shard_map/ppermute | solution.py:569
  91.7 0.7 shard_map.87.refs_3_
  92.5 0.7 collective-permute-start.16
  93.2 7.6 %collective-permute-start.14 = (bf16[2,384,512]{2,1,0:T(8,128)(2,1)S(1)}, bf16[2,384,512]{2,1,0:T(8,128)(2,1)S(1)}, u32[]{:S(2)}, u32[]{:S(2)}) collective-permute-start(bf16[2,384,512]{2,1,0:T(8,128)(2,1)S(1)} %get-tuple-element.98), channel_id=1, source_target_pairs={{0,8},{24,16},{1,9},{25,17},{2,10},{26,18},{3,11},{27,19},{4,12},{... | collective-permute-start | bytes 2359304 | tf_op jit(solution)/shard_map/ppermute | solution.py:569
  100.8 7.8 %collective-permute-done.17.refs_0_ = bf16[2,384,512]{2,1,0:T(8,128)(2,1)S(1)} collective-permute-done((bf16[2,384,512]{2,1,0:T(8,128)(2,1)S(1)}, bf16[2,384,512]{2,1,0:T(8,128)(2,1)S(1)}, u32[]{:S(2)}, u32[]{:S(2)}) %collective-permute-start.17) | collective-permute-done | bytes 786464 | tf_op jit(solution)/shard_map/ppermute | solution.py:569
  108.6 0.7 shard_map.88.refs_0_
  109.3 0.7 collective-permute-start.19
  110.1 0.6 shard_map.89.refs_3_
  110.7 6.2 %collective-permute-start.20 = (bf16[384,512]{1,0:T(8,128)(2,1)S(1)}, bf16[384,512]{1,0:T(8,128)(2,1)S(1)}, u32[]{:S(2)}, u32[]{:S(2)}) collective-permute-start(bf16[384,512]{1,0:T(8,128)(2,1)S(1)} %shard_map.89.refs_3_), channel_id=1, source_target_pairs={{0,8},{8,0},{16,24},{24,16},{1,9},{9,1},{17,25},{25,17},{2,10},{10... | collective-permute-start | bytes 1179656 | tf_op jit(solution)/shard_map/ppermute | solution.py:459
  116.9 8.5 %collective-permute-done.14.refs_0_ = bf16[2,384,512]{2,1,0:T(8,128)(2,1)S(1)} collective-permute-done((bf16[2,384,512]{2,1,0:T(8,128)(2,1)S(1)}, bf16[2,384,512]{2,1,0:T(8,128)(2,1)S(1)}, u32[]{:S(2)}, u32[]{:S(2)}) %collective-permute-start.14) | collective-permute-done | bytes 786464 | tf_op jit(solution)/shard_map/ppermute | solution.py:569
  125.5 0.7 shard_map.90
  126.2 0.7 collective-permute-start.18
  126.9 0.7 collective-permute-start.22
  127.6 5.7 %collective-permute-done.20.refs_0_.even_ref = bf16[384,512]{1,0:T(8,128)(2,1)S(1)} collective-permute-done((bf16[384,512]{1,0:T(8,128)(2,1)S(1)}, bf16[384,512]{1,0:T(8,128)(2,1)S(1)}, u32[]{:S(2)}, u32[]{:S(2)}) %collective-permute-start.20) | collective-permute-done | bytes 393248 | tf_op jit(solution)/shard_map/ppermute | solution.py:459
  133.3 0.6 shard_map.91.refs_0_
  133.9 2.5 %collective-permute-start.23 = (bf16[384,512]{1,0:T(8,128)(2,1)S(1)}, bf16[384,512]{1,0:T(8,128)(2,1)S(1)}, u32[]{:S(2)}, u32[]{:S(2)}) collective-permute-start(bf16[384,512]{1,0:T(8,128)(2,1)S(1)} %shard_map.91.refs_0_), channel_id=1, source_target_pairs={{0,8},{8,0},{16,24},{24,16},{1,9},{9,1},{17,25},{25,17},{2,10},{10... | collective-permute-start | bytes 1179656 | tf_op jit(solution)/shard_map/ppermute | solution.py:459
  136.5 0.6 shard_map.92
  137.1 6.2 %collective-permute-start.21 = (bf16[384,512]{1,0:T(8,128)(2,1)S(1)}, bf16[384,512]{1,0:T(8,128)(2,1)S(1)}, u32[]{:S(2)}, u32[]{:S(2)}) collective-permute-start(bf16[384,512]{1,0:T(8,128)(2,1)S(1)} %shard_map.92), channel_id=1, source_target_pairs={{0,8},{8,0},{16,24},{24,16},{1,9},{9,1},{17,25},{25,17},{2,10},{10... | collective-permute-start | bytes 1179656 | tf_op jit(solution)/shard_map/ppermute | solution.py:459
  143.3 1.6 %shard_map.93.refs_0_ = f32[3,384,512]{2,1,0:T(8,128)} custom-call(s32[4]{0:T(128)S(1)} %pad_add_fusion.info_ref.refs_0_, bf16[384,512]{1,0:T(8,128)(2,1)S(1)} %collective-permute-done.20.refs_0_.even_ref, bf16[2,384,512]{2,1,0:T(8,128)(2,1)S(1)} %collective-permute-done.16.arrived_ref.odd_ref, ...), custom_call_target="tpu_custom_call" | custom-call | tf_op jit(solution)/shard_map/pallas_call | solution.py:599
  144.8 1.6 %collective-permute-done.23.even_ref = bf16[384,512]{1,0:T(8,128)(2,1)S(1)} collective-permute-done((bf16[384,512]{1,0:T(8,128)(2,1)S(1)}, bf16[384,512]{1,0:T(8,128)(2,1)S(1)}, u32[]{:S(2)}, u32[]{:S(2)}) %collective-permute-start.23) | collective-permute-done | bytes 393248 | tf_op jit(solution)/shard_map/ppermute | solution.py:459
  146.4 1.6 %shard_map.94.refs_0_ = f32[3,384,512]{2,1,0:T(8,128)} custom-call(s32[4]{0:T(128)S(1)} %pad_add_fusion.info_ref.refs_0_, bf16[384,512]{1,0:T(8,128)(2,1)S(1)} %collective-permute-done.23.even_ref, bf16[2,384,512]{2,1,0:T(8,128)(2,1)S(1)} %collective-permute-done.19.arrived_ref.odd_ref, ...), custom_call_target="tpu_custom_call", output_to_operand_aliasing={{}: (4, {})} | custom-call | tf_op jit(solution)/shard_map/pallas_call | solution.py:599
  148.0 5.6 %collective-permute-done.21.even_ref = bf16[384,512]{1,0:T(8,128)(2,1)S(1)} collective-permute-done((bf16[384,512]{1,0:T(8,128)(2,1)S(1)}, bf16[384,512]{1,0:T(8,128)(2,1)S(1)}, u32[]{:S(2)}, u32[]{:S(2)}) %collective-permute-start.21) | collective-permute-done | bytes 393248 | tf_op jit(solution)/shard_map/ppermute | solution.py:459
  153.6 1.6 %shard_map.95 = f32[3,384,512]{2,1,0:T(8,128)} custom-call(s32[4]{0:T(128)S(1)} %pad_add_fusion.info_ref.refs_0_, bf16[384,512]{1,0:T(8,128)(2,1)S(1)} %collective-permute-done.21.even_ref, bf16[1,384,512]{2,1,0:T(8,128)(2,1)S(1)} %collective-permute-done.22.odd_ref, ...), custom_call_target="tpu_custom_call", output_to_operand_aliasing={{}: (4, {})} | custom-call | tf_op jit(solution)/shard_map/pallas_call | solution.py:599
  (17 shorter events, 0.0 us)
Async XLA Ops:
  0.6 43.2 %collective-permute-start.4 = (bf16[384,3072]{1,0:T(8,128)(2,1)}, bf16[384,3072]{1,0:T(8,128)(2,1)S(1)}, u32[]{:S(2)}, u32[]{:S(2)}) collective-permute-start(bf16[384,3072]{1,0:T(8,128)(2,1)} %bitcast.12), channel_id=1, source_target_pairs={{0,4},{4,0},{1,5},{5,1},{2,6},{6,2},{3,7},{7,3},{8,12},{12,8},{9,1... | collective-permute-start | bytes 7077896 | tf_op jit(solution)/shard_map/ppermute | solution.py:462
  1.2 1.7 %copy-start = (bf16[1,384,3072]{2,1,0:T(8,128)(2,1)S(1)}, bf16[1,384,3072]{2,1,0:T(8,128)(2,1)}, u32[]{:S(2)}) copy-start(bf16[1,384,3072]{2,1,0:T(8,128)(2,1)} %param.6) | copy-start | bytes 7077892
  2.9 1.0 copy-start.1
  3.9 18.2 %copy-start.2 = (f32[2]{0:T(128)S(1)}, f32[2]{0:T(128)}, u32[]{:S(2)}) copy-start(f32[2]{0:T(128)} %param.10) | copy-start | bytes 28
  11.3 23.5 %collective-permute-start.1 = (bf16[384,1024]{1,0:T(8,128)(2,1)S(1)}, bf16[384,1024]{1,0:T(8,128)(2,1)S(1)}, u32[]{:S(2)}, u32[]{:S(2)}) collective-permute-start(bf16[384,1024]{1,0:T(8,128)(2,1)S(1)} %get-tuple-element.56), channel_id=1, source_target_pairs={{8,16},{16,8},{9,17},{17,9},{10,18},{18,10},{11,19},{19,11},{12,20... | collective-permute-start | bytes 2359304 | tf_op jit(solution)/shard_map/ppermute | solution.py:459
  12.0 23.3 %collective-permute-start = (bf16[384,1024]{1,0:T(8,128)(2,1)S(1)}, bf16[384,1024]{1,0:T(8,128)(2,1)S(1)}, u32[]{:S(2)}, u32[]{:S(2)}) collective-permute-start(bf16[384,1024]{1,0:T(8,128)(2,1)S(1)} %get-tuple-element.55), channel_id=1, source_target_pairs={{0,8},{8,0},{16,24},{24,16},{1,9},{9,1},{17,25},{25,17},{2,10},{10... | collective-permute-start | bytes 2359304 | tf_op jit(solution)/shard_map/ppermute | solution.py:459
  17.4 17.3 %collective-permute-start.2 = (f32[1,1024]{1,0:T(1,128)S(1)}, f32[1,1024]{1,0:T(1,128)S(1)}, u32[]{:S(2)}, u32[]{:S(2)}) collective-permute-start(f32[1,1024]{1,0:T(1,128)S(1)} %get-tuple-element.57.refs_4_), channel_id=1, source_target_pairs={{0,16},{8,24},{1,17},{9,25},{2,18},{10,26},{3,19},{11,27},{4,20},{... | collective-permute-start | bytes 12296 | tf_op jit(solution)/shard_map/ppermute | solution.py:449
  19.3 15.4 %collective-permute-start.3 = (f32[1,1024]{1,0:T(1,128)S(1)}, f32[1,1024]{1,0:T(1,128)S(1)}, u32[]{:S(2)}, u32[]{:S(2)}) collective-permute-start(f32[1,1024]{1,0:T(1,128)S(1)} %get-tuple-element.57.refs_4_), channel_id=1, source_target_pairs={{0,24},{1,25},{2,26},{3,27},{4,28},{5,29},{6,30},{7,31}} | collective-permute-start | bytes 12296 | tf_op jit(solution)/shard_map/ppermute | solution.py:449
  37.1 7.9 %collective-permute-start.5 = (bf16[2,256,256]{2,1,0:T(8,128)(2,1)S(1)}, bf16[2,256,256]{2,1,0:T(8,128)(2,1)S(1)}, u32[]{:S(2)}, u32[]{:S(2)}) collective-permute-start(bf16[2,256,256]{2,1,0:T(8,128)(2,1)S(1)} %get-tuple-element.74), channel_id=1, source_target_pairs={{8,16},{16,8},{9,17},{17,9},{10,18},{18,10},{11,19},{19,11},{12,20... | collective-permute-start | bytes 786440 | tf_op jit(solution)/shard_map/ppermute | solution.py:459
  37.8 15.7 %collective-permute-start.6 = (bf16[2,256,256]{2,1,0:T(8,128)(2,1)S(1)}, bf16[2,256,256]{2,1,0:T(8,128)(2,1)S(1)}, u32[]{:S(2)}, u32[]{:S(2)}) collective-permute-start(bf16[2,256,256]{2,1,0:T(8,128)(2,1)S(1)} %get-tuple-element.75), channel_id=1, source_target_pairs={{16,0},{8,24},{17,1},{9,25},{18,2},{10,26},{19,3},{11,27},{20,4},{... | collective-permute-start | bytes 786440 | tf_op jit(solution)/shard_map/ppermute | solution.py:459
  39.1 17.2 %collective-permute-start.7 = (bf16[2,256,256]{2,1,0:T(8,128)(2,1)S(1)}, bf16[2,256,256]{2,1,0:T(8,128)(2,1)S(1)}, u32[]{:S(2)}, u32[]{:S(2)}) collective-permute-start(bf16[2,256,256]{2,1,0:T(8,128)(2,1)S(1)} %get-tuple-element.76), channel_id=1, source_target_pairs={{8,0},{16,24},{9,1},{17,25},{10,2},{18,26},{11,3},{19,27},{12,4},{... | collective-permute-start | bytes 786440 | tf_op jit(solution)/shard_map/ppermute | solution.py:459
  59.2 3.9 %collective-permute-start.9 = (bf16[384,512]{1,0:T(8,128)(2,1)S(1)}, bf16[384,512]{1,0:T(8,128)(2,1)S(1)}, u32[]{:S(2)}, u32[]{:S(2)}) collective-permute-start(bf16[384,512]{1,0:T(8,128)(2,1)S(1)} %get-tuple-element.82.refs_2_), channel_id=1, source_target_pairs={{0,4},{4,0},{1,5},{5,1},{2,6},{6,2},{3,7},{7,3},{8,12},{12,8},{9,1... | collective-permute-start | bytes 1179656 | tf_op jit(solution)/shard_map/ppermute | solution.py:462
  59.2 6.9 %collective-permute-start.8 = (f32[32,384]{1,0:T(8,128)S(1)}, f32[32,384]{1,0:T(8,128)S(1)}, u32[]{:S(2)}, u32[]{:S(2)}) collective-permute-start(f32[32,384]{1,0:T(8,128)S(1)} %get-tuple-element.80.refs_3_), channel_id=1, source_target_pairs={{8,0},{16,8},{24,16},{9,1},{17,9},{25,17},{10,2},{18,10},{26,18},{... | collective-permute-start | bytes 147464 | tf_op jit(solution)/shard_map/ppermute | solution.py:449
  60.5 9.7 %collective-permute-start.11 = (f32[32,384]{1,0:T(8,128)S(1)}, f32[32,384]{1,0:T(8,128)S(1)}, u32[]{:S(2)}, u32[]{:S(2)}) collective-permute-start(f32[32,384]{1,0:T(8,128)S(1)} %get-tuple-element.80.refs_3_), channel_id=1, source_target_pairs={{16,0},{24,8},{17,1},{25,9},{18,2},{26,10},{19,3},{27,11},{20,4},{... | collective-permute-start | bytes 147464 | tf_op jit(solution)/shard_map/ppermute | solution.py:449
  61.8 9.0 %collective-permute-start.12 = (f32[32,384]{1,0:T(8,128)S(1)}, f32[32,384]{1,0:T(8,128)S(1)}, u32[]{:S(2)}, u32[]{:S(2)}) collective-permute-start(f32[32,384]{1,0:T(8,128)S(1)} %get-tuple-element.80.refs_3_), channel_id=1, source_target_pairs={{24,0},{25,1},{26,2},{27,3},{28,4},{29,5},{30,6},{31,7}} | collective-permute-start | bytes 147464 | tf_op jit(solution)/shard_map/ppermute | solution.py:449
  69.7 4.5 %collective-permute-start.10 = (bf16[384,512]{1,0:T(8,128)(2,1)S(1)}, bf16[384,512]{1,0:T(8,128)(2,1)S(1)}, u32[]{:S(2)}, u32[]{:S(2)}) collective-permute-start(bf16[384,512]{1,0:T(8,128)(2,1)S(1)} %get-tuple-element.93.refs_2_), channel_id=1, source_target_pairs={{0,4},{4,0},{1,5},{5,1},{2,6},{6,2},{3,7},{7,3},{8,12},{12,8},{9,1... | collective-permute-start | bytes 1179656 | tf_op jit(solution)/shard_map/ppermute | solution.py:462
  70.8 21.0 %collective-permute-start.15 = (bf16[2,384,512]{2,1,0:T(8,128)(2,1)S(1)}, bf16[2,384,512]{2,1,0:T(8,128)(2,1)S(1)}, u32[]{:S(2)}, u32[]{:S(2)}) collective-permute-start(bf16[2,384,512]{2,1,0:T(8,128)(2,1)S(1)} %get-tuple-element.100), channel_id=1, source_target_pairs={{0,8},{24,16},{1,9},{25,17},{2,10},{26,18},{3,11},{27,19},{4,12},{... | collective-permute-start | bytes 2359304 | tf_op jit(solution)/shard_map/ppermute | solution.py:569
  74.2 4.5 %collective-permute-start.13 = (bf16[384,512]{1,0:T(8,128)(2,1)S(1)}, bf16[384,512]{1,0:T(8,128)(2,1)S(1)}, u32[]{:S(2)}, u32[]{:S(2)}) collective-permute-start(bf16[384,512]{1,0:T(8,128)(2,1)S(1)} %shard_map.84.refs_2_), channel_id=1, source_target_pairs={{0,4},{4,0},{1,5},{5,1},{2,6},{6,2},{3,7},{7,3},{8,12},{12,8},{9,1... | collective-permute-start | bytes 1179656 | tf_op jit(solution)/shard_map/ppermute | solution.py:462
  77.1 31.5 %collective-permute-start.17 = (bf16[2,384,512]{2,1,0:T(8,128)(2,1)S(1)}, bf16[2,384,512]{2,1,0:T(8,128)(2,1)S(1)}, u32[]{:S(2)}, u32[]{:S(2)}) collective-permute-start(bf16[2,384,512]{2,1,0:T(8,128)(2,1)S(1)} %get-tuple-element.102), channel_id=1, source_target_pairs={{0,8},{24,16},{1,9},{25,17},{2,10},{26,18},{3,11},{27,19},{4,12},{... | collective-permute-start | bytes 2359304 | tf_op jit(solution)/shard_map/ppermute | solution.py:569
  92.5 17.6 %collective-permute-start.16 = (bf16[2,384,512]{2,1,0:T(8,128)(2,1)S(1)}, bf16[2,384,512]{2,1,0:T(8,128)(2,1)S(1)}, u32[]{:S(2)}, u32[]{:S(2)}) collective-permute-start(bf16[2,384,512]{2,1,0:T(8,128)(2,1)S(1)} %shard_map.87.refs_3_), channel_id=1, source_target_pairs={{8,16},{16,8},{9,17},{17,9},{10,18},{18,10},{11,19},{19,11},{12,20... | collective-permute-start | bytes 2359304 | tf_op jit(solution)/shard_map/ppermute | solution.py:459
  93.2 32.3 %collective-permute-start.14 = (bf16[2,384,512]{2,1,0:T(8,128)(2,1)S(1)}, bf16[2,384,512]{2,1,0:T(8,128)(2,1)S(1)}, u32[]{:S(2)}, u32[]{:S(2)}) collective-permute-start(bf16[2,384,512]{2,1,0:T(8,128)(2,1)S(1)} %get-tuple-element.98), channel_id=1, source_target_pairs={{0,8},{24,16},{1,9},{25,17},{2,10},{26,18},{3,11},{27,19},{4,12},{... | collective-permute-start | bytes 2359304 | tf_op jit(solution)/shard_map/ppermute | solution.py:569
  109.3 18.2 %collective-permute-start.19 = (bf16[2,384,512]{2,1,0:T(8,128)(2,1)S(1)}, bf16[2,384,512]{2,1,0:T(8,128)(2,1)S(1)}, u32[]{:S(2)}, u32[]{:S(2)}) collective-permute-start(bf16[2,384,512]{2,1,0:T(8,128)(2,1)S(1)} %shard_map.88.refs_0_), channel_id=1, source_target_pairs={{8,16},{16,8},{9,17},{17,9},{10,18},{18,10},{11,19},{19,11},{12,20... | collective-permute-start | bytes 2359304 | tf_op jit(solution)/shard_map/ppermute | solution.py:459
  110.7 22.6 %collective-permute-start.20 = (bf16[384,512]{1,0:T(8,128)(2,1)S(1)}, bf16[384,512]{1,0:T(8,128)(2,1)S(1)}, u32[]{:S(2)}, u32[]{:S(2)}) collective-permute-start(bf16[384,512]{1,0:T(8,128)(2,1)S(1)} %shard_map.89.refs_3_), channel_id=1, source_target_pairs={{0,8},{8,0},{16,24},{24,16},{1,9},{9,1},{17,25},{25,17},{2,10},{10... | collective-permute-start | bytes 1179656 | tf_op jit(solution)/shard_map/ppermute | solution.py:459
  126.2 10.3 %collective-permute-start.18 = (bf16[1,384,512]{2,1,0:T(8,128)(2,1)S(1)}, bf16[1,384,512]{2,1,0:T(8,128)(2,1)S(1)}, u32[]{:S(2)}, u32[]{:S(2)}) collective-permute-start(bf16[1,384,512]{2,1,0:T(8,128)(2,1)S(1)} %get-tuple-element.104.refs_1_), channel_id=1, source_target_pairs={{8,16},{16,8},{9,17},{17,9},{10,18},{18,10},{11,19},{19,11},{12,20... | collective-permute-start | bytes 1179656 | tf_op jit(solution)/shard_map/ppermute | solution.py:459
  126.9 21.1 %collective-permute-start.22 = (bf16[1,384,512]{2,1,0:T(8,128)(2,1)S(1)}, bf16[1,384,512]{2,1,0:T(8,128)(2,1)S(1)}, u32[]{:S(2)}, u32[]{:S(2)}) collective-permute-start(bf16[1,384,512]{2,1,0:T(8,128)(2,1)S(1)} %get-tuple-element.105.refs_2_), channel_id=1, source_target_pairs={{8,16},{16,8},{9,17},{17,9},{10,18},{18,10},{11,19},{19,11},{12,20... | collective-permute-start | bytes 1179656 | tf_op jit(solution)/shard_map/ppermute | solution.py:459
  133.9 12.5 %collective-permute-start.23 = (bf16[384,512]{1,0:T(8,128)(2,1)S(1)}, bf16[384,512]{1,0:T(8,128)(2,1)S(1)}, u32[]{:S(2)}, u32[]{:S(2)}) collective-permute-start(bf16[384,512]{1,0:T(8,128)(2,1)S(1)} %shard_map.91.refs_0_), channel_id=1, source_target_pairs={{0,8},{8,0},{16,24},{24,16},{1,9},{9,1},{17,25},{25,17},{2,10},{10... | collective-permute-start | bytes 1179656 | tf_op jit(solution)/shard_map/ppermute | solution.py:459
  137.1 16.6 %collective-permute-start.21 = (bf16[384,512]{1,0:T(8,128)(2,1)S(1)}, bf16[384,512]{1,0:T(8,128)(2,1)S(1)}, u32[]{:S(2)}, u32[]{:S(2)}) collective-permute-start(bf16[384,512]{1,0:T(8,128)(2,1)S(1)} %shard_map.92), channel_id=1, source_target_pairs={{0,8},{8,0},{16,24},{24,16},{1,9},{9,1},{17,25},{25,17},{2,10},{10... | collective-permute-start | bytes 1179656 | tf_op jit(solution)/shard_map/ppermute | solution.py:459
